TPU v7x, 256 devices: a whole 4x4x8 slice. The times are simulated.
256 devices in a mesh: dp: 8 (over z), mp: 32 (over y, x, core).
Axes of the slice: x: 4, y: 4, z: 8, core: 2. Of those that a mesh axis runs over, the one named last changes fastest.
Arguments:
- grads: bfloat16 [8, 8, 1024, 1024], P('dp', None, 'mp'), may hold values from -0.15625 to 0.15625
- block_slot: int32 [8], replicated, may hold values from 0 to 15, as said below
- left_stats: float32 [16, 1024, 1024], P('dp', 'mp'), as said below
- right_stats: float32 [16, 1024, 1024], P('dp', 'mp'), as said below
- left_basis: bfloat16 [16, 1024, 1024], P('dp', 'mp'), as said below
- right_basis: bfloat16 [16, 1024, 1024], P('dp', 'mp'), as said below
- first_moment: float32 [16, 1024, 1024], P('dp', 'mp'), may hold values from -0.125 to 0.125
- second_moment: float32 [16, 1024, 1024], P('dp', 'mp'), may hold values from 4.8828126e-05 to 0.001953125
Outputs:
- update: bfloat16 [8, 1024, 1024], P('dp')
- new_left_stats: float32 [16, 1024, 1024], P('dp', 'mp')
- new_right_stats: float32 [16, 1024, 1024], P('dp', 'mp')
- new_left_basis: bfloat16 [16, 1024, 1024], P('dp', 'mp')
- new_right_basis: bfloat16 [16, 1024, 1024], P('dp', 'mp')
Inputs may be any that keep to these rules, and one draw needn't show every extreme that they name: `block_slot`: distinct blocks name distinct slots; slot s belongs to index s // 2 of dp, and some index of dp holds 2 blocks in every draw. `left_stats`: every slot is symmetric positive definite. `right_stats`: every slot is symmetric positive definite. `left_basis`: every slot is invertible. `right_basis`: every slot is invertible.
All inputs are finite; a program needn't handle non-finite values.
Results may differ from a plain program's by a relative error of at most 0.022.
Values may be sent and summed in bfloat16 or wider, within the bound.
A program may use at most 192 MiB of HBM per device.

v0:
```python
import jax
import jax.numpy as jnp
from jax import lax
from jax.sharding import PartitionSpec as P

BETA_STATS = 0.95
BETA_FIRST = 0.9
BETA_SECOND = 0.95
EPSILON = 1e-08
highest = lax.Precision.HIGHEST


def factor_inverse(factor):
    width = factor.shape[-1]
    identity = jnp.eye(width, dtype=jnp.float32)

    def single(one_factor):
        return jax.scipy.linalg.solve_triangular(one_factor, identity, lower=True)

    return jax.vmap(single)(factor)


def advance(
    grad_rows, left_stats, right_stats, left_basis, right_basis, first_moment, second_moment
):
    slot_count, row_count, block_width = grad_rows.shape
    row_start = lax.axis_index("mp") * row_count
    grad_full, left_old, right_old = (
        lax.all_gather(grad_rows, "mp", axis=1, tiled=True),
        lax.all_gather(left_basis, "mp", axis=1, tiled=True),
        lax.all_gather(right_basis, "mp", axis=1, tiled=True),
    )
    grad_cols = lax.dynamic_slice_in_dim(grad_full, row_start, row_count, 2)
    left_term = jnp.einsum("krc,kjc->krj", grad_rows, grad_full, preferred_element_type=jnp.float32)
    right_term = jnp.einsum(
        "kic,kij->kcj", grad_cols, grad_full, preferred_element_type=jnp.float32
    )
    left_next = BETA_STATS * left_stats + (1.0 - BETA_STATS) * left_term
    right_next = BETA_STATS * right_stats + (1.0 - BETA_STATS) * right_term
    left_rows = jnp.einsum(
        "krj,kjc->krc", left_next.astype(jnp.bfloat16), left_old, preferred_element_type=jnp.float32
    ).astype(jnp.bfloat16)
    right_rows = jnp.einsum(
        "krj,kjc->krc",
        right_next.astype(jnp.bfloat16),
        right_old,
        preferred_element_type=jnp.float32,
    ).astype(jnp.bfloat16)
    left_power, right_power = (
        lax.all_gather(left_rows, "mp", axis=1, tiled=True),
        lax.all_gather(right_rows, "mp", axis=1, tiled=True),
    )
    left_factor = jnp.linalg.cholesky(
        jnp.einsum("kij,kil->kjl", left_power, left_power, preferred_element_type=jnp.float32)
    )
    right_factor = jnp.linalg.cholesky(
        jnp.einsum("kij,kil->kjl", right_power, right_power, preferred_element_type=jnp.float32)
    )
    left_inverse = factor_inverse(left_factor)
    right_inverse = factor_inverse(right_factor)
    left_q_rows = jnp.einsum(
        "krj,kcj->krc",
        left_rows.astype(jnp.float32),
        left_inverse,
        precision=highest,
        preferred_element_type=jnp.float32,
    )
    right_q_rows = jnp.einsum(
        "krj,kcj->krc",
        right_rows.astype(jnp.float32),
        right_inverse,
        precision=highest,
        preferred_element_type=jnp.float32,
    )
    inverse_part = lax.dynamic_slice_in_dim(left_inverse, row_start, row_count, 1)
    left_q_cols = jnp.einsum(
        "kij,kcj->kic",
        left_power.astype(jnp.float32),
        inverse_part,
        precision=highest,
        preferred_element_type=jnp.float32,
    )
    moved_rows = jnp.einsum(
        "kic,kij->kcj",
        left_q_cols,
        grad_full.astype(jnp.float32),
        precision=highest,
        preferred_element_type=jnp.float32,
    )
    mixed_rows = jnp.einsum(
        "krj,kji->kri",
        moved_rows,
        right_power.astype(jnp.float32),
        precision=highest,
        preferred_element_type=jnp.float32,
    )
    rotated = jnp.einsum(
        "kri,kci->krc",
        mixed_rows,
        right_inverse,
        precision=highest,
        preferred_element_type=jnp.float32,
    )
    first_next = BETA_FIRST * first_moment + (1.0 - BETA_FIRST) * rotated
    second_next = BETA_SECOND * second_moment + (1.0 - BETA_SECOND) * rotated * rotated
    normed = first_next / (jnp.sqrt(second_next) + EPSILON)
    scaled = jnp.einsum(
        "krj,kjc->krc", normed, right_inverse, precision=highest, preferred_element_type=jnp.float32
    )
    half_part = jnp.einsum(
        "krj,kij->kri",
        scaled,
        right_power.astype(jnp.float32),
        precision=highest,
        preferred_element_type=jnp.float32,
    ).astype(jnp.bfloat16)
    half_full = lax.all_gather(half_part, "mp", axis=1, tiled=True)
    update_rows = jnp.einsum(
        "krj,kji->kri",
        left_q_rows,
        half_full.astype(jnp.float32),
        precision=highest,
        preferred_element_type=jnp.float32,
    ).astype(jnp.bfloat16)
    return (
        update_rows,
        left_next,
        right_next,
        left_q_rows.astype(jnp.bfloat16),
        right_q_rows.astype(jnp.bfloat16),
    )


def per_device(
    grads, block_slot, left_stats, right_stats, left_basis, right_basis, first_moment, second_moment
):
    capacity, row_count, block_width = left_stats.shape
    group_size = lax.axis_size("dp")
    owner_index = lax.axis_index("dp")
    block_total = block_slot.shape[0]
    per_home = block_total // group_size
    slot_total = capacity * group_size
    local_grads = grads[0]
    slot_ids = owner_index * capacity + jnp.arange(capacity, dtype=jnp.int32)
    held = jnp.any(block_slot[:, None] == slot_ids[None, :], axis=0)
    local_index = block_slot - owner_index * capacity
    owned = (local_index >= 0) & (local_index < capacity)
    safe_index = jnp.clip(local_index, 0, capacity - 1)
    placing = (
        block_slot[:, None] == lax.broadcasted_iota(jnp.int32, (block_total, slot_total), 1)
    ).astype(jnp.bfloat16)
    slot_grads = jnp.einsum("bs,brc->src", placing, local_grads, preferred_element_type=jnp.float32)
    grad_rows = lax.psum_scatter(
        slot_grads.astype(jnp.bfloat16), "dp", scatter_dimension=0, tiled=True
    )
    update_rows, left_next, right_next, left_new, right_new = advance(
        grad_rows, left_stats, right_stats, left_basis, right_basis, first_moment, second_moment
    )
    picked = jnp.take(update_rows, safe_index, axis=0)
    arrived = lax.all_to_all(
        jnp.where(owned[:, None, None], picked, jnp.zeros_like(picked)),
        "dp",
        split_axis=0,
        concat_axis=0,
        tiled=True,
    )
    home_rows = jnp.sum(arrived.reshape(group_size, per_home, row_count, block_width), axis=0)
    held_mask = held[:, None, None]
    new_left_stats = jnp.where(held_mask, left_next, left_stats)
    new_right_stats = jnp.where(held_mask, right_next, right_stats)
    new_left_basis = jnp.where(held_mask, left_new, left_basis)
    new_right_basis = jnp.where(held_mask, right_new, right_basis)
    update = lax.all_gather(home_rows, "mp", axis=1, tiled=True)
    return (update, new_left_stats, new_right_stats, new_left_basis, new_right_basis)


def solution(mesh):
    placed = (
        P("dp", None, "mp", None),
        P(),
        P("dp", "mp", None),
        P("dp", "mp", None),
        P("dp", "mp", None),
        P("dp", "mp", None),
        P("dp", "mp", None),
        P("dp", "mp", None),
    )
    return jax.shard_map(
        per_device,
        mesh=mesh,
        in_specs=placed,
        out_specs=(
            P("dp", None, None),
            P("dp", "mp", None),
            P("dp", "mp", None),
            P("dp", "mp", None),
            P("dp", "mp", None),
        ),
        check_vma=False,
    )
```

profile of v0, /device:TPU:1, one launch (start us, length us, event | category | flops | bytes accessed | tf_op | source)
XLA Modules:
  0.0 1823.3 jit_solution(15431169304434265148)
XLA Ops:
  11.1 38.1 %reduce-scatter.2.cloned.1.call-done = bf16[2,32,1024]{2,1,0:T(8,128)(2,1)} async-done(((bf16[16,32,1024]{2,1,0:T(8,128)(2,1)}), bf16[2,32,1024]{2,1,0:T(8,128)(2,1)}) %reduce-scatter.2.cloned.1.call-update) | async-done | bytes 131088 | tf_op jit(solution)/shard_map/reduce_scatter | solution.py:153
  53.1 53.9 %all-gather.9.cloned.1.call-done = bf16[2,1024,1024]{2,0,1:T(2,128)(2,1)} async-done(((bf16[2,32,1024]{2,0,1:T(2,128)(2,1)}), bf16[2,1024,1024]{2,0,1:T(2,128)(2,1)}) %all-gather.9.cloned.1.call-update) | async-done | bytes 4194320 | tf_op jit(solution)/shard_map/all_gather | solution.py:29
  112.4 4.4 broadcast_select_fusion
  116.8 43.5 %all-gather.15.cloned.1.call-done = bf16[2,1024,1024]{2,1,0:T(8,128)(2,1)} async-done(((bf16[2,32,1024]{2,1,0:T(8,128)(2,1)}), bf16[2,1024,1024]{2,1,0:T(8,128)(2,1)}) %all-gather.15.cloned.1.call-update) | async-done | bytes 4194320 | tf_op jit(solution)/shard_map/all_gather | solution.py:31
  164.0 49.3 %all-gather.11.cloned.1.call-done = bf16[2,1024,1024]{2,1,0:T(8,128)(2,1)} async-done(((bf16[2,32,1024]{2,1,0:T(8,128)(2,1)}), bf16[2,1024,1024]{2,1,0:T(8,128)(2,1)}) %all-gather.11.cloned.1.call-update) | async-done | bytes 4194320 | tf_op jit(solution)/shard_map/all_gather | solution.py:30
  220.3 45.9 %all-gather.17.cloned.1.call-done = bf16[2,1024,1024]{2,1,0:T(8,128)(2,1)} async-done(((bf16[2,32,1024]{2,1,0:T(8,128)(2,1)}), bf16[2,1024,1024]{2,1,0:T(8,128)(2,1)}) %all-gather.17.cloned.1.call-update) | async-done | bytes 4194320 | tf_op jit(solution)/shard_map/all_gather | solution.py:51
  266.2 11.2 fusion.241
  277.5 9.2 copy.151
  286.6 12.1 fusion
  299.6 23.5 %custom-call.87 = f32[2,128,128]{2,1,0:T(8,128)S(1)} custom-call(f32[2,128,128]{2,1,0:T(8,128)S(1)} %cholesky.927), custom_call_target="Cholesky" | custom-call | tf_op jit(solution)/shard_map/jit(cholesky)/cholesky | solution.py:56
  323.7 20.5 %custom-call.88 = f32[2,1,128,128]{2,3,1,0:T(8,128)S(1)} custom-call(f32[2,1,128,128]{3,2,1,0:T(8,128)} %select_bitcast_fusion.6), custom_call_target="InvertDiagBlocksLowerTriangular" | custom-call | tf_op jit(solution)/shard_map/jit(cholesky)/cholesky | solution.py:56
  355.3 24.4 %custom-call.89 = f32[2,128,128]{2,1,0:T(8,128)S(1)} custom-call(f32[2,128,128]{2,1,0:T(8,128)} %cholesky.931), custom_call_target="Cholesky" | custom-call | tf_op jit(solution)/shard_map/jit(cholesky)/cholesky | solution.py:56
  380.5 21.1 %custom-call.90 = f32[2,1,128,128]{2,3,1,0:T(8,128)} custom-call(f32[2,1,128,128]{3,2,1,0:T(8,128)} %get-tuple-element.133), custom_call_target="InvertDiagBlocksLowerTriangular" | custom-call | tf_op jit(solution)/shard_map/jit(cholesky)/cholesky | solution.py:56
  409.3 25.1 %custom-call.91 = f32[2,128,128]{2,1,0:T(8,128)} custom-call(f32[2,128,128]{2,1,0:T(8,128)} %cholesky.936), custom_call_target="Cholesky" | custom-call | tf_op jit(solution)/shard_map/jit(cholesky)/cholesky | solution.py:56
  436.1 21.1 %custom-call.92 = f32[2,1,128,128]{2,3,1,0:T(8,128)} custom-call(f32[2,1,128,128]{3,2,1,0:T(8,128)} %get-tuple-element.131), custom_call_target="InvertDiagBlocksLowerTriangular" | custom-call | tf_op jit(solution)/shard_map/jit(cholesky)/cholesky | solution.py:56
  465.1 25.3 %custom-call.93 = f32[2,128,128]{2,1,0:T(8,128)} custom-call(f32[2,128,128]{2,1,0:T(8,128)} %cholesky.941), custom_call_target="Cholesky" | custom-call | tf_op jit(solution)/shard_map/jit(cholesky)/cholesky | solution.py:56
  492.1 21.1 %custom-call.94 = f32[2,1,128,128]{2,3,1,0:T(8,128)} custom-call(f32[2,1,128,128]{3,2,1,0:T(8,128)} %get-tuple-element.129), custom_call_target="InvertDiagBlocksLowerTriangular" | custom-call | tf_op jit(solution)/shard_map/jit(cholesky)/cholesky | solution.py:56
  520.9 24.3 %custom-call.95 = f32[2,128,128]{2,1,0:T(8,128)S(1)} custom-call(f32[2,128,128]{2,1,0:T(8,128)} %cholesky.946), custom_call_target="Cholesky" | custom-call | tf_op jit(solution)/shard_map/jit(cholesky)/cholesky | solution.py:56
  545.9 21.3 %custom-call.96 = f32[2,1,128,128]{2,3,1,0:T(8,128)} custom-call(f32[2,1,128,128]{3,2,1,0:T(8,128)} %get-tuple-element.127), custom_call_target="InvertDiagBlocksLowerTriangular" | custom-call | tf_op jit(solution)/shard_map/jit(cholesky)/cholesky | solution.py:56
  574.6 25.1 %custom-call.97 = f32[2,128,128]{2,1,0:T(8,128)} custom-call(f32[2,128,128]{2,1,0:T(8,128)} %cholesky.951), custom_call_target="Cholesky" | custom-call | tf_op jit(solution)/shard_map/jit(cholesky)/cholesky | solution.py:56
  599.7 11.2 fusion.239
  610.9 8.7 copy.124
  619.6 12.0 fusion.1
  633.2 24.3 %custom-call.71 = f32[2,128,128]{2,1,0:T(8,128)S(1)} custom-call(f32[2,128,128]{2,1,0:T(8,128)} %cholesky.894), custom_call_target="Cholesky" | custom-call | tf_op jit(solution)/shard_map/jit(cholesky)/cholesky | solution.py:53
  659.2 21.5 %custom-call.98 = f32[2,1,128,128]{2,3,1,0:T(8,128)} custom-call(f32[2,1,128,128]{3,2,1,0:T(8,128)} %get-tuple-element.125), custom_call_target="InvertDiagBlocksLowerTriangular" | custom-call | tf_op jit(solution)/shard_map/jit(cholesky)/cholesky | solution.py:56
  687.3 24.9 %custom-call.99 = f32[2,128,128]{2,1,0:T(8,128)} custom-call(f32[2,128,128]{2,1,0:T(8,128)} %cholesky.956), custom_call_target="Cholesky" | custom-call | tf_op jit(solution)/shard_map/jit(cholesky)/cholesky | solution.py:56
  712.2 21.2 %custom-call.72 = f32[2,1,128,128]{2,3,1,0:T(8,128)} custom-call(f32[2,1,128,128]{3,2,1,0:T(8,128)} %get-tuple-element.149), custom_call_target="InvertDiagBlocksLowerTriangular" | custom-call | tf_op jit(solution)/shard_map/jit(cholesky)/cholesky | solution.py:53
  744.5 24.9 %custom-call.73 = f32[2,128,128]{2,1,0:T(8,128)} custom-call(f32[2,128,128]{2,1,0:T(8,128)} %cholesky.898), custom_call_target="Cholesky" | custom-call | tf_op jit(solution)/shard_map/jit(cholesky)/cholesky | solution.py:53
  771.2 21.1 %custom-call.100 = f32[2,1,128,128]{2,3,1,0:T(8,128)} custom-call(f32[2,1,128,128]{3,2,1,0:T(8,128)} %get-tuple-element.123), custom_call_target="InvertDiagBlocksLowerTriangular" | custom-call | tf_op jit(solution)/shard_map/jit(cholesky)/cholesky | solution.py:56
  797.5 25.1 %custom-call.101 = f32[2,128,128]{2,1,0:T(8,128)} custom-call(f32[2,128,128]{2,1,0:T(8,128)} %convolution_subtract_fusion.10), custom_call_target="Cholesky" | custom-call | tf_op jit(solution)/shard_map/jit(cholesky)/cholesky | solution.py:56
  822.6 21.1 %custom-call.74 = f32[2,1,128,128]{2,3,1,0:T(8,128)} custom-call(f32[2,1,128,128]{3,2,1,0:T(8,128)} %get-tuple-element.148), custom_call_target="InvertDiagBlocksLowerTriangular" | custom-call | tf_op jit(solution)/shard_map/jit(cholesky)/cholesky | solution.py:53
  851.3 25.3 %custom-call.75 = f32[2,128,128]{2,1,0:T(8,128)} custom-call(f32[2,128,128]{2,1,0:T(8,128)} %cholesky.903), custom_call_target="Cholesky" | custom-call | tf_op jit(solution)/shard_map/jit(cholesky)/cholesky | solution.py:53
  878.2 21.1 %custom-call.76 = f32[2,1,128,128]{2,3,1,0:T(8,128)} custom-call(f32[2,1,128,128]{3,2,1,0:T(8,128)} %get-tuple-element.143), custom_call_target="InvertDiagBlocksLowerTriangular" | custom-call | tf_op jit(solution)/shard_map/jit(cholesky)/cholesky | solution.py:53
  907.3 25.0 %custom-call.77 = f32[2,128,128]{2,1,0:T(8,128)} custom-call(f32[2,128,128]{2,1,0:T(8,128)} %cholesky.908), custom_call_target="Cholesky" | custom-call | tf_op jit(solution)/shard_map/jit(cholesky)/cholesky | solution.py:53
  934.0 21.1 %custom-call.78 = f32[2,1,128,128]{2,3,1,0:T(8,128)} custom-call(f32[2,1,128,128]{3,2,1,0:T(8,128)} %get-tuple-element.141), custom_call_target="InvertDiagBlocksLowerTriangular" | custom-call | tf_op jit(solution)/shard_map/jit(cholesky)/cholesky | solution.py:53
  962.8 24.9 %custom-call.79 = f32[2,128,128]{2,1,0:T(8,128)} custom-call(f32[2,128,128]{2,1,0:T(8,128)} %cholesky.913), custom_call_target="Cholesky" | custom-call | tf_op jit(solution)/shard_map/jit(cholesky)/cholesky | solution.py:53
  989.4 21.3 %custom-call.80 = f32[2,1,128,128]{2,3,1,0:T(8,128)} custom-call(f32[2,1,128,128]{3,2,1,0:T(8,128)} %get-tuple-element.139), custom_call_target="InvertDiagBlocksLowerTriangular" | custom-call | tf_op jit(solution)/shard_map/jit(cholesky)/cholesky | solution.py:53
  1018.1 24.9 %custom-call.81 = f32[2,128,128]{2,1,0:T(8,128)} custom-call(f32[2,128,128]{2,1,0:T(8,128)} %cholesky.918), custom_call_target="Cholesky" | custom-call | tf_op jit(solution)/shard_map/jit(cholesky)/cholesky | solution.py:53
  1044.6 21.5 %custom-call.82 = f32[2,1,128,128]{2,3,1,0:T(8,128)} custom-call(f32[2,1,128,128]{3,2,1,0:T(8,128)} %get-tuple-element.137), custom_call_target="InvertDiagBlocksLowerTriangular" | custom-call | tf_op jit(solution)/shard_map/jit(cholesky)/cholesky | solution.py:53
  1072.7 24.9 %custom-call.83 = f32[2,128,128]{2,1,0:T(8,128)} custom-call(f32[2,128,128]{2,1,0:T(8,128)} %cholesky.923), custom_call_target="Cholesky" | custom-call | tf_op jit(solution)/shard_map/jit(cholesky)/cholesky | solution.py:53
  1099.3 21.1 %custom-call.84 = f32[2,1,128,128]{2,3,1,0:T(8,128)} custom-call(f32[2,1,128,128]{3,2,1,0:T(8,128)} %get-tuple-element.135), custom_call_target="InvertDiagBlocksLowerTriangular" | custom-call | tf_op jit(solution)/shard_map/jit(cholesky)/cholesky | solution.py:53
  1125.4 25.0 %custom-call.85 = f32[2,128,128]{2,1,0:T(8,128)} custom-call(f32[2,128,128]{2,1,0:T(8,128)} %convolution_subtract_fusion.11), custom_call_target="Cholesky" | custom-call | tf_op jit(solution)/shard_map/jit(cholesky)/cholesky | solution.py:53
  1154.2 11.6 select_select_fusion
  1166.9 29.9 %while.5 = (s32[]{:T(128)}, f32[2,1024,1024]{2,1,0:T(8,128)}, s32[8,2]{0,1:T(2,128)S(1)}, f32[8,2,128,128]{3,2,0,1:T(8,128)}, s32[]{:T(128)}) while((s32[]{:T(128)}, f32[2,1024,1024]{2,1,0:T(8,128)}, s32[8,2]{0,1:T(2,128)S(1)}, f32[8,2,128,128]{3,2,0,1:T(8,128)}, s32[]{:T(128)}) %tuple.143), condition=%wide.while_cond.clone, body=%wide.while_body.clone.sunk | while | flops 2 | bytes 263777 | solution.py:18
  1196.7 158.6 %custom-call.102 = f32[2,8,128,128]{2,3,1,0:T(8,128)} custom-call(f32[2,8,128,128]{3,2,1,0:T(8,128)} %bitcast.267), custom_call_target="InvertDiagBlocksLowerTriangular" | custom-call | tf_op jit(solution)/shard_map/vmap(jit(_solve_triangular))/triangular_solve | solution.py:18
  1356.5 29.9 %while.4 = (s32[]{:T(128)}, f32[2,1024,1024]{2,1,0:T(8,128)}, s32[8,2]{0,1:T(2,128)S(1)}, f32[8,2,128,128]{3,2,0,1:T(8,128)}, s32[]{:T(128)}) while((s32[]{:T(128)}, f32[2,1024,1024]{2,1,0:T(8,128)}, s32[8,2]{0,1:T(2,128)S(1)}, f32[8,2,128,128]{3,2,0,1:T(8,128)}, s32[]{:T(128)}) %tuple.164), condition=%wide.while_cond, body=%wide.while_body.sunk | while | flops 2 | bytes 263777 | solution.py:18
  1386.3 158.8 %custom-call.86 = f32[2,8,128,128]{2,3,1,0:T(8,128)} custom-call(f32[2,8,128,128]{3,2,1,0:T(8,128)} %bitcast.266), custom_call_target="InvertDiagBlocksLowerTriangular" | custom-call | tf_op jit(solution)/shard_map/vmap(jit(_solve_triangular))/triangular_solve | solution.py:18
  1586.2 5.2 fusion.77
  1595.4 4.8 fusion.80
  1604.0 5.6 convolution_subtract_fusion.3
  1613.0 5.6 convolution_subtract_fusion.6
  1621.6 6.1 convolution_subtract_fusion.2
  1630.9 6.4 convolution_subtract_fusion.5
  1639.2 5.5 convolution_subtract_fusion
  1646.8 5.7 convolution_subtract_fusion.1
  1657.2 8.9 fusion.179
  1671.2 7.9 fusion.242
  1679.1 5.0 fusion.168
  1688.9 8.2 convert_select_fusion
  1697.0 42.2 %all-gather.19.cloned.1.call-done = bf16[2,1024,1024]{2,1,0:T(8,128)(2,1)} async-done(((bf16[2,32,1024]{2,1,0:T(8,128)(2,1)}), bf16[2,1024,1024]{2,1,0:T(8,128)(2,1)}) %all-gather.19.cloned.1.call-update) | async-done | bytes 4194320 | tf_op jit(solution)/shard_map/all_gather | solution.py:117
  1739.2 4.4 convolution_convert_fusion.2
  1744.4 24.0 %all_to_all.5 = bf16[8,32,1024]{2,1,0:T(8,128)(2,1)S(1)} all-to-all(bf16[8,32,1024]{2,1,0:T(8,128)(2,1)S(1)} %select_select_fusion.2), channel_id=1, replica_groups=mesh['dp'=8,'mp'=32] {'dp'}, dimensions={0} | all-to-all | bytes 1048576 | tf_op jit(solution)/shard_map/all_to_all | solution.py:160
  1769.1 8.1 fusion.125
  1777.3 35.9 %all-gather.21.cloned.1.call-done = bf16[1024,1024]{1,0:T(8,128)(2,1)} async-done(((bf16[32,1024]{1,0:T(8,128)(2,1)}), bf16[1024,1024]{1,0:T(8,128)(2,1)}) %all-gather.21.cloned.1.call-update) | async-done | bytes 2097168 | tf_op jit(solution)/shard_map/all_gather | solution.py:173
  (255 shorter events, 297.4 us)
Async XLA Ops:
  7.2 1.1 copy-start
  7.2 105.2 %copy-start.22 = (f32[2,32,1024]{2,1,0:T(8,128)S(1)}, f32[2,32,1024]{2,1,0:T(8,128)}, u32[]{:S(2)}) copy-start(f32[2,32,1024]{2,1,0:T(8,128)} %param.13) | copy-start | bytes 786436
  7.2 105.2 %copy-start.32 = (f32[2,32,1024]{2,1,0:T(8,128)S(1)}, f32[2,32,1024]{2,1,0:T(8,128)}, u32[]{:S(2)}) copy-start(f32[2,32,1024]{2,1,0:T(8,128)} %param.14) | copy-start | bytes 786436
  7.2 42.0 %reduce-scatter.2.cloned.1.call-start = ((), (), s32[]{:S(2)}) async-start(), calls=%async_computation.2 | async-start | bytes 1179648 | tf_op jit(solution)/shard_map/reduce_scatter | solution.py:153
  11.0 96.0 %all-gather.9.cloned.1.call-start = ((), (), s32[]{:S(2)}) async-start(), calls=%async_computation.3 | async-start | bytes 4325376 | tf_op jit(solution)/shard_map/all_gather | solution.py:29
  50.9 109.3 %all-gather.15.cloned.1.call-start = ((), (), s32[]{:S(2)}) async-start(), calls=%async_computation.6 | async-start | bytes 4325376 | tf_op jit(solution)/shard_map/all_gather | solution.py:31
  51.6 161.6 %all-gather.11.cloned.1.call-start = ((), (), s32[]{:S(2)}) async-start(), calls=%async_computation.4 | async-start | bytes 4325376 | tf_op jit(solution)/shard_map/all_gather | solution.py:30
  52.2 214.0 %all-gather.17.cloned.1.call-start = ((), (), s32[]{:S(2)}) async-start(), calls=%async_computation.7 | async-start | bytes 4325376 | tf_op jit(solution)/shard_map/all_gather | solution.py:51
  163.9 435.8 %all-gather.13.cloned.1.call-start = ((), (), s32[]{:S(2)}) async-start(), calls=%async_computation.5 | async-start | bytes 4325376 | tf_op jit(solution)/shard_map/all_gather | solution.py:50
  216.9 1522.3 %all-gather.19.cloned.1.call-start = ((), (), s32[]{:S(2)}) async-start(), calls=%async_computation.8 | async-start | bytes 4325376 | tf_op jit(solution)/shard_map/all_gather | solution.py:117
  353.7 0.9 copy-start.11
  379.7 139.7 %copy-start.30 = (f32[2,128,128]{2,1,0:T(8,128)}, f32[2,128,128]{2,1,0:T(8,128)S(1)}, u32[]{:S(2)}) copy-start(f32[2,128,128]{2,1,0:T(8,128)S(1)} %custom-call.89) | copy-start | bytes 393220
  407.8 0.9 copy-start.12
  463.6 0.8 copy-start.14
  519.4 0.8 copy-start.18
  545.1 65.8 %copy-start.31 = (f32[2,128,128]{2,1,0:T(8,128)}, f32[2,128,128]{2,1,0:T(8,128)S(1)}, u32[]{:S(2)}) copy-start(f32[2,128,128]{2,1,0:T(8,128)S(1)} %custom-call.95) | copy-start | bytes 393220
  573.2 0.7 copy-start.20
  685.9 0.7 copy-start.25
  733.4 4.3 copy-start.35
  742.9 0.9 copy-start.10
  849.8 0.9 copy-start.13
  905.8 0.8 copy-start.15
  961.4 0.8 copy-start.19
  1016.7 0.7 copy-start.21
  1071.4 0.7 copy-start.26
  1548.7 10.6 copy-start.7
  1564.7 6.0 copy-start.6
  1570.7 15.5 copy-start.9
  1574.5 11.7 copy-start.29
  1578.1 8.2 copy-start.8
  1591.4 8.9 copy-start.23
  1600.2 9.3 copy-start.24
  1646.8 19.3 %copy-start.3 = (bf16[2,1024,1024]{2,0,1:T(2,128)(2,1)S(1)}, bf16[2,1024,1024]{2,0,1:T(2,128)(2,1)}, u32[]{:S(2)}) copy-start(bf16[2,1024,1024]{2,0,1:T(2,128)(2,1)} %all-gather.9.cloned.1.call-done) | copy-start | bytes 12582916
  1652.5 16.6 copy-start.4
  1654.6 24.5 %copy-start.2 = (f32[2,1024,1024]{2,1,0:T(8,128)}, f32[2,1024,1024]{2,1,0:T(8,128)S(1)}, u32[]{:S(2)}) copy-start(f32[2,1024,1024]{2,1,0:T(8,128)S(1)} %convolution_dynamic-update-slice_fusion) | copy-start | bytes 25165828
  1657.2 21.9 %copy-start.5 = (f32[2,1024,1024]{2,1,0:T(8,128)}, f32[2,1024,1024]{2,1,0:T(8,128)S(1)}, u32[]{:S(2)}) copy-start(f32[2,1024,1024]{2,1,0:T(8,128)S(1)} %convolution_dynamic-update-slice_fusion.1) | copy-start | bytes 25165828
  1666.1 13.0 copy-start.33
  1666.1 13.0 copy-start.34
  1679.1 9.7 copy-start.36
  1679.1 9.7 copy-start.17
  1679.1 9.7 copy-start.27
  1688.5 124.6 %all-gather.21.cloned.1.call-start = ((), (), s32[]{:S(2)}) async-start(), calls=%async_computation.9 | async-start | bytes 2162688 | tf_op jit(solution)/shard_map/all_gather | solution.py:173
  1688.9 80.3 %copy-start.16 = (bf16[2,32,1024]{2,1,0:T(8,128)(2,1)S(1)}, bf16[2,32,1024]{2,1,0:T(8,128)(2,1)}, u32[]{:S(2)}) copy-start(bf16[2,32,1024]{2,1,0:T(8,128)(2,1)} %convolution_convert_fusion.4) | copy-start | bytes 393220
  1688.9 80.3 %copy-start.28 = (bf16[2,32,1024]{2,1,0:T(8,128)(2,1)S(1)}, bf16[2,32,1024]{2,1,0:T(8,128)(2,1)}, u32[]{:S(2)}) copy-start(bf16[2,32,1024]{2,1,0:T(8,128)(2,1)} %param.16) | copy-start | bytes 393220
  1739.2 77.0 %copy-start.1 = (bf16[1,8,32,1024]{3,2,1,0:T(8,128)(2,1)S(1)}, bf16[1,8,32,1024]{3,2,1,0:T(8,128)(2,1)}, u32[]{:S(2)}) copy-start(bf16[1,8,32,1024]{3,2,1,0:T(8,128)(2,1)} %param.11) | copy-start | bytes 1572868
Sparse Core Ops, SparseCore 0:
  11.1 37.9 reduce-scatter.1
  52.3 54.7 all-gather.8
  109.7 50.5 all-gather.14
  162.7 50.5 all-gather.10
  215.7 50.5 all-gather.16
  269.3 50.6 all-gather.12
  1688.7 50.5 all-gather.18
  1769.2 43.8 all-gather.20
where the time goes:
time: 1840 us; the launch traced here: 1820 us
  other arithmetic  1070 us (58%)
  waiting for transfers between devices  310 us (17%)
  matrix products  284 us (15%)
  local copies, waits for them, and re-layouts  119 us (6%)
  blocking collectives  24 us (1%)
    another operation x28, other arithmetic, advance(): jnp.linalg.cholesky(jnp.einsum('kij,kil->kjl', right_power, right_power,...  357 us
    another operation x27, other arithmetic, advance(): jnp.linalg.cholesky(jnp.einsum('kij,kil->kjl', left_power, left_power, pr...  356 us
    another operation x5, other arithmetic, single(): return jax.scipy.linalg.solve_triangular(one_factor, identity, lower=True)  330 us
    another operation x30, matrix products, single(): return jax.scipy.linalg.solve_triangular(one_factor, identity, lower=True)  112 us
    another operation x52, local copies, waits for them, and re-layouts, single(): return jax.scipy.linalg.solve_triangular(one_factor, identity, lower=True)  63.3 us
    all_gather x1, waiting for transfers between devices, advance(): lax.all_gather(grad_rows, 'mp', axis=1, tiled=True)  53.9 us
    all_gather x1, waiting for transfers between devices, advance(): lax.all_gather(left_basis, 'mp', axis=1, tiled=True)  49.3 us
    all_gather x1, waiting for transfers between devices, advance(): lax.all_gather(right_rows, 'mp', axis=1, tiled=True)  45.9 us
  transfers between devices with their start and end apart: 8, of which 7 were waited for; matrix products, arithmetic and copies ran while one was open for 20% of the time, Pallas kernels for 0%

commit v1 on v0

v1 whole, which is shorter than its diff:
```python
import functools

import jax
import jax.numpy as jnp
from jax import lax
from jax.experimental import pallas as pl
from jax.experimental.pallas import tpu as pltpu
from jax.sharding import Mesh
from jax.sharding import PartitionSpec as P

BETA_STATS = 0.95
BETA_FIRST = 0.9
BETA_SECOND = 0.95
EPSILON = 1e-08
F32 = jnp.float32
BF = jnp.bfloat16
T = 128
MP = ("y", "h", "s", "c")
QUAD = ("s", "c")
RING = ("y", "h")


def split(x):
    high = x.astype(BF)
    return high, (x - high.astype(F32)).astype(BF)


def dot3(a_parts, b_parts, dims):
    (ah, al), (bh, bl) = a_parts, b_parts
    dot = functools.partial(
        lax.dot_general, dimension_numbers=(dims, ((), ())), preferred_element_type=F32
    )
    return dot(ah, bh) + (dot(ah, bl) + dot(al, bh))


def base_factor(block):
    sub = lax.broadcasted_iota(jnp.int32, (8, T), 0)
    lane = lax.broadcasted_iota(jnp.int32, (8, T), 1)
    groups = T // 8
    rows = [block[8 * g : 8 * g + 8, :] for g in range(groups)]
    inv = [(lane == sub + 8 * g).astype(F32) for g in range(groups)]

    def spread(x, q):
        return jnp.broadcast_to(x[q : q + 1, :], (8, T))

    for g in range(groups):
        r, e = rows[g], inv[g]
        cols = [jnp.broadcast_to(r[:, 8 * g + q : 8 * g + q + 1], (8, T)) for q in range(8)]
        scale = jnp.zeros((8, T), F32)
        for q in range(8):
            pivot = spread(cols[q], q)
            scale = jnp.where(sub == q, pivot, scale)
            if q < 7:
                mult = jnp.where(sub > q, cols[q] / pivot, 0.0)
                r = r - mult * spread(r, q)
                e = e - mult * spread(e, q)
                for p in range(q + 1, 8):
                    cols[p] = cols[p] - mult * spread(cols[p], q)
        scale = lax.rsqrt(scale)
        r, e = r * scale, e * scale
        inv[g] = e
        if g < groups - 1:
            turned = r.T
            r_rows = [spread(r, q) for q in range(8)]
            e_rows = [spread(e, q) for q in range(8)]
            for h in range(g + 1, groups):
                x, y = rows[h], inv[h]
                for q in range(8):
                    m = jnp.broadcast_to(turned[8 * h : 8 * h + 8, q : q + 1], (8, T))
                    x = x - m * r_rows[q]
                    y = y - m * e_rows[q]
                rows[h], inv[h] = x, y
    return jnp.concatenate(inv, axis=0)


def factor_kernel(gram_ref, power_ref, q_ref, a, high, low):
    width = gram_ref.shape[0]
    left, right = slice(0, width), slice(width, 2 * width)
    a[...] = gram_ref[...]
    q_ref[...] = power_ref[...].astype(F32)

    def panel(i, carry):
        here = pl.ds(pl.multiple_of(i * T, T), T)
        inverse = split(base_factor(a[here, here]))
        u = dot3(inverse, split(a[here, :]), ((1,), (0,)))
        w = dot3(inverse, split(q_ref[here, :]), ((1,), (0,)))
        q_ref[here, :] = w
        high[:, left], low[:, left] = split(u)
        high[:, right], low[:, right] = split(w)

        def trail(j, inner):
            there = pl.ds(pl.multiple_of(j * T, T), T)
            m = (high[:, there], low[:, there])
            a[there, :] -= dot3(m, (high[:, left], low[:, left]), ((0,), (0,)))
            q_ref[there, :] -= dot3(m, (high[:, right], low[:, right]), ((0,), (0,)))
            return inner

        lax.fori_loop(i + 1, width // T, trail, 0)
        return carry

    lax.fori_loop(0, width // T, panel, 0)


def orthogonal(gram, power_t):
    width = gram.shape[0]
    return pl.pallas_call(
        factor_kernel,
        out_shape=jax.ShapeDtypeStruct((width, width), F32),
        in_specs=[pl.BlockSpec(memory_space=pltpu.VMEM)] * 2,
        out_specs=pl.BlockSpec(memory_space=pltpu.VMEM),
        scratch_shapes=[
            pltpu.VMEM((width, width), F32),
            pltpu.VMEM((T, 2 * width), BF),
            pltpu.VMEM((T, 2 * width), BF),
        ],
        compiler_params=pltpu.CompilerParams(vmem_limit_bytes=40 * 2**20),
    )(gram, power_t)


def dot(a, b, a_dim, b_dim):
    return lax.dot_general(a, b, (((a_dim,), (b_dim,)), ((), ())), preferred_element_type=F32)


def quad_exchange(pieces):
    return lax.all_to_all(pieces, QUAD, split_axis=0, concat_axis=0, tiled=True)


def per_device(
    grads, block_slot, left_stats, right_stats, left_basis, right_basis, first_moment, second_moment
):
    capacity, row_count, width = left_stats.shape
    group_size = lax.axis_size("dp")
    owner_index = lax.axis_index("dp")
    block_total = block_slot.shape[0]
    slot_total = capacity * group_size
    side, core = lax.axis_index("s"), lax.axis_index("c")
    ring_index = lax.axis_index(RING)
    local_grads = grads[0]
    slot_ids = owner_index * capacity + jnp.arange(capacity, dtype=jnp.int32)
    held = jnp.any(block_slot[:, None] == slot_ids[None, :], axis=0)
    local_index = block_slot - owner_index * capacity
    owned = (local_index >= 0) & (local_index < capacity)
    safe_index = jnp.clip(local_index, 0, capacity - 1)

    sent = jnp.concatenate(
        [
            jnp.concatenate([left_stats, right_stats], axis=0).astype(BF),
            jnp.concatenate([left_basis, right_basis], axis=0),
        ],
        axis=1,
    )
    got = quad_exchange(sent)
    got = got.reshape(4, 2, row_count, width).transpose(1, 0, 2, 3).reshape(2, 4 * row_count, width)
    old = lax.all_gather(got, RING, axis=1, tiled=True)
    old_stat, old_basis = old[0], old[1]
    moments = jnp.concatenate([first_moment, second_moment], axis=1).astype(BF)
    moments = quad_exchange(jnp.concatenate([moments, moments], axis=0))
    moments = moments.reshape(4, 2, row_count, width).astype(F32)
    first_old = moments[:, 0].reshape(4 * row_count, width)
    second_old = moments[:, 1].reshape(4 * row_count, width)

    placing = (
        block_slot[:, None] == lax.broadcasted_iota(jnp.int32, (block_total, slot_total), 1)
    ).astype(BF)
    slot_grads = jnp.einsum("bs,brc->src", placing, local_grads, preferred_element_type=F32)
    grad_rows = lax.psum_scatter(slot_grads.astype(BF), "dp", scatter_dimension=0, tiled=True)
    mine = jnp.where(core == 0, grad_rows[0], grad_rows[1])
    other = jnp.where(core == 0, grad_rows[1], grad_rows[0])
    came = lax.ppermute(other, "c", [(0, 1), (1, 0)])
    pair = jnp.where(core == 0, jnp.stack([mine, came]), jnp.stack([came, mine]))
    grad = lax.all_gather(
        pair.reshape(2 * row_count, width), ("y", "h", "s"), axis=0, tiled=True
    )

    term = lax.cond(
        side == 0, lambda g: dot(g, g, 1, 1), lambda g: dot(g, g, 0, 0), grad
    )
    stat = (BETA_STATS * old_stat.astype(F32) + (1.0 - BETA_STATS) * term).astype(BF)
    power_t = dot(old_basis, stat, 0, 0).astype(BF)
    gram = dot(power_t, power_t, 1, 1)
    q_t = orthogonal(gram, power_t)
    q_half = q_t.astype(BF)

    term_rows = lax.dynamic_slice_in_dim(term, ring_index * 4 * row_count, 4 * row_count, 0)
    terms = quad_exchange(term_rows.reshape(4, row_count, width))
    held_mask = held[:, None, None]
    new_left_stats = jnp.where(
        held_mask, BETA_STATS * left_stats + (1.0 - BETA_STATS) * terms[:2], left_stats
    )
    new_right_stats = jnp.where(
        held_mask, BETA_STATS * right_stats + (1.0 - BETA_STATS) * terms[2:], right_stats
    )

    q_cols = lax.dynamic_slice_in_dim(q_half, ring_index * 4 * row_count, 4 * row_count, 1)
    q_part = lax.dynamic_slice_in_dim(q_half, ring_index * 4 * row_count, 4 * row_count, 0)
    both = jnp.concatenate(
        [q_cols.T.reshape(4, row_count, width), q_part.reshape(4, row_count, width)], axis=1
    )
    both = quad_exchange(both)
    bases = both[:, :row_count]
    new_left_basis = jnp.where(held_mask, bases[:2], left_basis)
    new_right_basis = jnp.where(held_mask, bases[2:], right_basis)

    def to_home(slot_rows):
        picked = jnp.take(slot_rows, safe_index, axis=0)
        arrived = lax.all_to_all(
            jnp.where(owned[:, None, None], picked, jnp.zeros_like(picked)),
            "dp",
            split_axis=0,
            concat_axis=0,
            tiled=True,
        )
        return lax.all_gather(jnp.sum(arrived, axis=0), MP, axis=0, tiled=True)

    q_home = to_home(both[:2, row_count:])

    left_part = lax.ppermute(q_part, "s", [(0, 1), (1, 0)])
    moved = dot(grad, q_half, 1, 1).astype(BF)
    rotated = dot(left_part, moved, 1, 0)
    first_next = BETA_FIRST * first_old + (1.0 - BETA_FIRST) * rotated
    second_next = BETA_SECOND * second_old + (1.0 - BETA_SECOND) * rotated * rotated
    normed = first_next / (jnp.sqrt(second_next) + EPSILON)
    half = dot(normed.astype(BF), q_half, 1, 0).astype(BF)
    halves = quad_exchange(half.reshape(4, row_count, width))[2:]
    half_home = to_home(halves)
    update = dot(q_home, half_home, 0, 0).astype(BF)
    return (update[None], new_left_stats, new_right_stats, new_left_basis, new_right_basis)


def solution(mesh):
    groups = mesh.shape["dp"]
    fine = Mesh(mesh.devices.reshape(groups, 4, 2, 2, 2), ("dp",) + MP)
    rows = P("dp", MP, None)
    return jax.shard_map(
        per_device,
        mesh=fine,
        in_specs=(P("dp", None, MP, None), P()) + (rows,) * 6,
        out_specs=(P("dp", None, None),) + (rows,) * 4,
        check_vma=False,
    )
```

time: 1840 us -> 449 us (0.24)
  other arithmetic: 1070 us -> 9.37 us
  matrix products: 284 us -> 29.6 us
  local copies, waits for them, and re-layouts: 119 us -> 7.3 us
  Pallas kernels: 0 us -> 67.6 us
  waiting for transfers between devices: 310 us -> 246 us
  blocking collectives: 24 us -> 50.7 us
  starting transfers between devices: 0.54 us -> 24.4 us
    another operation x60 -> x2, other arithmetic: 1040 us -> 0.03 us  [the longest x28 357 us: advance(): jnp.linalg.cholesky(jnp.einsum('kij,kil->kjl', right_power, right_power,...]
    another operation x58 -> x0, matrix products: 193 us -> none  [the longest x30 112 us: single(): return jax.scipy.linalg.solve_triangular(one_factor, identity, lower=True)]
    all_gather x7 -> x4, waiting for transfers between devices: 271 us -> 187 us  [the longest x2 78 us: to_home(): return lax.all_gather(jnp.sum(arrived, axis=0), MP, axis=0, tiled=True)]
    another operation x68 -> x0, local copies, waits for them, and re-layouts: 82.3 us -> none  [the longest x52 63.3 us: single(): return jax.scipy.linalg.solve_triangular(one_factor, identity, lower=True)]
    pallas_call x0 -> x1, Pallas kernels: none -> 67.6 us  [orthogonal(): pl.pallas_call(factor_kernel, out_shape=jax.ShapeDtypeStruct((width, widt...]
    dot_general x16 -> x7, matrix products: 90.9 us -> 29.6 us  [the longest x6 28.3 us: dot(): lax.dot_general(a, b, (((a_dim,), (b_dim,)), ((), ())), preferred_element...]
    all_to_all x1 -> x3, blocking collectives: 24 us -> 50.7 us  [the longest x2 39.5 us: to_home(): lax.all_to_all(jnp.where(owned[:, None, None], picked, jnp.zeros_like(pic...]
    div x2 -> x0, other arithmetic: 24.1 us -> none  [the longest x1 12.1 us: advance(): jnp.linalg.cholesky(jnp.einsum('kij,kil->kjl', right_power, right_power,...]
  transfers between devices with their start and end apart: 8 -> 11, of which waited for: 7 -> 10; matrix products, arithmetic and copies ran while one was open for 20% -> 3% of each run, Pallas kernels for 0% -> 0%
where the time goes in v1:
time: 449 us
  waiting for transfers between devices  246 us (55%)
  Pallas kernels  67.6 us (15%)
  blocking collectives  50.7 us (11%)
  matrix products  29.6 us (7%)
  starting transfers between devices  24.4 us (5%)
  between operations  14 us (3%)
  other arithmetic  9.37 us (2%)
  local copies, waits for them, and re-layouts  7.3 us (2%)
    all_gather x2, waiting for transfers between devices, to_home(): return lax.all_gather(jnp.sum(arrived, axis=0), MP, axis=0, tiled=True)  78 us
    pallas_call x1, Pallas kernels, orthogonal(): pl.pallas_call(factor_kernel, out_shape=jax.ShapeDtypeStruct((width, widt...  67.6 us
    all_gather x1, waiting for transfers between devices, per_device(): old = lax.all_gather(got, RING, axis=1, tiled=True)  61.5 us
    all_gather x1, waiting for transfers between devices, per_device(): lax.all_gather(pair.reshape(2 * row_count, width), ('y', 'h', 's'), axis=...  47.7 us
    all_to_all x2, blocking collectives, to_home(): lax.all_to_all(jnp.where(owned[:, None, None], picked, jnp.zeros_like(pic...  39.5 us
    reduce_scatter x1, waiting for transfers between devices, per_device(): lax.psum_scatter(slot_grads.astype(BF), 'dp', scatter_dimension=0, tiled=...  37.6 us
    dot_general x6, matrix products, dot(): lax.dot_general(a, b, (((a_dim,), (b_dim,)), ((), ())), preferred_element...  28.3 us
    all_to_all x4, waiting for transfers between devices, quad_exchange(): return lax.all_to_all(pieces, QUAD, split_axis=0, concat_axis=0, tiled=True)  20 us
  transfers between devices with their start and end apart: 11, of which 10 were waited for; matrix products, arithmetic and copies ran while one was open for 3% of the time, Pallas kernels for 0%

profile of v1, /device:TPU:1, one launch (start us, length us, event | category | flops | bytes accessed | tf_op | source)
XLA Modules:
  0.0 448.7 jit_solution(10062185335304840687)
XLA Ops:
  7.2 0.0 copy-start
  7.2 0.0 reduce-scatter.2.cloned.1.call-start
  7.2 1.0 copy-done
  8.2 1.2 convolution_convert_fusion
  9.4 1.5 copy.43
  11.0 0.0 reduce-scatter.2.cloned.1.call-update
  11.0 0.0 all-gather.7.cloned.1.call-start
  11.1 37.6 %reduce-scatter.2.cloned.1.call-done = bf16[2,32,1024]{2,1,0:T(8,128)(2,1)} async-done(((bf16[16,32,1024]{2,1,0:T(8,128)(2,1)}), bf16[2,32,1024]{2,1,0:T(8,128)(2,1)}) %reduce-scatter.2.cloned.1.call-update) | async-done | bytes 131088 | tf_op jit(solution)/shard_map/reduce_scatter | solution.py:166
  48.7 0.9 broadcast_select_fusion
  49.6 5.7 %collective-permute-start = (bf16[32,1024]{1,0:T(8,128)(2,1)S(1)}, bf16[32,1024]{1,0:T(8,128)(2,1)S(1)}, u32[]{:S(2)}, u32[]{:S(2)}) collective-permute-start(bf16[32,1024]{1,0:T(8,128)(2,1)S(1)} %get-tuple-element.23), channel_id=1, source_target_pairs={{0,1},{1,0},{2,3},{3,2},{4,5},{5,4},{6,7},{7,6},{8,9},{9,8},{10,11... | collective-permute-start | bytes 196616 | tf_op jit(solution)/shard_map/ppermute | solution.py:169
  55.3 0.9 collective-permute-done
  56.2 0.7 maximum_select_fusion
  56.8 0.0 all-gather.7.cloned.1.call-update
  56.9 47.7 %all-gather.7.cloned.1.call-done = bf16[1024,1024]{1,0:T(8,128)(2,1)} async-done(((bf16[64,1024]{1,0:T(8,128)(2,1)}), bf16[1024,1024]{1,0:T(8,128)(2,1)}) %all-gather.7.cloned.1.call-update) | async-done | bytes 2097168 | tf_op jit(solution)/shard_map/all_gather | solution.py:171
  104.6 6.6 %conditional.1 = (f32[1024,1024]{1,0:T(8,128)}) conditional(s32[]{:T(128)} %convert_element_type.45, bf16[1024,1024]{1,0:T(8,128)(2,1)} %all-gather.7.cloned.1.call-done, bf16[1024,1024]{1,0:T(8,128)(2,1)} %all-gather.7.cloned.1.call-done), branch_computations={%region_1.2_spmd, %region_2.3_spmd} | conditional | flops 2147483648 | bytes 6291464 | solution.py:175
  104.6 6.6 %fusion.35 = f32[1024,1024]{1,0:T(8,128)} fusion(bf16[1024,1024]{1,0:T(8,128)(2,1)} %param.1), kind=kOutput, calls=%fused_computation.59 | convolution fusion | flops 2147483648 | bytes 6291456 | tf_op jit(solution)/shard_map/cond/branch_1_fun/dot_general | solution.py:121
  111.2 0.0 copy-start.3
  111.2 2.0 constant_dynamic-slice_fusion
  113.2 4.9 %all-to-all-start.6 = ((f32[4,32,1024]{2,1,0:T(8,128)}), f32[4,32,1024]{2,1,0:T(8,128)S(1)}, u32[]{:S(2)}, u32[]{:S(2)}) async-start(f32[4,32,1024]{2,1,0:T(8,128)} %bitcast.19), calls=%async_computation.7 | async-start | bytes 1048576 | tf_op jit(solution)/shard_map/all_to_all | solution.py:125
  118.1 0.2 compare_reduce_fusion
  118.3 7.8 %all-to-all-done.6 = f32[4,32,1024]{2,1,0:T(8,128)S(1)} async-done(((f32[4,32,1024]{2,1,0:T(8,128)}), f32[4,32,1024]{2,1,0:T(8,128)S(1)}, u32[]{:S(2)}, u32[]{:S(2)}) %all-to-all-start.6) | async-done | bytes 524320 | tf_op jit(solution)/shard_map/all_to_all | solution.py:125
  126.1 1.0 fusion.26
  127.1 0.0 copy-done.3
  127.1 11.2 %all_to_all.35 = bf16[4,64,1024]{2,1,0:T(8,128)(2,1)S(1)} all-to-all(bf16[4,64,1024]{2,1,0:T(8,128)(2,1)S(1)} %maximum_maximum_fusion), channel_id=1, replica_groups=mesh['dp'=8,'y'=4,'h'=2,'s'=2,'c'=2] {'s','c'}, dimensions={0} | all-to-all | bytes 1048576 | tf_op jit(solution)/shard_map/all_to_all | solution.py:125
  138.4 0.9 copy.41
  139.2 0.0 all-gather.5.cloned.1.call-update
  139.2 0.0 copy-done.5
  139.3 0.9 maximum_maximum_fusion.1
  140.2 4.5 all-to-all-start.3
  144.7 8.0 %all-to-all-done.3 = bf16[4,64,1024]{2,1,0:T(8,128)(2,1)S(1)} async-done(((bf16[4,64,1024]{2,1,0:T(8,128)(2,1)}), bf16[4,64,1024]{2,1,0:T(8,128)(2,1)S(1)}, u32[]{:S(2)}, u32[]{:S(2)}) %all-to-all-start.3) | async-done | bytes 524320 | tf_op jit(solution)/shard_map/all_to_all | solution.py:125
  152.6 1.1 convert.19
  153.7 61.5 %all-gather.5.cloned.1.call-done = bf16[2,1024,1024]{2,1,0:T(8,128)(2,1)} async-done(((bf16[2,128,1024]{2,1,0:T(8,128)(2,1)}), bf16[2,1024,1024]{2,1,0:T(8,128)(2,1)}) %all-gather.5.cloned.1.call-update) | async-done | bytes 4194320 | tf_op jit(solution)/shard_map/all_gather | solution.py:154
  215.2 5.9 %fusion.8.power_ref = bf16[1024,1024]{1,0:T(8,128)(2,1)S(1)} fusion(f32[1024,1024]{1,0:T(8,128)} %get-tuple-element.27, bf16[2,1024,1024]{2,1,0:T(8,128)(2,1)} %all-gather.5.cloned.1.call-done), kind=kOutput, calls=%fused_computation.12 | convolution fusion | flops 2153775104 | bytes 10485760 | tf_op jit(solution)/shard_map/dot_general | solution.py:121
  221.1 2.4 fusion.36.gram_ref
  223.5 67.6 %shard_map.119 = f32[1024,1024]{1,0:T(8,128)S(1)} custom-call(f32[1024,1024]{1,0:T(8,128)S(1)} %fusion.36.gram_ref, bf16[1024,1024]{1,0:T(8,128)(2,1)S(1)} %fusion.8.power_ref), custom_call_target="tpu_custom_call" | custom-call | tf_op jit(solution)/shard_map/pallas_call | solution.py:106
  291.1 0.0 copy-start.1
  291.1 0.3 convert_element_type.49
  291.5 0.4 collective-permute-start.1
  291.8 0.5 copy-done.1
  292.3 1.1 fusion.18
  293.4 0.1 dynamic-slice_bitcast_fusion
  293.4 0.1 copy.44
  293.6 0.9 pad_maximum_fusion
  294.5 4.5 %all-to-all-start.1 = ((bf16[4,64,1024]{2,1,0:T(8,128)(2,1)}), bf16[4,64,1024]{2,1,0:T(8,128)(2,1)S(1)}, u32[]{:S(2)}, u32[]{:S(2)}) async-start(bf16[4,64,1024]{2,1,0:T(8,128)(2,1)} %pad_maximum_fusion), calls=%async_computation.2 | async-start | bytes 1048576 | tf_op jit(solution)/shard_map/all_to_all | solution.py:125
  299.0 0.0 collective-permute-done.1
  299.0 5.4 %fusion.22 = bf16[128,1024]{1,0:T(8,128)(2,1)} fusion(f32[4,1,32,1024]{3,2,0,1:T(8,128)} %get-tuple-element.14, bf16[128,1024]{1,0:T(8,128)(2,1)} %collective-permute-done.1, bf16[1024,1024]{1,0:T(8,128)(2,1)} %all-gather.7.cloned.1.call-done, bf16[1024,1024]{1,0:T(8,128)(2,1)S(1)} %convert_element_type.49, f32[4,1,32,1024]{3,2,0,1:T(8,128)} %get-tuple-element.13), kind=kOutput, calls=%fused_computation.32 | convolution fusion | flops 2418016256 | bytes 5767168 | tf_op jit(solution)/shard_map/dot_general | solution.py:121
  304.4 2.1 convolution_convert_fusion.1
  306.5 0.5 all-to-all-done.1
  307.0 4.3 all-to-all-start.4
  311.3 0.8 slice_select_fusion
  312.1 0.6 gather_fusion
  312.6 3.8 all-to-all-done.4
  316.4 0.6 gather_fusion.1
  317.0 0.2 select_select_fusion
  317.2 22.3 %all_to_all.36 = bf16[8,32,1024]{2,1,0:T(8,128)(2,1)S(1)} all-to-all(bf16[8,32,1024]{2,1,0:T(8,128)(2,1)S(1)} %get-tuple-element.24), channel_id=1, replica_groups=mesh['dp'=8,'y'=4,'h'=2,'s'=2,'c'=2] {'dp'}, dimensions={0} | all-to-all | bytes 1048576 | tf_op jit(solution)/shard_map/all_to_all | solution.py:206
  339.5 0.7 reduce_sum.25
  340.2 0.0 all-gather.11.cloned.1.call-update
  340.2 0.0 all-gather.9.cloned.1.call-start
  340.3 17.2 %all_to_all.37 = bf16[8,32,1024]{2,1,0:T(8,128)(2,1)S(1)} all-to-all(bf16[8,32,1024]{2,1,0:T(8,128)(2,1)S(1)} %get-tuple-element.25), channel_id=1, replica_groups=mesh['dp'=8,'y'=4,'h'=2,'s'=2,'c'=2] {'dp'}, dimensions={0} | all-to-all | bytes 1048576 | tf_op jit(solution)/shard_map/all_to_all | solution.py:206
  357.5 0.7 reduce_sum.24
  358.2 0.0 all-gather.9.cloned.1.call-update
  358.2 26.9 %all-gather.11.cloned.1.call-done = bf16[1024,1024]{1,0:T(8,128)(2,1)} async-done(((bf16[32,1024]{1,0:T(8,128)(2,1)}), bf16[1024,1024]{1,0:T(8,128)(2,1)}) %all-gather.11.cloned.1.call-update) | async-done | bytes 2097168 | tf_op jit(solution)/shard_map/all_gather | solution.py:213
  385.1 51.1 %all-gather.9.cloned.1.call-done = bf16[1024,1024]{1,0:T(8,128)(2,1)} async-done(((bf16[32,1024]{1,0:T(8,128)(2,1)}), bf16[1024,1024]{1,0:T(8,128)(2,1)}) %all-gather.9.cloned.1.call-update) | async-done | bytes 2097168 | tf_op jit(solution)/shard_map/all_gather | solution.py:213
  436.2 5.9 %convert_bitcast_fusion = bf16[1,1024,1024]{2,1,0:T(8,128)(2,1)} fusion(bf16[1024,1024]{1,0:T(8,128)(2,1)} %all-gather.9.cloned.1.call-done, bf16[1024,1024]{1,0:T(8,128)(2,1)} %all-gather.11.cloned.1.call-done), kind=kOutput, calls=%fused_computation.7 | convolution fusion | flops 2148532224 | bytes 6291456 | tf_op jit(solution)/shard_map/dot_general | solution.py:121
  (23 shorter events, 0.2 us)
Async XLA Ops:
  7.2 1.0 copy-start
  7.2 41.5 %reduce-scatter.2.cloned.1.call-start = ((), (), s32[]{:S(2)}) async-start(), calls=%async_computation.9 | async-start | bytes 1179648 | tf_op jit(solution)/shard_map/reduce_scatter | solution.py:166
  11.0 93.6 %all-gather.7.cloned.1.call-start = ((), (), s32[]{:S(2)}) async-start(), calls=%async_computation.10 | async-start | bytes 2228224 | tf_op jit(solution)/shard_map/all_gather | solution.py:171
  49.6 6.6 %collective-permute-start = (bf16[32,1024]{1,0:T(8,128)(2,1)S(1)}, bf16[32,1024]{1,0:T(8,128)(2,1)S(1)}, u32[]{:S(2)}, u32[]{:S(2)}) collective-permute-start(bf16[32,1024]{1,0:T(8,128)(2,1)S(1)} %get-tuple-element.23), channel_id=1, source_target_pairs={{0,1},{1,0},{2,3},{3,2},{4,5},{5,4},{6,7},{7,6},{8,9},{9,8},{10,11... | collective-permute-start | bytes 196616 | tf_op jit(solution)/shard_map/ppermute | solution.py:169
  111.2 6.9 %copy-start.9 = (s32[8]{0:T(128)S(1)}, s32[8]{0:T(128)}, u32[]{:S(2)}) copy-start(s32[8]{0:T(128)} %param.13) | copy-start | bytes 100
  111.2 14.9 %copy-start.7 = (f32[2,32,1024]{2,1,0:T(8,128)S(1)}, f32[2,32,1024]{2,1,0:T(8,128)}, u32[]{:S(2)}) copy-start(f32[2,32,1024]{2,1,0:T(8,128)} %param.15) | copy-start | bytes 786436
  111.2 14.9 %copy-start.8 = (f32[2,32,1024]{2,1,0:T(8,128)S(1)}, f32[2,32,1024]{2,1,0:T(8,128)}, u32[]{:S(2)}) copy-start(f32[2,32,1024]{2,1,0:T(8,128)} %param.14) | copy-start | bytes 786436
  111.2 15.9 %copy-start.2 = (bf16[2,32,1024]{2,1,0:T(8,128)(2,1)S(1)}, bf16[2,32,1024]{2,1,0:T(8,128)(2,1)}, u32[]{:S(2)}) copy-start(bf16[2,32,1024]{2,1,0:T(8,128)(2,1)} %param.17) | copy-start | bytes 393220
  111.2 15.9 %copy-start.3 = (bf16[2,32,1024]{2,1,0:T(8,128)(2,1)S(1)}, bf16[2,32,1024]{2,1,0:T(8,128)(2,1)}, u32[]{:S(2)}) copy-start(bf16[2,32,1024]{2,1,0:T(8,128)(2,1)} %param.16) | copy-start | bytes 393220
  113.2 12.9 %all-to-all-start.6 = ((f32[4,32,1024]{2,1,0:T(8,128)}), f32[4,32,1024]{2,1,0:T(8,128)S(1)}, u32[]{:S(2)}, u32[]{:S(2)}) async-start(f32[4,32,1024]{2,1,0:T(8,128)} %bitcast.19), calls=%async_computation.7 | async-start | bytes 1048576 | tf_op jit(solution)/shard_map/all_to_all | solution.py:125
  118.1 97.1 %all-gather.5.cloned.1.call-start = ((), (), s32[]{:S(2)}) async-start(), calls=%async_computation.8 | async-start | bytes 4718592 | tf_op jit(solution)/shard_map/all_gather | solution.py:154
  127.1 12.2 %copy-start.5 = (f32[2,32,1024]{2,1,0:T(8,128)S(1)}, f32[2,32,1024]{2,1,0:T(8,128)}, u32[]{:S(2)}) copy-start(f32[2,32,1024]{2,1,0:T(8,128)} %param.18) | copy-start | bytes 786436
  127.1 12.2 %copy-start.6 = (f32[2,32,1024]{2,1,0:T(8,128)S(1)}, f32[2,32,1024]{2,1,0:T(8,128)}, u32[]{:S(2)}) copy-start(f32[2,32,1024]{2,1,0:T(8,128)} %param.19) | copy-start | bytes 786436
  140.2 12.5 %all-to-all-start.3 = ((bf16[4,64,1024]{2,1,0:T(8,128)(2,1)}), bf16[4,64,1024]{2,1,0:T(8,128)(2,1)S(1)}, u32[]{:S(2)}, u32[]{:S(2)}) async-start(bf16[4,64,1024]{2,1,0:T(8,128)(2,1)} %maximum_maximum_fusion.1), calls=%async_computation.4 | async-start | bytes 1048576 | tf_op jit(solution)/shard_map/all_to_all | solution.py:125
  291.1 1.2 copy-start.1
  291.5 7.5 %collective-permute-start.1 = (bf16[128,1024]{1,0:T(8,128)(2,1)S(1)}, bf16[128,1024]{1,0:T(8,128)(2,1)}, u32[]{:S(2)}, u32[]{:S(2)}) collective-permute-start(bf16[128,1024]{1,0:T(8,128)(2,1)S(1)} %constant_dynamic-slice_fusion.1), channel_id=1, source_target_pairs={{0,2},{2,0},{1,3},{3,1},{4,6},{6,4},{5,7},{7,5},{8,10},{10,8},{9,1... | collective-permute-start | bytes 786440 | tf_op jit(solution)/shard_map/ppermute | solution.py:217
  294.5 12.5 %all-to-all-start.1 = ((bf16[4,64,1024]{2,1,0:T(8,128)(2,1)}), bf16[4,64,1024]{2,1,0:T(8,128)(2,1)S(1)}, u32[]{:S(2)}, u32[]{:S(2)}) async-start(bf16[4,64,1024]{2,1,0:T(8,128)(2,1)} %pad_maximum_fusion), calls=%async_computation.2 | async-start | bytes 1048576 | tf_op jit(solution)/shard_map/all_to_all | solution.py:125
  304.4 6.9 %copy-start.4 = (bf16[2,32,1024]{2,1,0:T(8,128)(2,1)S(1)}, bf16[2,32,1024]{2,1,0:T(8,128)(2,1)}, u32[]{:S(2)}) copy-start(bf16[2,32,1024]{2,1,0:T(8,128)(2,1)} %param.16) | copy-start | bytes 393220
  307.0 9.5 %all-to-all-start.4 = ((bf16[4,32,1024]{2,1,0:T(8,128)(2,1)}), bf16[4,32,1024]{2,1,0:T(8,128)(2,1)S(1)}, u32[]{:S(2)}, u32[]{:S(2)}) async-start(bf16[4,32,1024]{2,1,0:T(8,128)(2,1)} %bitcast.17), calls=%async_computation.5 | async-start | bytes 524288 | tf_op jit(solution)/shard_map/all_to_all | solution.py:125
  311.3 73.8 %all-gather.11.cloned.1.call-start = ((), (), s32[]{:S(2)}) async-start(), calls=%async_computation.12 | async-start | bytes 2162688 | tf_op jit(solution)/shard_map/all_gather | solution.py:213
  340.2 96.0 %all-gather.9.cloned.1.call-start = ((), (), s32[]{:S(2)}) async-start(), calls=%async_computation.11 | async-start | bytes 2162688 | tf_op jit(solution)/shard_map/all_gather | solution.py:213
Sparse Core Ops, SparseCore 0:
  11.1 37.5 reduce-scatter.1
  57.0 47.5 all-gather.6
  139.4 75.8 all-gather.4
  340.4 44.6 all-gather.10
  388.1 48.1 all-gather.8

commit v2 on v1

v2 whole, which is shorter than its diff:
```python
import functools

import jax
import jax.numpy as jnp
from jax import lax
from jax.experimental import pallas as pl
from jax.experimental.pallas import tpu as pltpu
from jax.sharding import Mesh
from jax.sharding import PartitionSpec as P

BETA_STATS = 0.95
BETA_FIRST = 0.9
BETA_SECOND = 0.95
EPSILON = 1e-08
F32 = jnp.float32
BF = jnp.bfloat16
T = 128
MP = ("yh", "k", "xh", "s", "c")
MESH = pl.DeviceIdType.MESH
ANY = pl.BlockSpec(memory_space=pl.ANY)


def split(x):
    high = x.astype(BF)
    return high, (x - high.astype(F32)).astype(BF)


def dot3(a_parts, b_parts, dims):
    (ah, al), (bh, bl) = a_parts, b_parts
    dot = functools.partial(
        lax.dot_general, dimension_numbers=(dims, ((), ())), preferred_element_type=F32
    )
    return dot(ah, bh) + (dot(ah, bl) + dot(al, bh))


def base_factor(block):
    sub = lax.broadcasted_iota(jnp.int32, (8, T), 0)
    lane = lax.broadcasted_iota(jnp.int32, (8, T), 1)
    groups = T // 8
    rows = [block[8 * g : 8 * g + 8, :] for g in range(groups)]
    inv = [(lane == sub + 8 * g).astype(F32) for g in range(groups)]

    def spread(x, q):
        return jnp.broadcast_to(x[q : q + 1, :], (8, T))

    for g in range(groups):
        r, e = rows[g], inv[g]
        cols = [jnp.broadcast_to(r[:, 8 * g + q : 8 * g + q + 1], (8, T)) for q in range(8)]
        scale = jnp.zeros((8, T), F32)
        for q in range(8):
            pivot = spread(cols[q], q)
            scale = jnp.where(sub == q, pivot, scale)
            if q < 7:
                mult = jnp.where(sub > q, cols[q] / pivot, 0.0)
                r = r - mult * spread(r, q)
                e = e - mult * spread(e, q)
                for p in range(q + 1, 8):
                    cols[p] = cols[p] - mult * spread(cols[p], q)
        scale = lax.rsqrt(scale)
        r, e = r * scale, e * scale
        inv[g] = e
        if g < groups - 1:
            turned = r.T
            r_rows = [spread(r, q) for q in range(8)]
            e_rows = [spread(e, q) for q in range(8)]
            for h in range(g + 1, groups):
                x, y = rows[h], inv[h]
                for q in range(8):
                    m = jnp.broadcast_to(turned[8 * h : 8 * h + 8, q : q + 1], (8, T))
                    x = x - m * r_rows[q]
                    y = y - m * e_rows[q]
                rows[h], inv[h] = x, y
    return jnp.concatenate(inv, axis=0)


def factor_kernel(gram_ref, power_ref, q_ref, a, high, low):
    width = gram_ref.shape[0]
    left, right = slice(0, width), slice(width, 2 * width)
    a[...] = gram_ref[...]
    q_ref[...] = power_ref[...].astype(F32)

    def panel(i, carry):
        here = pl.ds(pl.multiple_of(i * T, T), T)
        inverse = split(base_factor(a[here, here]))
        u = dot3(inverse, split(a[here, :]), ((1,), (0,)))
        w = dot3(inverse, split(q_ref[here, :]), ((1,), (0,)))
        q_ref[here, :] = w
        high[:, left], low[:, left] = split(u)
        high[:, right], low[:, right] = split(w)

        def trail(j, inner):
            there = pl.ds(pl.multiple_of(j * T, T), T)
            m = (high[:, there], low[:, there])
            a[there, :] -= dot3(m, (high[:, left], low[:, left]), ((0,), (0,)))
            q_ref[there, :] -= dot3(m, (high[:, right], low[:, right]), ((0,), (0,)))
            return inner

        lax.fori_loop(i + 1, width // T, trail, 0)
        return carry

    lax.fori_loop(0, width // T, panel, 0)


def orthogonal(gram, power_t):
    width = gram.shape[0]
    return pl.pallas_call(
        factor_kernel,
        out_shape=jax.ShapeDtypeStruct((width, width), F32),
        in_specs=[pl.BlockSpec(memory_space=pltpu.VMEM)] * 2,
        out_specs=pl.BlockSpec(memory_space=pltpu.VMEM),
        scratch_shapes=[
            pltpu.VMEM((width, width), F32),
            pltpu.VMEM((T, 2 * width), BF),
            pltpu.VMEM((T, 2 * width), BF),
        ],
        compiler_params=pltpu.CompilerParams(vmem_limit_bytes=40 * 2**20),
    )(gram, power_t)


def dot(a, b, a_dim, b_dim):
    return lax.dot_general(a, b, (((a_dim,), (b_dim,)), ((), ())), preferred_element_type=F32)


def chip_coords(t):
    return {"yh": t // 8, "k": (t // 4) % 2, "xh": (t // 2) % 2, "s": t % 2}


def place():
    yh, k, xh, s, c = (lax.axis_index(a) for a in MP)
    return ((yh * 2 + k) * 2 + xh) * 2 + s, c


def remote(src, dst, send, recv, coords):
    return pltpu.make_async_remote_copy(
        src_ref=src, dst_ref=dst, send_sem=send, recv_sem=recv, device_id=coords, device_id_type=MESH
    )


def greet(me, chip, core):
    barrier = pltpu.get_barrier_semaphore()

    def to_dp(j, carry):
        pl.semaphore_signal(barrier, inc=1, device_id={"dp": (me + j) % 8}, device_id_type=MESH)
        return carry

    def to_chip(j, carry):
        pl.semaphore_signal(
            barrier, inc=1, device_id=chip_coords((chip + j) % 16), device_id_type=MESH
        )
        return carry

    lax.fori_loop(1, 8, to_dp, 0)
    lax.fori_loop(1, 16, to_chip, 0)
    pl.semaphore_signal(barrier, inc=1, device_id={"c": 1 - core}, device_id_type=MESH)
    pl.semaphore_wait(barrier, 7 + 15 + 1)


def loop(low, high, body):
    def step(j, carry):
        body(j)
        return carry

    lax.fori_loop(low, high, step, 0)


def gather_kernel(
    slot_grads, state, moments, grad_out, stat_out, basis_out, moments_out,
    parts, total, dp_send, dp_recv, state_send, state_recv, quad_send, quad_recv,
    grad_send, grad_recv, pair_send, pair_recv, own,
):
    me = lax.axis_index("dp")
    chip, core = place()
    quad_base = chip - 4 * ((chip // 4) % 2) - chip % 2
    local = 2 * ((chip // 4) % 2) + chip % 2
    pair = {"c": 1 - core}
    greet(me, chip, core)

    def dp_copy(j, source):
        there = (me + j) % 8
        return remote(
            slot_grads.at[there], parts.at[source], dp_send.at[there], dp_recv.at[source], {"dp": there}
        )

    def state_copy(which, out, j, source):
        there = (chip + j) % 16
        return remote(
            state.at[(there // 4) % 2, there % 2, which],
            out.at[source, core],
            state_send.at[which, there],
            state_recv.at[which, source],
            chip_coords(there),
        )

    def quad_copy(j, source):
        number = (local + j) % 4
        there = quad_base + 4 * (number // 2) + number % 2
        return remote(
            moments.at[number // 2],
            moments_out.at[source],
            quad_send.at[number],
            quad_recv.at[source],
            chip_coords(there),
        )

    def grad_copy(j, source):
        there = (chip + j) % 16
        return remote(
            total.at[(there // 4) % 2],
            grad_out.at[source, core],
            grad_send.at[there],
            grad_recv.at[source],
            chip_coords(there),
        )

    loop(1, 8, lambda j: dp_copy(j, me).start())
    mine = pltpu.make_async_copy(slot_grads.at[me], parts.at[me], own.at[0])
    mine.start()
    k, s = (chip // 4) % 2, chip % 2
    keep = [
        pltpu.make_async_copy(state.at[k, s, 0], stat_out.at[chip, core], own.at[1]),
        pltpu.make_async_copy(state.at[k, s, 1], basis_out.at[chip, core], own.at[2]),
        pltpu.make_async_copy(moments.at[k], moments_out.at[local], own.at[3]),
    ]
    for copy in keep:
        copy.start()
    loop(1, 16, lambda j: state_copy(0, stat_out, j, chip).start())
    loop(1, 16, lambda j: state_copy(1, basis_out, j, chip).start())
    loop(1, 4, lambda j: quad_copy(j, local).start())

    mine.wait()
    loop(1, 8, lambda j: dp_copy(j, (me + 8 - j) % 8).wait_recv())
    for slot in range(2):
        acc = parts[0, slot].astype(F32)
        for d in range(1, 8):
            acc = acc + parts[d, slot].astype(F32)
        total[slot] = acc.astype(BF)
    loop(1, 16, lambda j: grad_copy(j, chip).start())
    last = pltpu.make_async_copy(total.at[k], grad_out.at[chip, core], own.at[4])
    last.start()

    def share(out, n):
        return remote(out.at[:, core], out.at[:, core], pair_send.at[n], pair_recv.at[n], pair)

    def shared(out, n):
        return remote(out.at[:, 1 - core], out.at[:, 1 - core], pair_send.at[n], pair_recv.at[n], pair)

    for copy in keep:
        copy.wait()
    loop(1, 16, lambda j: state_copy(0, stat_out, j, (chip + 16 - j) % 16).wait_recv())
    share(stat_out, 0).start()
    loop(1, 16, lambda j: state_copy(1, basis_out, j, (chip + 16 - j) % 16).wait_recv())
    share(basis_out, 1).start()
    last.wait()
    loop(1, 16, lambda j: grad_copy(j, (chip + 16 - j) % 16).wait_recv())
    share(grad_out, 2).start()
    loop(1, 4, lambda j: quad_copy(j, (local + 4 - j) % 4).wait_recv())
    for n, out in enumerate((stat_out, basis_out, grad_out)):
        shared(out, n).wait_recv()
        share(out, n).wait_send()
    loop(1, 8, lambda j: dp_copy(j, me).wait_send())
    loop(1, 16, lambda j: state_copy(0, stat_out, j, chip).wait_send())
    loop(1, 16, lambda j: state_copy(1, basis_out, j, chip).wait_send())
    loop(1, 16, lambda j: grad_copy(j, chip).wait_send())
    loop(1, 4, lambda j: quad_copy(j, local).wait_send())


def gather_inputs(slot_grads, state, moments):
    rows, width = state.shape[-2:]
    full = jax.ShapeDtypeStruct((16, 2, rows, width), BF)
    dma = pltpu.SemaphoreType.DMA
    return pl.pallas_call(
        gather_kernel,
        out_shape=(full, full, full, jax.ShapeDtypeStruct((4, 2, rows, width), BF)),
        in_specs=[ANY] * 3,
        out_specs=(ANY,) * 4,
        scratch_shapes=[
            pltpu.VMEM((8, 2, rows, width), BF),
            pltpu.VMEM((2, rows, width), BF),
            dma((8,)), dma((8,)), dma((2, 16)), dma((2, 16)), dma((4,)), dma((4,)),
            dma((16,)), dma((16,)), dma((3,)), dma((3,)), dma((5,)),
        ],
        compiler_params=pltpu.CompilerParams(
            collective_id=0, has_side_effects=True, vmem_limit_bytes=16 * 2**20
        ),
    )(slot_grads, state, moments)


def home_kernel(
    owned, payload, term, q, home_out, terms_out, bases_out,
    box, pieces, parts, total, dp_send, dp_recv, box_send, box_recv, row_send, row_recv,
    home_send, home_recv, pair_send, pair_recv, own,
):
    me = lax.axis_index("dp")
    chip, core = place()
    quad_base = chip - 4 * ((chip // 4) % 2) - chip % 2
    local = 2 * ((chip // 4) % 2) + chip % 2
    rows = payload.shape[1]
    pair = {"c": 1 - core}
    greet(me, chip, core)

    def member(number):
        return quad_base + 4 * (number // 2) + number % 2

    def box_copy(j, source):
        number = (local + j) % 4
        return remote(
            payload.at[number], box.at[source], box_send.at[number], box_recv.at[source],
            chip_coords(member(number)),
        )

    def row_copy(which, j, source):
        number = (local + j) % 4
        there = member(number)
        src, out = ((term, terms_out), (q, bases_out))[which]
        return remote(
            src.at[2 * there + core], out.at[source], row_send.at[which, number],
            row_recv.at[which, source], chip_coords(there),
        )

    def dp_copy(j, source):
        there = (me + j) % 8
        return remote(
            pieces.at[there], parts.at[source], dp_send.at[there], dp_recv.at[source], {"dp": there}
        )

    def home_copy(j, source):
        there = (chip + j) % 16
        return remote(
            total, home_out.at[:, source, core], home_send.at[there], home_recv.at[source],
            chip_coords(there),
        )

    loop(1, 4, lambda j: box_copy(j, local).start())
    mine = pltpu.make_async_copy(payload.at[local], box.at[local], own.at[0])
    mine.start()
    mine.wait()
    loop(1, 4, lambda j: box_copy(j, (local + 4 - j) % 4).wait_recv())

    def piece(b):
        first, second = owned[2 * b], owned[2 * b + 1]
        for which in range(2):
            pieces[b, which] = (
                box[which].astype(F32) * first + box[2 + which].astype(F32) * second
            ).astype(BF)

    def send_piece(j):
        piece((me + j) % 8)
        dp_copy(j, me).start()

    loop(1, 8, send_piece)
    piece(me)
    keep = [
        pltpu.make_async_copy(pieces.at[me], parts.at[me], own.at[1]),
        pltpu.make_async_copy(term.at[2 * chip + core], terms_out.at[local], own.at[2]),
        pltpu.make_async_copy(q.at[2 * chip + core], bases_out.at[local], own.at[3]),
    ]
    for copy in keep:
        copy.start()
    loop(1, 4, lambda j: row_copy(0, j, local).start())
    loop(1, 4, lambda j: row_copy(1, j, local).start())
    for copy in keep:
        copy.wait()
    loop(1, 8, lambda j: dp_copy(j, (me + 8 - j) % 8).wait_recv())
    for which in range(2):
        acc = parts[0, which].astype(F32)
        for d in range(1, 8):
            acc = acc + parts[d, which].astype(F32)
        total[which] = acc.astype(BF)
    loop(1, 16, lambda j: home_copy(j, chip).start())
    last = pltpu.make_async_copy(total, home_out.at[:, chip, core], own.at[4])
    last.start()
    last.wait()
    loop(1, 16, lambda j: home_copy(j, (chip + 16 - j) % 16).wait_recv())
    share = remote(
        home_out.at[:, :, core], home_out.at[:, :, core], pair_send.at[0], pair_recv.at[0], pair
    )
    share.start()
    other = 1 - core
    remote(
        home_out.at[:, :, other], home_out.at[:, :, other], pair_send.at[0], pair_recv.at[0], pair
    ).wait_recv()
    share.wait_send()
    for which in range(2):
        loop(1, 4, lambda j: row_copy(which, j, (local + 4 - j) % 4).wait_recv())
        loop(1, 4, lambda j: row_copy(which, j, local).wait_send())
    loop(1, 4, lambda j: box_copy(j, local).wait_send())
    loop(1, 8, lambda j: dp_copy(j, me).wait_send())
    loop(1, 16, lambda j: home_copy(j, chip).wait_send())


def bring_home(owned, payload, term, q):
    rows, width = payload.shape[-2:]
    dma = pltpu.SemaphoreType.DMA
    return pl.pallas_call(
        home_kernel,
        out_shape=(
            jax.ShapeDtypeStruct((2, 16, 2, rows, width), BF),
            jax.ShapeDtypeStruct((4, rows, width), F32),
            jax.ShapeDtypeStruct((4, rows, width), BF),
        ),
        in_specs=[pl.BlockSpec(memory_space=pltpu.SMEM), ANY, ANY, ANY],
        out_specs=(ANY,) * 3,
        scratch_shapes=[
            pltpu.VMEM((4, rows, width), BF),
            pltpu.VMEM((8, 2, rows, width), BF),
            pltpu.VMEM((8, 2, rows, width), BF),
            pltpu.VMEM((2, rows, width), BF),
            dma((8,)), dma((8,)), dma((4,)), dma((4,)), dma((2, 4)), dma((2, 4)),
            dma((16,)), dma((16,)), dma((1,)), dma((1,)), dma((5,)),
        ],
        compiler_params=pltpu.CompilerParams(
            collective_id=1, has_side_effects=True, vmem_limit_bytes=16 * 2**20
        ),
    )(owned, payload, term, q)


def per_device(
    grads, block_slot, left_stats, right_stats, left_basis, right_basis, first_moment, second_moment
):
    capacity, rows, width = left_stats.shape
    group_size = lax.axis_size("dp")
    block_total = block_slot.shape[0]
    slot_total = capacity * group_size
    side = lax.axis_index("s")
    slot_ids = lax.axis_index("dp") * capacity + jnp.arange(capacity, dtype=jnp.int32)
    owns = block_slot[:, None] == slot_ids[None, :]
    held_mask = jnp.any(owns, axis=0)[:, None, None]

    placing = (
        block_slot[:, None] == lax.broadcasted_iota(jnp.int32, (block_total, slot_total), 1)
    ).astype(BF)
    slot_grads = jnp.einsum("bs,brc->src", placing, grads[0], preferred_element_type=F32).astype(BF)
    stats = jnp.stack([left_stats, right_stats], axis=1).astype(BF)
    bases = jnp.stack([left_basis, right_basis], axis=1)
    grad, old_stat, old_basis, moments = gather_inputs(
        slot_grads.reshape(group_size, capacity, rows, width),
        jnp.stack([stats, bases], axis=2),
        jnp.stack([first_moment, second_moment], axis=1).astype(BF),
    )
    grad, old_stat, old_basis = (
        x.reshape(width, width) for x in (grad, old_stat, old_basis)
    )
    first_old = moments[:, 0].astype(F32).reshape(4 * rows, width)
    second_old = moments[:, 1].astype(F32).reshape(4 * rows, width)

    term = lax.cond(side == 0, lambda g: dot(g, g, 1, 1), lambda g: dot(g, g, 0, 0), grad)
    stat = (BETA_STATS * old_stat.astype(F32) + (1.0 - BETA_STATS) * term).astype(BF)
    power_t = dot(old_basis, stat, 0, 0).astype(BF)
    gram = dot(power_t, power_t, 1, 1)
    q_t = orthogonal(gram, power_t).astype(BF)

    yh, xh, core = (lax.axis_index(a) for a in ("yh", "xh", "c"))
    parts = q_t.reshape(2, 2, 2, 2, 2, rows, width)
    parts = lax.dynamic_index_in_dim(parts, yh, 0, keepdims=False)
    parts = lax.dynamic_index_in_dim(parts, xh, 1, keepdims=False)
    parts = lax.dynamic_index_in_dim(parts, core, 2, keepdims=False)
    q_part = parts.reshape(4 * rows, width)
    left_part = lax.ppermute(q_part, "s", [(0, 1), (1, 0)])
    moved = dot(grad, q_t, 1, 1).astype(BF)
    rotated = dot(left_part, moved, 1, 0)
    first_next = BETA_FIRST * first_old + (1.0 - BETA_FIRST) * rotated
    second_next = BETA_SECOND * second_old + (1.0 - BETA_SECOND) * rotated * rotated
    normed = first_next / (jnp.sqrt(second_next) + EPSILON)
    half = dot(normed.astype(BF), q_t, 1, 0).astype(BF)

    payload = jnp.where(side == 0, q_part, half).reshape(4, rows, width)
    home, terms, new_bases = bring_home(
        owns.astype(F32).reshape(block_total * capacity),
        payload,
        term.reshape(width // rows, rows, width),
        q_t.T.reshape(width // rows, rows, width),
    )
    home = home.reshape(2, width, width)
    update = dot(home[0], home[1], 0, 0).astype(BF)

    def merged(new, old):
        return jnp.where(held_mask, new, old)

    terms = terms.reshape(2, 2, rows, width)
    new_bases = new_bases.reshape(2, 2, rows, width)
    return (
        update[None],
        merged(BETA_STATS * left_stats + (1.0 - BETA_STATS) * terms[:, 0], left_stats),
        merged(BETA_STATS * right_stats + (1.0 - BETA_STATS) * terms[:, 1], right_stats),
        merged(new_bases[:, 0], left_basis),
        merged(new_bases[:, 1], right_basis),
    )


def solution(mesh):
    groups = mesh.shape["dp"]
    fine = Mesh(mesh.devices.reshape(groups, 2, 2, 2, 2, 2), ("dp",) + MP)
    rows = P("dp", MP, None)
    return jax.shard_map(
        per_device,
        mesh=fine,
        in_specs=(P("dp", None, MP, None), P()) + (rows,) * 6,
        out_specs=(P("dp", None, None),) + (rows,) * 4,
        check_vma=False,
    )
```

time: 449 us -> 244 us (0.54)
  waiting for transfers between devices: 246 us -> 0.01 us
  Pallas kernels: 67.6 us -> 193 us
  blocking collectives: 50.7 us -> 0 us
  starting transfers between devices: 24.4 us -> 1.55 us
  between operations: 14 us -> 0.95 us
  matrix products: 29.6 us -> 21.5 us
  other arithmetic: 9.37 us -> 14.7 us
  local copies, waits for them, and re-layouts: 7.3 us -> 12.4 us
    all_gather x4 -> x0, waiting for transfers between devices: 187 us -> none  [the longest x2 78 us: to_home(): return lax.all_gather(jnp.sum(arrived, axis=0), MP, axis=0, tiled=True)]
    pallas_call x0 -> x2, Pallas kernels: none -> 125 us  [the longest x1 68.7 us: bring_home(): pl.pallas_call(home_kernel, out_shape=(jax.ShapeDtypeStruct((2, 16, 2, ro...]
    all_to_all x3 -> x0, blocking collectives: 50.7 us -> none  [the longest x2 39.5 us: to_home(): lax.all_to_all(jnp.where(owned[:, None, None], picked, jnp.zeros_like(pic...]
    reduce_scatter x1 -> x0, waiting for transfers between devices: 37.6 us -> none  [per_device(): lax.psum_scatter(slot_grads.astype(BF), 'dp', scatter_dimension=0, tiled=...]
    all_to_all x4 -> x0, waiting for transfers between devices: 20 us -> none  [quad_exchange(): return lax.all_to_all(pieces, QUAD, split_axis=0, concat_axis=0, tiled=True)]
    all_to_all x4 -> x0, starting transfers between devices: 18.3 us -> none  [quad_exchange(): return lax.all_to_all(pieces, QUAD, split_axis=0, concat_axis=0, tiled=True)]
    dot_general x6, matrix products: 28.3 us -> 20.2 us  [dot(): lax.dot_general(a, b, (((a_dim,), (b_dim,)), ((), ())), preferred_element...]
    ppermute x1 -> x0, starting transfers between devices: 5.65 us -> none  [per_device(): came = lax.ppermute(other, 'c', [(0, 1), (1, 0)])]
  transfers between devices with their start and end apart: 11 -> 1, of which waited for: 10 -> 0; matrix products, arithmetic and copies ran while one was open for 3% -> 3% of each run, Pallas kernels for 0% -> 0%
where the time goes in v2:
time: 244 us
  Pallas kernels  193 us (79%)
  matrix products  21.5 us (9%)
  other arithmetic  14.7 us (6%)
  local copies, waits for them, and re-layouts  12.4 us (5%)
    pallas_call x1, Pallas kernels, bring_home(): pl.pallas_call(home_kernel, out_shape=(jax.ShapeDtypeStruct((2, 16, 2, ro...  68.7 us
    pallas_call x1, Pallas kernels, orthogonal(): pl.pallas_call(factor_kernel, out_shape=jax.ShapeDtypeStruct((width, widt...  67.6 us
    pallas_call x1, Pallas kernels, gather_inputs(): pl.pallas_call(gather_kernel, out_shape=(full, full, full, jax.ShapeDtype...  56.3 us
    dot_general x6, matrix products, dot(): lax.dot_general(a, b, (((a_dim,), (b_dim,)), ((), ())), preferred_element...  20.2 us
    unnamed x34, local copies, waits for them, and re-layouts  6.62 us
  transfers between devices with their start and end apart: 1, of which 0 were waited for; matrix products, arithmetic and copies ran while one was open for 3% of the time, Pallas kernels for 0%

profile of v2, /device:TPU:1, one launch (start us, length us, event | category | flops | bytes accessed | tf_op | source)
XLA Modules:
  0.0 243.7 jit_solution(6044463330555619062)
XLA Ops:
  0.6 0.0 copy-start
  0.6 0.0 copy-start.8
  0.7 0.0 copy-start.6
  0.7 1.0 copy-done
  1.7 0.0 copy-start.10
  1.7 0.0 copy-start.11
  1.7 1.3 convolution_convert_fusion.1
  3.0 0.0 copy-start.13
  3.0 0.0 copy-start.14
  3.0 0.6 copy.21
  3.6 0.0 copy-done.8
  3.6 0.0 copy-done.6
  3.6 0.0 copy-done.10
  3.6 0.0 copy-done.11
  3.7 0.2 copy-done.13
  3.9 0.1 copy-done.14
  4.1 0.1 pad_maximum_fusion.state
  4.1 56.3 %shard_map.119 = (bf16[16,2,32,1024]{3,2,1,0:T(8,128)(2,1)S(1)}, bf16[16,2,32,1024]{3,2,1,0:T(8,128)(2,1)S(1)}, bf16[16,2,32,1024]{3,2,1,0:T(8,128)(2,1)S(1)}, bf16[4,2,32,1024]{3,2,1,0:T(8,128)(2,1)S(1)}) custom-call(bf16[8,2,32,1024]{3,2,1,0:T(8,128)(2,1)S(1)} %bitcast.120, bf16[2,2,2,32,1024]{4,3,2,1,0:T(8,128)(2,1)S(1)} %pad_maximum_fusion.state, ...), custom_call_target="tpu_custom_call" | custom-call | tf_op jit(solution)/shard_map/pallas_call | solution.py:271
  60.5 0.0 copy-start.2
  60.5 1.3 copy-done.2
  61.8 0.0 copy-start.16
  61.8 2.6 %convert_multiply_fusion = f32[16,2,32,1024]{3,2,1,0:T(8,128)} fusion(bf16[16,2,32,1024]{3,2,1,0:T(8,128)(2,1)S(1)} %get-tuple-element.19), kind=kLoop, calls=%fused_computation.3 | loop fusion | flops 2097152 | bytes 6291456 | tf_op jit(solution)/shard_map/mul | solution.py:447
  64.4 0.0 copy-done.16
  64.4 6.5 %conditional.1 = (f32[1024,1024]{1,0:T(8,128)}, f32[32,32,1024]{2,1,0:T(8,128)S(1)}) conditional(s32[]{:T(128)} %convert_element_type.62, bf16[1024,1024]{1,0:T(8,128)(2,1)S(1)} %bitcast.130, bf16[1024,1024]{1,0:T(8,128)(2,1)S(1)} %bitcast.131), branch_computations={%region_0.0_spmd, %region_1.0_spmd} | conditional | flops 2147483648 | bytes 14680080 | solution.py:446
  64.4 4.4 %fusion.39 = f32[1024,1024]{1,0:T(8,128)} fusion(bf16[1024,1024]{1,0:T(8,128)(2,1)S(1)} %param.1), kind=kOutput, calls=%fused_computation.55 | convolution fusion | flops 2147483648 | bytes 6291456 | tf_op jit(solution)/shard_map/cond/branch_1_fun/dot_general | solution.py:121
  68.8 2.2 copy.37
  70.9 0.0 copy-start.4
  71.0 1.9 copy-done.4
  72.9 0.0 copy-start.3
  72.9 4.7 %fusion = bf16[1024,1024]{1,0:T(8,128)(2,1)S(1)} fusion(f32[16,2,32,1024]{3,2,1,0:T(8,128)} %convert_multiply_fusion, f32[1024,1024]{1,0:T(8,128)} %get-tuple-element.21), kind=kLoop, calls=%fused_computation.2 | loop fusion | flops 3145728 | bytes 10485760 | tf_op jit(solution)/shard_map/convert_element_type | solution.py:447
  77.6 0.0 copy-done.3
  77.6 2.4 convolution_convert_fusion.power_ref
  80.1 2.4 fusion.40.gram_ref
  82.4 67.6 %shard_map.120 = f32[1024,1024]{1,0:T(8,128)S(1)} custom-call(f32[1024,1024]{1,0:T(8,128)S(1)} %fusion.40.gram_ref, bf16[1024,1024]{1,0:T(8,128)(2,1)S(1)} %convolution_convert_fusion.power_ref), custom_call_target="tpu_custom_call" | custom-call | tf_op jit(solution)/shard_map/pallas_call | solution.py:106
  150.0 0.0 copy-start.1
  150.0 2.0 copy-done.1
  152.0 0.3 convert_element_type.65
  152.3 0.0 copy-start.5
  152.4 0.0 copy-start.15
  152.4 1.6 collective-permute-start
  154.0 3.9 %convert_bitcast_fusion.4 = bf16[1024,1024]{0,1:T(8,128)(2,1)} fusion(f32[1024,1024]{1,0:T(8,128)} %copy-done.1), kind=kLoop, calls=%fused_computation.57 | loop fusion | flops 1048576 | bytes 6291456 | tf_op jit(solution)/shard_map/transpose | solution.py:471
  157.9 0.0 copy-done.5
  157.9 0.0 copy-done.15
  157.9 0.1 compare_reduce_fusion
  158.0 2.9 %copy.22 = bf16[1024,1024]{1,0:T(8,128)(2,1)S(1)} copy(bf16[1024,1024]{0,1:T(8,128)(2,1)} %convert_bitcast_fusion.4) | data formatting | bytes 4194304 | tf_op jit(solution)/shard_map/transpose | solution.py:471
  160.8 0.1 reshape.138.owned
  160.9 1.1 convert_multiply_fusion.2
  162.1 0.0 collective-permute-done
  162.1 5.3 %fusion.22 = bf16[128,1024]{1,0:T(8,128)(2,1)S(1)} fusion(f32[4,1,32,1024]{3,2,1,0:T(8,128)} %get-tuple-element.30, bf16[128,1024]{1,0:T(8,128)(2,1)} %collective-permute-done, bf16[1024,1024]{1,0:T(8,128)(2,1)} %bitcast.132, bf16[1024,1024]{1,0:T(8,128)(2,1)} %copy-done.5, f32[4,1,32,1024]{3,2,1,0:T(8,128)} %get-tuple-element.29), kind=kOutput, calls=%fused_computation.25 | convolution fusion | flops 2418016256 | bytes 5767168 | tf_op jit(solution)/shard_map/dot_general | solution.py:121
  167.4 2.0 fusion.14
  169.4 68.7 %shard_map.121 = (bf16[2,16,2,32,1024]{4,3,2,1,0:T(8,128)(2,1)S(1)}, f32[4,32,1024]{2,1,0:T(8,128)S(1)}, bf16[4,32,1024]{2,1,0:T(8,128)(2,1)S(1)}) custom-call(f32[16]{0:T(128)S(1)} %reshape.138.owned, bf16[4,32,1024]{2,1,0:T(8,128)(2,1)S(1)} %bitcast.121, f32[32,32,1024]{2,1,0:T(8,128)} %copy-done.4, bf16[32,32,1024]{2,1,0:T(8,128)(2,1)S(1)} %bitcast.119), custom_call_target="tpu_custom_call" | custom-call | tf_op jit(solution)/shard_map/pallas_call | solution.py:394
  238.1 0.0 copy-start.7
  238.1 0.0 copy-start.9
  238.1 0.0 copy-start.12
  238.1 3.8 %fusion.7 = bf16[1,1024,1024]{2,1,0:T(8,128)(2,1)} fusion(bf16[2,16,2,32,1024]{4,3,2,1,0:T(8,128)(2,1)S(1)} %get-tuple-element.24), kind=kOutput, calls=%fused_computation.11 | convolution fusion | flops 2148532224 | bytes 6291456 | tf_op jit(solution)/shard_map/dot_general | solution.py:121
  241.9 0.0 copy-done.7
  241.9 0.0 copy-done.9
  241.9 1.0 fusion.28
  242.9 0.0 copy-done.12
  242.9 0.8 fusion.33
  (6 shorter events, 0.2 us)
Async XLA Ops:
  0.6 1.0 copy-start
  0.6 2.9 %copy-start.8 = (f32[2,32,1024]{2,1,0:T(8,128)S(1)}, f32[2,32,1024]{2,1,0:T(8,128)}, u32[]{:S(2)}) copy-start(f32[2,32,1024]{2,1,0:T(8,128)} %param.12) | copy-start | bytes 786436
  0.7 2.9 %copy-start.6 = (f32[2,32,1024]{2,1,0:T(8,128)S(1)}, f32[2,32,1024]{2,1,0:T(8,128)}, u32[]{:S(2)}) copy-start(f32[2,32,1024]{2,1,0:T(8,128)} %param.13) | copy-start | bytes 786436
  1.7 2.0 copy-start.10
  1.7 2.0 copy-start.11
  3.0 1.0 copy-start.13
  3.0 1.0 copy-start.14
  60.5 1.3 copy-start.2
  61.8 2.6 %copy-start.16 = (bf16[16,2,32,1024]{3,2,1,0:T(8,128)(2,1)}, bf16[16,2,32,1024]{3,2,1,0:T(8,128)(2,1)S(1)}, u32[]{:S(2)}) copy-start(bf16[16,2,32,1024]{3,2,1,0:T(8,128)(2,1)S(1)} %get-tuple-element.20) | copy-start | bytes 6291460
  70.9 1.9 copy-start.4
  72.9 4.7 %copy-start.3 = (bf16[16,2,32,1024]{3,2,1,0:T(8,128)(2,1)S(1)}, bf16[16,2,32,1024]{3,2,1,0:T(8,128)(2,1)}, u32[]{:S(2)}) copy-start(bf16[16,2,32,1024]{3,2,1,0:T(8,128)(2,1)} %copy-done.2) | copy-start | bytes 6291460
  150.0 2.0 copy-start.1
  152.3 5.5 %copy-start.5 = (bf16[1024,1024]{1,0:T(8,128)(2,1)}, bf16[1024,1024]{1,0:T(8,128)(2,1)S(1)}, u32[]{:S(2)}) copy-start(bf16[1024,1024]{1,0:T(8,128)(2,1)S(1)} %convert_element_type.65) | copy-start | bytes 6291460
  152.4 5.5 %copy-start.15 = (s32[8]{0:T(128)S(1)}, s32[8]{0:T(128)}, u32[]{:S(2)}) copy-start(s32[8]{0:T(128)} %param.11) | copy-start | bytes 100
  152.4 9.6 %collective-permute-start = (bf16[128,1024]{1,0:T(8,128)(2,1)S(1)}, bf16[128,1024]{1,0:T(8,128)(2,1)}, u32[]{:S(2)}, u32[]{:S(2)}) collective-permute-start(bf16[128,1024]{1,0:T(8,128)(2,1)S(1)} %bitcast.126), channel_id=1, source_target_pairs={{0,2},{2,0},{1,3},{3,1},{4,6},{6,4},{5,7},{7,5},{8,10},{10,8},{9,1... | collective-permute-start | bytes 786440 | tf_op jit(solution)/shard_map/ppermute | solution.py:458
  238.1 3.8 %copy-start.7 = (f32[2,32,1024]{2,1,0:T(8,128)S(1)}, f32[2,32,1024]{2,1,0:T(8,128)}, u32[]{:S(2)}) copy-start(f32[2,32,1024]{2,1,0:T(8,128)} %param.13) | copy-start | bytes 786436
  238.1 3.8 %copy-start.9 = (f32[2,32,1024]{2,1,0:T(8,128)S(1)}, f32[2,32,1024]{2,1,0:T(8,128)}, u32[]{:S(2)}) copy-start(f32[2,32,1024]{2,1,0:T(8,128)} %param.12) | copy-start | bytes 786436
  238.1 4.8 %copy-start.12 = (bf16[2,32,1024]{2,1,0:T(8,128)(2,1)S(1)}, bf16[2,32,1024]{2,1,0:T(8,128)(2,1)}, u32[]{:S(2)}) copy-start(bf16[2,32,1024]{2,1,0:T(8,128)(2,1)} %param.14) | copy-start | bytes 393220

commit v3 on v2

v3 whole, which is shorter than its diff:
```python
import functools

import jax
import jax.numpy as jnp
from jax import lax
from jax.experimental import pallas as pl
from jax.experimental.pallas import tpu as pltpu
from jax.sharding import Mesh
from jax.sharding import PartitionSpec as P

BETA_STATS = 0.95
BETA_FIRST = 0.9
BETA_SECOND = 0.95
EPSILON = 1e-08
F32 = jnp.float32
BF = jnp.bfloat16
T = 128
MP = ("yh", "k", "xh", "s", "c")
MESH = pl.DeviceIdType.MESH
ANY = pl.BlockSpec(memory_space=pl.ANY)


def split(x):
    high = x.astype(BF)
    return high, (x - high.astype(F32)).astype(BF)


def dot(a, b, a_dim, b_dim):
    return lax.dot_general(a, b, (((a_dim,), (b_dim,)), ((), ())), preferred_element_type=F32)


def reciprocal(x):
    r = pl.reciprocal(x, approx=True)
    return r * (2.0 - x * r)


def tree(terms):
    while len(terms) > 1:
        terms = [a + b for a, b in zip(terms[::2], terms[1::2])]
    return terms[0]


def base_factor(block, hook):
    sub = lax.broadcasted_iota(jnp.int32, (8, T), 0)
    lane = lax.broadcasted_iota(jnp.int32, (8, T), 1)
    groups = T // 8

    def spread(x, q):
        return jnp.broadcast_to(x[q : q + 1, :], (8, T))

    def column(x, at):
        return jnp.broadcast_to(x[:, at : at + 1], (8, T))

    eye = lax.broadcasted_iota(jnp.int32, (T, T), 0) == lax.broadcasted_iota(jnp.int32, (T, T), 1)
    diag = jnp.where(eye, block, 0.0)
    across = lax.rsqrt(jnp.sum(diag, axis=0, keepdims=True))
    down = jnp.sum(jnp.where(eye, jnp.broadcast_to(across, (T, T)), 0.0), axis=1, keepdims=True)
    block = block * across * down
    rows = [block[8 * g : 8 * g + 8, :] for g in range(groups)]
    inv = [(lane == sub + 8 * g).astype(F32) for g in range(groups)]
    out = []
    for g in range(groups):
        r, e = rows[g], inv[g]
        f = e
        cols = [column(r, 8 * g + q) for q in range(8)]
        scale = jnp.zeros((8, T), F32)
        coef = jnp.zeros((8, T), F32)
        for q in range(0, 8, 2):
            x, y = cols[q], cols[q + 1]
            a, b, c = spread(x, q), spread(x, q + 1), spread(y, q + 1)
            det = a * c - b * b
            rd = reciprocal(det)
            i11, i22, i12 = c * rd, a * rd, -(b * rd)
            root = lax.rsqrt(a)
            scale = jnp.where(sub == q, root, scale)
            scale = jnp.where(sub == q + 1, a * root * lax.rsqrt(det), scale)
            coef = jnp.where(sub == q + 1, b * root * root, coef)
            m0 = x * i11 + y * i12
            m1 = x * i12 + y * i22
            if q < 6:
                f = f - (
                    jnp.where(sub > q + 1, m0, 0.0) * spread(f, q)
                    + jnp.where(sub > q + 1, m1, 0.0) * spread(f, q + 1)
                )
            m0 = jnp.where(sub == q, 1.0 - i11, jnp.where(sub == q + 1, -i12, m0))
            m1 = jnp.where(sub == q, -i12, jnp.where(sub == q + 1, 1.0 - i22, m1))
            for p in range(q + 2, 8):
                cols[p] = cols[p] - (m0 * spread(cols[p], q) + m1 * spread(cols[p], q + 1))
            if g < groups - 1:
                r = r - (m0 * spread(r, q) + m1 * spread(r, q + 1))
                e = e - (m0 * spread(e, q) + m1 * spread(e, q + 1))
        out.append((f - coef * pltpu.roll(f, 1, 0)) * scale * across)
        hook(g)
        if g < groups - 1:
            rr = [spread(r, q) for q in range(8)]
            ee = [spread(e, q) for q in range(8)]
            for h in range(g + 1, groups):
                m = [column(rows[h], 8 * g + q) for q in range(8)]
                rows[h] = rows[h] - tree([m[q] * rr[q] for q in range(8)])
                inv[h] = inv[h] - tree([m[q] * ee[q] for q in range(8)])
    return jnp.concatenate(out, axis=0)


def loop(low, high, body):
    def step(j, carry):
        body(j)
        return carry

    lax.fori_loop(low, high, step, 0)


def core_kernel(
    where, grad, old_stat, basis, q_t, q_part, q_rows, term_rows, a, q, stat, mul, cat, d_ref, turned
):
    width = grad.shape[0]
    rows = q_part.shape[1]
    half = width // 4
    side, core, corner = where[0], where[1], where[2]

    def tile(j):
        return pl.ds(pl.multiple_of(j * half, half), half)

    @pl.when(side == 0)
    def _():
        def body(j):
            a[tile(j), :] = dot(grad[tile(j), :], grad[...], 1, 1)

        loop(0, 4, body)

    @pl.when(side != 0)
    def _():
        def body(j):
            a[tile(j), :] = dot(grad[:, tile(j)], grad[...], 0, 0)

        loop(0, 4, body)

    def owned_rows(n):
        chip = corner + 4 * (n // 2) + n % 2
        return pl.ds(pl.multiple_of((2 * chip + core) * rows, rows), rows)

    for n in range(4):
        term_rows[n] = a[owned_rows(n), :]

    def mix(j):
        stat[tile(j), :] = (
            BETA_STATS * old_stat[tile(j), :].astype(F32) + (1.0 - BETA_STATS) * a[tile(j), :]
        ).astype(BF)

    loop(0, 4, mix)

    def power(j):
        q[tile(j), :] = dot(basis[:, tile(j)], stat[...], 0, 0).astype(BF).astype(F32)

    loop(0, 4, power)

    def keep(j):
        stat[tile(j), :] = q[tile(j), :].astype(BF)

    loop(0, 4, keep)

    def gram(j):
        a[tile(j), :] = dot(stat[tile(j), :], stat[...], 1, 1)

    loop(0, 4, gram)

    mul[...] = jnp.zeros_like(mul)
    cat[...] = jnp.zeros_like(cat)
    d_ref[...] = a[0:T, 0:T]
    lane = lax.broadcasted_iota(jnp.int32, (T, width), 1)

    def trail(g):
        if g % 2 == 0:
            return
        start = g // 2 * T
        there = slice(start, start + T)
        m = mul[:, there]
        a[there, start:width] -= dot(m, cat[:, start:width], 0, 0)
        q[there, :] -= dot(m, cat[:, width : 2 * width], 0, 0)

    def panel(i):
        here = pl.ds(pl.multiple_of(i * T, T), T)
        high, low = split(base_factor(d_ref[...], trail))
        inverse = jnp.concatenate([high, low, high], axis=1)
        for ref, start in ((a, 0), (q, width)):
            high, low = split(ref[here, :])
            u = dot(inverse, jnp.concatenate([high, high, low], axis=0), 1, 0)
            high, low = split(u)
            part = slice(start, start + width)
            cat[0:T, part], cat[T : 2 * T, part], cat[2 * T : 3 * T, part] = high, high, low
            if start == 0:
                high, low = split(jnp.where(lane >= (i + 1) * T, u, 0.0))
                mul[0:T, :], mul[T : 2 * T, :], mul[2 * T : 3 * T, :] = high, low, high
            else:
                q[here, :] = u
        following = pl.ds(pl.multiple_of(jnp.minimum(i + 1, width // T - 1) * T, T), T)
        d_ref[...] = a[following, following] - dot(mul[:, following], cat[:, following], 0, 0)

    loop(0, width // T, panel)

    def out(j):
        q_t[tile(j), :] = q[tile(j), :].astype(BF)

    loop(0, 4, out)
    for n in range(4):
        q_part[n] = q[owned_rows(n), :].astype(BF)
    for k in range(2):
        columns = pl.ds(pl.multiple_of((corner + 4 * k) // 2 * T, T), T)
        turned[...] = q[:, columns].T
        for side_to in range(2):
            these = pl.ds(pl.multiple_of((2 * side_to + core) * rows, rows), rows)
            q_rows[2 * k + side_to] = turned[these, :].astype(BF)


def factored(where, grad, old_stat, basis, rows):
    width = grad.shape[0]
    vmem = pl.BlockSpec(memory_space=pltpu.VMEM)
    return pl.pallas_call(
        core_kernel,
        out_shape=(
            jax.ShapeDtypeStruct((width, width), BF),
            jax.ShapeDtypeStruct((4, rows, width), BF),
            jax.ShapeDtypeStruct((4, rows, width), BF),
            jax.ShapeDtypeStruct((4, rows, width), F32),
        ),
        in_specs=[pl.BlockSpec(memory_space=pltpu.SMEM), vmem, vmem, vmem],
        out_specs=(vmem,) * 4,
        scratch_shapes=[
            pltpu.VMEM((width, width), F32),
            pltpu.VMEM((width, width), F32),
            pltpu.VMEM((width, width), BF),
            pltpu.VMEM((3 * T, width), BF),
            pltpu.VMEM((3 * T, 2 * width), BF),
            pltpu.VMEM((T, T), F32),
            pltpu.VMEM((T, width), F32),
        ],
        compiler_params=pltpu.CompilerParams(vmem_limit_bytes=48 * 2**20),
    )(where, grad, old_stat, basis)


def chip_coords(t):
    return {"yh": t // 8, "k": (t // 4) % 2, "xh": (t // 2) % 2, "s": t % 2}


def place():
    yh, k, xh, s, c = (lax.axis_index(a) for a in MP)
    return ((yh * 2 + k) * 2 + xh) * 2 + s, c


def remote(src, dst, send, recv, coords):
    return pltpu.make_async_remote_copy(
        src_ref=src, dst_ref=dst, send_sem=send, recv_sem=recv, device_id=coords, device_id_type=MESH
    )


def greet(me, chip, core):
    barrier = pltpu.get_barrier_semaphore()

    def to_dp(j, carry):
        pl.semaphore_signal(barrier, inc=1, device_id={"dp": (me + j) % 8}, device_id_type=MESH)
        return carry

    def to_chip(j, carry):
        pl.semaphore_signal(
            barrier, inc=1, device_id=chip_coords((chip + j) % 16), device_id_type=MESH
        )
        return carry

    lax.fori_loop(1, 8, to_dp, 0)
    lax.fori_loop(1, 16, to_chip, 0)
    pl.semaphore_signal(barrier, inc=1, device_id={"c": 1 - core}, device_id_type=MESH)
    pl.semaphore_wait(barrier, 7 + 15 + 1)


def gather_kernel(
    slot_grads, state, moments, grad_out, stat_out, basis_out, moments_out,
    parts, total, dp_send, dp_recv, state_send, state_recv, quad_send, quad_recv,
    grad_send, grad_recv, pair_send, pair_recv, own,
):
    me = lax.axis_index("dp")
    chip, core = place()
    quad_base = chip - 4 * ((chip // 4) % 2) - chip % 2
    local = 2 * ((chip // 4) % 2) + chip % 2
    pair = {"c": 1 - core}
    greet(me, chip, core)

    def dp_copy(j, source):
        there = (me + j) % 8
        return remote(
            slot_grads.at[there], parts.at[source], dp_send.at[there], dp_recv.at[source], {"dp": there}
        )

    def state_copy(which, out, j, source):
        there = (chip + j) % 16
        return remote(
            state.at[(there // 4) % 2, there % 2, which],
            out.at[source, core],
            state_send.at[which, there],
            state_recv.at[which, source],
            chip_coords(there),
        )

    def quad_copy(j, source):
        number = (local + j) % 4
        there = quad_base + 4 * (number // 2) + number % 2
        return remote(
            moments.at[number // 2],
            moments_out.at[source],
            quad_send.at[number],
            quad_recv.at[source],
            chip_coords(there),
        )

    def grad_copy(j, source):
        there = (chip + j) % 16
        return remote(
            total.at[(there // 4) % 2],
            grad_out.at[source, core],
            grad_send.at[there],
            grad_recv.at[source],
            chip_coords(there),
        )

    loop(1, 8, lambda j: dp_copy(j, me).start())
    mine = pltpu.make_async_copy(slot_grads.at[me], parts.at[me], own.at[0])
    mine.start()
    k, s = (chip // 4) % 2, chip % 2
    keep = [
        pltpu.make_async_copy(state.at[k, s, 0], stat_out.at[chip, core], own.at[1]),
        pltpu.make_async_copy(state.at[k, s, 1], basis_out.at[chip, core], own.at[2]),
        pltpu.make_async_copy(moments.at[k], moments_out.at[local], own.at[3]),
    ]
    for copy in keep:
        copy.start()
    loop(1, 16, lambda j: state_copy(0, stat_out, j, chip).start())
    loop(1, 16, lambda j: state_copy(1, basis_out, j, chip).start())
    loop(1, 4, lambda j: quad_copy(j, local).start())

    mine.wait()
    loop(1, 8, lambda j: dp_copy(j, (me + 8 - j) % 8).wait_recv())
    for slot in range(2):
        acc = parts[0, slot].astype(F32)
        for d in range(1, 8):
            acc = acc + parts[d, slot].astype(F32)
        total[slot] = acc.astype(BF)
    loop(1, 16, lambda j: grad_copy(j, chip).start())
    last = pltpu.make_async_copy(total.at[k], grad_out.at[chip, core], own.at[4])
    last.start()

    def share(out, n):
        return remote(out.at[:, core], out.at[:, core], pair_send.at[n], pair_recv.at[n], pair)

    def shared(out, n):
        return remote(out.at[:, 1 - core], out.at[:, 1 - core], pair_send.at[n], pair_recv.at[n], pair)

    for copy in keep:
        copy.wait()
    loop(1, 16, lambda j: state_copy(0, stat_out, j, (chip + 16 - j) % 16).wait_recv())
    share(stat_out, 0).start()
    loop(1, 16, lambda j: state_copy(1, basis_out, j, (chip + 16 - j) % 16).wait_recv())
    share(basis_out, 1).start()
    last.wait()
    loop(1, 16, lambda j: grad_copy(j, (chip + 16 - j) % 16).wait_recv())
    share(grad_out, 2).start()
    loop(1, 4, lambda j: quad_copy(j, (local + 4 - j) % 4).wait_recv())
    for n, out in enumerate((stat_out, basis_out, grad_out)):
        shared(out, n).wait_recv()
        share(out, n).wait_send()
    loop(1, 8, lambda j: dp_copy(j, me).wait_send())
    loop(1, 16, lambda j: state_copy(0, stat_out, j, chip).wait_send())
    loop(1, 16, lambda j: state_copy(1, basis_out, j, chip).wait_send())
    loop(1, 16, lambda j: grad_copy(j, chip).wait_send())
    loop(1, 4, lambda j: quad_copy(j, local).wait_send())


def gather_inputs(slot_grads, state, moments):
    rows, width = state.shape[-2:]
    full = jax.ShapeDtypeStruct((16, 2, rows, width), BF)
    dma = pltpu.SemaphoreType.DMA
    return pl.pallas_call(
        gather_kernel,
        out_shape=(full, full, full, jax.ShapeDtypeStruct((4, 2, rows, width), BF)),
        in_specs=[ANY] * 3,
        out_specs=(ANY,) * 4,
        scratch_shapes=[
            pltpu.VMEM((8, 2, rows, width), BF),
            pltpu.VMEM((2, rows, width), BF),
            dma((8,)), dma((8,)), dma((2, 16)), dma((2, 16)), dma((4,)), dma((4,)),
            dma((16,)), dma((16,)), dma((3,)), dma((3,)), dma((5,)),
        ],
        compiler_params=pltpu.CompilerParams(
            collective_id=0, has_side_effects=True, vmem_limit_bytes=16 * 2**20
        ),
    )(slot_grads, state, moments)


def tail_kernel(
    owned, q_part, q_rows, term_rows, q_t, grad, moments, update, terms_out, bases_out,
    moved, left, half, box, pieces, parts, total, home,
    left_sem, box_send, box_recv, row_send, row_recv, dp_send, dp_recv, home_send, home_recv,
    pair_send, pair_recv, own,
):
    me = lax.axis_index("dp")
    chip, core = place()
    quad_base = chip - 4 * ((chip // 4) % 2) - chip % 2
    local = 2 * ((chip // 4) % 2) + chip % 2
    side = chip % 2
    width = grad.shape[0]
    rows = q_part.shape[1]
    greet(me, chip, core)

    def member(number):
        return quad_base + 4 * (number // 2) + number % 2

    def payload(which):
        return half if which else q_part

    def box_copy(which, number, source):
        return remote(
            payload(which).at[number], box.at[which, source], box_send.at[which, number],
            box_recv.at[which, source], chip_coords(member(number)),
        )

    def row_copy(which, j, source):
        number = (local + j) % 4
        src, out = ((term_rows, terms_out), (q_rows, bases_out))[which]
        return remote(
            src.at[number], out.at[source], row_send.at[which, number],
            row_recv.at[which, source], chip_coords(member(number)),
        )

    def dp_copy(which, j, source):
        there = (me + j) % 8
        return remote(
            pieces.at[which, there], parts.at[which, source], dp_send.at[which, there],
            dp_recv.at[which, source], {"dp": there},
        )

    def home_copy(which, j, source):
        there = (chip + j) % 16
        return remote(
            total.at[which], home.at[which, source, core], home_send.at[which, there],
            home_recv.at[which, source], chip_coords(there),
        )

    def share(which, part):
        return remote(
            home.at[which, :, part], home.at[which, :, part], pair_send.at[which],
            pair_recv.at[which], {"c": 1 - core},
        )

    left_copy = remote(q_part, left, left_sem.at[0], left_sem.at[1], {"s": 1 - side})

    def send_box(which):
        @pl.when(side == which)
        def _():
            loop(1, 4, lambda j: box_copy(which, (local + j) % 4, local).start())
            mine = pltpu.make_async_copy(payload(which).at[local], box.at[which, local], own.at[which])
            mine.start()
            mine.wait()

    def receive_box(which):
        for source in (which, which + 2):
            @pl.when(local != source)
            def _():
                box_copy(which, local, source).wait_recv()

        def piece(b):
            pieces[which, b] = (
                box[which, which].astype(F32) * owned[2 * b]
                + box[which, which + 2].astype(F32) * owned[2 * b + 1]
            ).astype(BF)

        def send_piece(j):
            piece((me + j) % 8)
            dp_copy(which, j, me).start()

        loop(1, 8, send_piece)
        piece(me)
        mine = pltpu.make_async_copy(pieces.at[which, me], parts.at[which, me], own.at[2 + which])
        mine.start()
        mine.wait()

    def gather_home(which):
        loop(1, 8, lambda j: dp_copy(which, j, (me + 8 - j) % 8).wait_recv())
        acc = parts[which, 0].astype(F32)
        for d in range(1, 8):
            acc = acc + parts[which, d].astype(F32)
        total[which] = acc.astype(BF)
        loop(1, 16, lambda j: home_copy(which, j, chip).start())
        mine = pltpu.make_async_copy(total.at[which], home.at[which, chip, core], own.at[4 + which])
        mine.start()
        mine.wait()

    @pl.when(side == 0)
    def _():
        left_copy.start()

    send_box(0)

    @pl.when(side == 1)
    def _():
        def body(j):
            tile = pl.ds(pl.multiple_of(j * (width // 4), width // 4), width // 4)
            moved[tile, :] = dot(grad[tile, :], q_t[...], 1, 1).astype(BF)

        loop(0, 4, body)

    receive_box(0)

    @pl.when(side == 1)
    def _():
        left_copy.wait_recv()
        for n in range(4):
            rotated = dot(left[n], moved[...], 1, 0)
            first = BETA_FIRST * moments[n, 0].astype(F32) + (1.0 - BETA_FIRST) * rotated
            second = (
                BETA_SECOND * moments[n, 1].astype(F32) + (1.0 - BETA_SECOND) * rotated * rotated
            )
            left[n] = (first / (jnp.sqrt(second) + EPSILON)).astype(BF)
        normed = left[...].reshape(4 * rows, width)
        half[...] = dot(normed, q_t[...], 1, 0).astype(BF).reshape(4, rows, width)

    send_box(1)
    receive_box(1)
    keep = [
        pltpu.make_async_copy(term_rows.at[local], terms_out.at[local], own.at[6]),
        pltpu.make_async_copy(q_rows.at[local], bases_out.at[local], own.at[7]),
    ]
    for copy in keep:
        copy.start()
    for which in range(2):
        loop(1, 4, lambda j: row_copy(which, j, local).start())
    for which in range(2):
        gather_home(which)
    for which in range(2):
        loop(1, 16, lambda j: home_copy(which, j, (chip + 16 - j) % 16).wait_recv())
        share(which, core).start()
    for which in range(2):
        share(which, 1 - core).wait_recv()
    n_tiles = 4
    step = width // n_tiles
    for j in range(n_tiles):
        tile = slice(j * step, (j + 1) * step)
        update[tile, :] = dot(
            home[0, :, :, :, tile].reshape(width, step), home[1].reshape(width, width), 0, 0
        ).astype(BF)

    for copy in keep:
        copy.wait()
    for which in range(2):
        loop(1, 4, lambda j: row_copy(which, j, (local + 4 - j) % 4).wait_recv())
        loop(1, 4, lambda j: row_copy(which, j, local).wait_send())
        loop(1, 8, lambda j: dp_copy(which, j, me).wait_send())
        loop(1, 16, lambda j: home_copy(which, j, chip).wait_send())
        share(which, core).wait_send()

        @pl.when(side == which)
        def _():
            loop(1, 4, lambda j: box_copy(which, (local + j) % 4, local).wait_send())

    @pl.when(side == 0)
    def _():
        left_copy.wait_send()


def rotate_and_gather(owned, q_part, q_rows, term_rows, q_t, grad, moments):
    rows, width = q_part.shape[-2:]
    dma = pltpu.SemaphoreType.DMA
    vmem = pl.BlockSpec(memory_space=pltpu.VMEM)
    return pl.pallas_call(
        tail_kernel,
        out_shape=(
            jax.ShapeDtypeStruct((width, width), BF),
            jax.ShapeDtypeStruct((4, rows, width), F32),
            jax.ShapeDtypeStruct((4, rows, width), BF),
        ),
        in_specs=[pl.BlockSpec(memory_space=pltpu.SMEM), ANY, ANY, ANY, vmem, vmem, vmem],
        out_specs=(vmem, ANY, ANY),
        scratch_shapes=[
            pltpu.VMEM((width, width), BF),
            pltpu.VMEM((4, rows, width), BF),
            pltpu.VMEM((4, rows, width), BF),
            pltpu.VMEM((2, 4, rows, width), BF),
            pltpu.VMEM((2, 8, rows, width), BF),
            pltpu.VMEM((2, 8, rows, width), BF),
            pltpu.VMEM((2, rows, width), BF),
            pltpu.VMEM((2, 16, 2, rows, width), BF),
            dma((2,)), dma((2, 4)), dma((2, 4)), dma((2, 4)), dma((2, 4)), dma((2, 8)), dma((2, 8)),
            dma((2, 16)), dma((2, 16)), dma((2,)), dma((2,)), dma((8,)),
        ],
        compiler_params=pltpu.CompilerParams(
            collective_id=1, has_side_effects=True, vmem_limit_bytes=40 * 2**20
        ),
    )(owned, q_part, q_rows, term_rows, q_t, grad, moments)


def per_device(
    grads, block_slot, left_stats, right_stats, left_basis, right_basis, first_moment, second_moment
):
    capacity, rows, width = left_stats.shape
    group_size = lax.axis_size("dp")
    block_total = block_slot.shape[0]
    slot_total = capacity * group_size
    side = lax.axis_index("s")
    slot_ids = lax.axis_index("dp") * capacity + jnp.arange(capacity, dtype=jnp.int32)
    owns = block_slot[:, None] == slot_ids[None, :]
    held_mask = jnp.any(owns, axis=0)[:, None, None]

    placing = (
        block_slot[:, None] == lax.broadcasted_iota(jnp.int32, (block_total, slot_total), 1)
    ).astype(BF)
    slot_grads = jnp.einsum("bs,brc->src", placing, grads[0], preferred_element_type=F32).astype(BF)
    stats = jnp.stack([left_stats, right_stats], axis=1).astype(BF)
    bases = jnp.stack([left_basis, right_basis], axis=1)
    grad, old_stat, old_basis, moments = gather_inputs(
        slot_grads.reshape(group_size, capacity, rows, width),
        jnp.stack([stats, bases], axis=2),
        jnp.stack([first_moment, second_moment], axis=1).astype(BF),
    )
    grad, old_stat, old_basis = (
        x.reshape(width, width) for x in (grad, old_stat, old_basis)
    )

    yh, xh, core = (lax.axis_index(axis) for axis in ("yh", "xh", "c"))
    where = jnp.stack([side, core, 8 * yh + 2 * xh]).astype(jnp.int32)
    q_t, q_part, q_rows, term_rows = factored(where, grad, old_stat, old_basis, rows)
    update, terms, new_bases = rotate_and_gather(
        owns.astype(F32).reshape(block_total * capacity), q_part, q_rows, term_rows, q_t, grad, moments
    )

    def merged(new, old):
        return jnp.where(held_mask, new, old)

    terms = terms.reshape(2, 2, rows, width)
    new_bases = new_bases.reshape(2, 2, rows, width)
    return (
        update[None],
        merged(BETA_STATS * left_stats + (1.0 - BETA_STATS) * terms[:, 0], left_stats),
        merged(BETA_STATS * right_stats + (1.0 - BETA_STATS) * terms[:, 1], right_stats),
        merged(new_bases[:, 0], left_basis),
        merged(new_bases[:, 1], right_basis),
    )


def solution(mesh):
    groups = mesh.shape["dp"]
    fine = Mesh(mesh.devices.reshape(groups, 2, 2, 2, 2, 2), ("dp",) + MP)
    rows = P("dp", MP, None)
    return jax.shard_map(
        per_device,
        mesh=fine,
        in_specs=(P("dp", None, MP, None), P()) + (rows,) * 6,
        out_specs=(P("dp", None, None),) + (rows,) * 4,
        check_vma=False,
    )
```

time: 244 us -> 201 us (0.82)
  matrix products: 21.5 us -> 0.57 us
  other arithmetic: 14.7 us -> 4.16 us
  Pallas kernels: 193 us -> 184 us
    dot_general x6 -> x0, matrix products: 20.2 us -> none  [dot(): lax.dot_general(a, b, (((a_dim,), (b_dim,)), ((), ())), preferred_element...]
    pallas_call x2, Pallas kernels: 136 us -> 127 us  [the longest x1 64.4 us: factored(): pl.pallas_call(core_kernel, out_shape=(jax.ShapeDtypeStruct((width, width...]
    convert_element_type x2 -> x0, other arithmetic: 5.03 us -> none  [the longest x1 4.7 us: per_device(): (BETA_STATS * old_stat.astype(F32) + (1.0 - BETA_STATS) * term).astype(BF)]
    transpose x1 -> x0, other arithmetic: 3.91 us -> none  [per_device(): q_t.T.reshape(width // rows, rows, width)]
    unnamed x34 -> x33, local copies, waits for them, and re-layouts: 6.62 us -> 10.4 us
    mul x2 -> x0, other arithmetic: 3.76 us -> none  [the longest x1 2.62 us: per_device(): BETA_STATS * old_stat.astype(F32) + (1.0 - BETA_STATS) * term]
    transpose x1 -> x0, local copies, waits for them, and re-layouts: 2.85 us -> none  [per_device(): q_t.T.reshape(width // rows, rows, width)]
  transfers between devices with their start and end apart: 1 -> 0, of which waited for: 0 -> 0; matrix products, arithmetic and copies ran while one was open for 3% -> 0% of each run, Pallas kernels for 0% -> 0%
where the time goes in v3:
time: 201 us; the launch traced here: 200 us
  Pallas kernels  184 us (92%)
  local copies, waits for them, and re-layouts  11.1 us (6%)
  other arithmetic  4.16 us (2%)
    pallas_call x1, Pallas kernels, factored(): pl.pallas_call(core_kernel, out_shape=(jax.ShapeDtypeStruct((width, width...  64.4 us
    pallas_call x1, Pallas kernels, rotate_and_gather(): pl.pallas_call(tail_kernel, out_shape=(jax.ShapeDtypeStruct((width, width...  63.1 us
    pallas_call x1, Pallas kernels, gather_inputs(): pl.pallas_call(gather_kernel, out_shape=(full, full, full, jax.ShapeDtype...  56.3 us
    unnamed x33, local copies, waits for them, and re-layouts  10.4 us

profile of v3, /device:TPU:1, one launch (start us, length us, event | category | flops | bytes accessed | tf_op | source)
XLA Modules:
  0.0 200.4 jit_solution(11278023745770396082)
XLA Ops:
  0.6 0.0 copy-start
  0.6 0.0 copy-start.14
  0.7 0.0 copy-start.13
  0.7 0.0 copy-start.15
  0.7 0.1 pad_add_fusion.where
  0.8 1.1 convert_bitcast_fusion.2
  1.9 1.0 maximum_bitcast_fusion
  2.9 0.1 pad_maximum_fusion.state
  3.0 0.0 copy-done.14
  3.0 0.0 copy-done.13
  3.1 0.0 copy-done
  3.1 0.0 copy-done.15
  3.1 0.6 convolution_convert_fusion
  3.7 0.6 copy.20
  4.2 56.3 %shard_map.119 = (bf16[16,2,32,1024]{3,2,1,0:T(8,128)(2,1)S(1)}, bf16[16,2,32,1024]{3,2,1,0:T(8,128)(2,1)S(1)}, bf16[16,2,32,1024]{3,2,1,0:T(8,128)(2,1)S(1)}, bf16[4,2,32,1024]{3,2,1,0:T(8,128)(2,1)S(1)}) custom-call(bf16[8,2,32,1024]{3,2,1,0:T(8,128)(2,1)S(1)} %bitcast.73, bf16[2,2,2,32,1024]{4,3,2,1,0:T(8,128)(2,1)S(1)} %pad_maximum_fusion.state, ...), custom_call_target="tpu_custom_call" | custom-call | tf_op jit(solution)/shard_map/pallas_call | solution.py:379
  60.6 0.0 copy-start.3
  60.6 1.3 copy-done.3
  61.9 0.0 copy-start.4
  61.9 1.3 copy-done.4
  63.2 64.4 %shard_map.120 = (bf16[1024,1024]{1,0:T(8,128)(2,1)S(1)}, bf16[4,32,1024]{2,1,0:T(8,128)(2,1)S(1)}, bf16[4,32,1024]{2,1,0:T(8,128)(2,1)S(1)}, f32[4,32,1024]{2,1,0:T(8,128)S(1)}) custom-call(s32[3]{0:T(128)S(1)} %pad_add_fusion.where, bf16[1024,1024]{1,0:T(8,128)(2,1)S(1)} %bitcast.71, bf16[1024,1024]{1,0:T(8,128)(2,1)} %bitcast.74, bf16[1024,1024]{1,0:T(8,128)(2,1)} %bitcast.75), custom_call_target="tpu_custom_call" | custom-call | tf_op jit(solution)/shard_map/pallas_call | solution.py:217
  127.6 0.0 copy-start.1
  127.6 1.3 copy-done.1
  128.9 0.0 copy-start.5
  128.9 0.8 copy-done.5
  129.7 0.0 copy-start.7
  129.7 0.7 copy-done.7
  130.4 0.1 compare_reduce_fusion
  130.5 0.1 reshape.83.owned
  130.6 0.0 copy-start.2
  130.6 1.6 copy-done.2
  132.2 0.0 copy-start.6
  132.2 1.0 copy-done.6
  133.2 0.0 copy-start.8
  133.2 0.9 copy-done.8
  134.2 0.0 copy-start.9
  134.2 0.0 copy-start.10
  134.2 0.0 copy-start.11
  134.2 0.0 copy-start.12
  134.2 63.1 %shard_map.121 = (bf16[1024,1024]{1,0:T(8,128)(2,1)S(1)}, f32[4,32,1024]{2,1,0:T(8,128)S(1)}, bf16[4,32,1024]{2,1,0:T(8,128)(2,1)S(1)}) custom-call(f32[16]{0:T(128)S(1)} %reshape.83.owned, bf16[4,32,1024]{2,1,0:T(8,128)(2,1)S(1)} %get-tuple-element.19.q_part, bf16[4,32,1024]{2,1,0:T(8,128)(2,1)S(1)} %copy-done.8, f32[4,32,1024]{2,1,0:T(8,128)S(1)} %copy-done.6, ...), custom_call_target="tpu_custom_call" | custom-call | tf_op jit(solution)/shard_map/pallas_call | solution.py:570
  197.3 0.0 copy-done.9
  197.3 0.0 copy-done.10
  197.3 1.0 fusion.4
  198.3 0.0 copy-done.11
  198.3 0.0 copy-done.12
  198.3 0.8 fusion.9
  199.1 1.3 copy.32
  (3 shorter events, 0.1 us)
Async XLA Ops:
  0.6 2.4 %copy-start = (bf16[1,8,32,1024]{3,2,1,0:T(8,128)(2,1)S(1)}, bf16[1,8,32,1024]{3,2,1,0:T(8,128)(2,1)}, u32[]{:S(2)}) copy-start(bf16[1,8,32,1024]{3,2,1,0:T(8,128)(2,1)} %param.8) | copy-start | bytes 1572868
  0.6 2.3 %copy-start.14 = (f32[2,32,1024]{2,1,0:T(8,128)S(1)}, f32[2,32,1024]{2,1,0:T(8,128)}, u32[]{:S(2)}) copy-start(f32[2,32,1024]{2,1,0:T(8,128)} %param.14) | copy-start | bytes 786436
  0.7 2.3 %copy-start.13 = (f32[2,32,1024]{2,1,0:T(8,128)S(1)}, f32[2,32,1024]{2,1,0:T(8,128)}, u32[]{:S(2)}) copy-start(f32[2,32,1024]{2,1,0:T(8,128)} %param.15) | copy-start | bytes 786436
  0.7 2.4 %copy-start.15 = (s32[8]{0:T(128)S(1)}, s32[8]{0:T(128)}, u32[]{:S(2)}) copy-start(s32[8]{0:T(128)} %param.9) | copy-start | bytes 100
  60.6 1.3 copy-start.3
  61.9 1.3 copy-start.4
  127.6 1.3 copy-start.1
  128.9 0.8 copy-start.5
  129.7 0.7 copy-start.7
  130.6 1.6 copy-start.2
  132.2 1.0 copy-start.6
  133.2 0.9 copy-start.8
  134.2 63.1 %copy-start.9 = (f32[2,32,1024]{2,1,0:T(8,128)S(1)}, f32[2,32,1024]{2,1,0:T(8,128)}, u32[]{:S(2)}) copy-start(f32[2,32,1024]{2,1,0:T(8,128)} %param.11) | copy-start | bytes 786436
  134.2 63.1 %copy-start.10 = (f32[2,32,1024]{2,1,0:T(8,128)S(1)}, f32[2,32,1024]{2,1,0:T(8,128)}, u32[]{:S(2)}) copy-start(f32[2,32,1024]{2,1,0:T(8,128)} %param.10) | copy-start | bytes 786436
  134.2 64.1 %copy-start.11 = (bf16[2,32,1024]{2,1,0:T(8,128)(2,1)S(1)}, bf16[2,32,1024]{2,1,0:T(8,128)(2,1)}, u32[]{:S(2)}) copy-start(bf16[2,32,1024]{2,1,0:T(8,128)(2,1)} %param.13) | copy-start | bytes 393220
  134.2 64.1 %copy-start.12 = (bf16[2,32,1024]{2,1,0:T(8,128)(2,1)S(1)}, bf16[2,32,1024]{2,1,0:T(8,128)(2,1)}, u32[]{:S(2)}) copy-start(bf16[2,32,1024]{2,1,0:T(8,128)(2,1)} %param.12) | copy-start | bytes 393220

commit v4 on v3

v4 whole, which is shorter than its diff:
```python
import functools

import jax
import jax.numpy as jnp
from jax import lax
from jax.experimental import pallas as pl
from jax.experimental.pallas import tpu as pltpu
from jax.sharding import Mesh
from jax.sharding import PartitionSpec as P

BETA_STATS = 0.95
BETA_FIRST = 0.9
BETA_SECOND = 0.95
EPSILON = 1e-08
F32 = jnp.float32
BF = jnp.bfloat16
T = 128
MP = ("yh", "k", "xh", "s", "c")
MESH = pl.DeviceIdType.MESH
ANY = pl.BlockSpec(memory_space=pl.ANY)


def split(x):
    high = x.astype(BF)
    return high, (x - high.astype(F32)).astype(BF)


def dot(a, b, a_dim, b_dim):
    return lax.dot_general(a, b, (((a_dim,), (b_dim,)), ((), ())), preferred_element_type=F32)


def reciprocal(x):
    r = pl.reciprocal(x, approx=True)
    return r * (2.0 - x * r)


def tree(terms):
    while len(terms) > 1:
        terms = [a + b for a, b in zip(terms[::2], terms[1::2])]
    return terms[0]


def base_factor(block, hook):
    sub = lax.broadcasted_iota(jnp.int32, (8, T), 0)
    lane = lax.broadcasted_iota(jnp.int32, (8, T), 1)
    groups = T // 8

    def spread(x, q):
        return jnp.broadcast_to(x[q : q + 1, :], (8, T))

    def column(x, at):
        return jnp.broadcast_to(x[:, at : at + 1], (8, T))

    eye = lax.broadcasted_iota(jnp.int32, (T, T), 0) == lax.broadcasted_iota(jnp.int32, (T, T), 1)
    diag = jnp.where(eye, block, 0.0)
    across = lax.rsqrt(jnp.sum(diag, axis=0, keepdims=True))
    down = jnp.sum(jnp.where(eye, jnp.broadcast_to(across, (T, T)), 0.0), axis=1, keepdims=True)
    block = block * across * down
    rows = [block[8 * g : 8 * g + 8, :] for g in range(groups)]
    inv = [(lane == sub + 8 * g).astype(F32) for g in range(groups)]
    out = []
    for g in range(groups):
        r, e = rows[g], inv[g]
        f = e
        cols = [column(r, 8 * g + q) for q in range(8)]
        scale = jnp.zeros((8, T), F32)
        coef = jnp.zeros((8, T), F32)
        for q in range(0, 8, 2):
            x, y = cols[q], cols[q + 1]
            a, b, c = spread(x, q), spread(x, q + 1), spread(y, q + 1)
            det = a * c - b * b
            rd = reciprocal(det)
            i11, i22, i12 = c * rd, a * rd, -(b * rd)
            root = lax.rsqrt(a)
            scale = jnp.where(sub == q, root, scale)
            scale = jnp.where(sub == q + 1, a * root * lax.rsqrt(det), scale)
            coef = jnp.where(sub == q + 1, b * root * root, coef)
            m0 = x * i11 + y * i12
            m1 = x * i12 + y * i22
            if q < 6:
                f = f - (
                    jnp.where(sub > q + 1, m0, 0.0) * spread(f, q)
                    + jnp.where(sub > q + 1, m1, 0.0) * spread(f, q + 1)
                )
            m0 = jnp.where(sub == q, 1.0 - i11, jnp.where(sub == q + 1, -i12, m0))
            m1 = jnp.where(sub == q, -i12, jnp.where(sub == q + 1, 1.0 - i22, m1))
            for p in range(q + 2, 8):
                cols[p] = cols[p] - (m0 * spread(cols[p], q) + m1 * spread(cols[p], q + 1))
            if g < groups - 1:
                r = r - (m0 * spread(r, q) + m1 * spread(r, q + 1))
                e = e - (m0 * spread(e, q) + m1 * spread(e, q + 1))
        out.append((f - coef * pltpu.roll(f, 1, 0)) * scale * across)
        hook(g)
        if g < groups - 1:
            rr = [spread(r, q) for q in range(8)]
            ee = [spread(e, q) for q in range(8)]
            for h in range(g + 1, groups):
                m = [column(rows[h], 8 * g + q) for q in range(8)]
                rows[h] = rows[h] - tree([m[q] * rr[q] for q in range(8)])
                inv[h] = inv[h] - tree([m[q] * ee[q] for q in range(8)])
    return jnp.concatenate(out, axis=0)


def loop(low, high, body):
    def step(j, carry):
        body(j)
        return carry

    lax.fori_loop(low, high, step, 0)


def chip_coords(t):
    return {"yh": t // 8, "k": (t // 4) % 2, "xh": (t // 2) % 2, "s": t % 2}


def place():
    yh, k, xh, s, c = (lax.axis_index(a) for a in MP)
    return ((yh * 2 + k) * 2 + xh) * 2 + s, c


def remote(src, dst, send, recv, coords):
    return pltpu.make_async_remote_copy(
        src_ref=src, dst_ref=dst, send_sem=send, recv_sem=recv, device_id=coords, device_id_type=MESH
    )


def greet(me, chip, core):
    barrier = pltpu.get_barrier_semaphore()

    def to_dp(j, carry):
        pl.semaphore_signal(barrier, inc=1, device_id={"dp": (me + j) % 8}, device_id_type=MESH)
        return carry

    def to_chip(j, carry):
        pl.semaphore_signal(
            barrier, inc=1, device_id=chip_coords((chip + j) % 16), device_id_type=MESH
        )
        return carry

    lax.fori_loop(1, 8, to_dp, 0)
    lax.fori_loop(1, 16, to_chip, 0)
    pl.semaphore_signal(barrier, inc=1, device_id={"c": 1 - core}, device_id_type=MESH)
    pl.semaphore_wait(barrier, 7 + 15 + 1)


def step_kernel(
    owned, slot_grads, state, moments, update, terms_out, bases_out,
    parts, total, grad, old_stat, basis, olds, a, q, stat, mul, cat, d_ref, turned,
    q_part, q_rows, term_rows, q_t, left, half, box, pieces, arrived, home_rows, home,
    dp_send, dp_recv, state_send, state_recv, quad_send, quad_recv, grad_send, grad_recv,
    left_sem, box_send, box_recv, row_send, row_recv, piece_send, piece_recv, home_send, home_recv,
    pair_send, pair_recv, own,
):
    me = lax.axis_index("dp")
    chip, core = place()
    k, side = (chip // 4) % 2, chip % 2
    corner = chip - 4 * k - side
    local = 2 * k + side
    rows, width = q_part.shape[1:]
    quarter = width // 4
    greet(me, chip, core)

    def member(number):
        return corner + 4 * (number // 2) + number % 2

    def dp_copy(j, source):
        there = (me + j) % 8
        return remote(
            slot_grads.at[there], parts.at[source], dp_send.at[there], dp_recv.at[source], {"dp": there}
        )

    def state_copy(which, j, source):
        there = (chip + j) % 16
        return remote(
            state.at[(there // 4) % 2, there % 2, which],
            (old_stat, basis)[which].at[source, core],
            state_send.at[which, there],
            state_recv.at[which, source],
            chip_coords(there),
        )

    def quad_copy(j, source):
        number = (local + j) % 4
        return remote(
            moments.at[number // 2], olds.at[source], quad_send.at[number], quad_recv.at[source],
            chip_coords(member(number)),
        )

    def grad_copy(j, source):
        there = (chip + j) % 16
        return remote(
            total.at[(there // 4) % 2], grad.at[source, core], grad_send.at[there],
            grad_recv.at[source], chip_coords(there),
        )

    def share(ref, part, n):
        return remote(
            ref.at[:, part], ref.at[:, part], pair_send.at[n], pair_recv.at[n], {"c": 1 - core}
        )

    loop(1, 8, lambda j: dp_copy(j, me).start())
    mine = pltpu.make_async_copy(slot_grads.at[me], parts.at[me], own.at[0])
    mine.start()
    keep = [
        pltpu.make_async_copy(state.at[k, side, 0], old_stat.at[chip, core], own.at[1]),
        pltpu.make_async_copy(state.at[k, side, 1], basis.at[chip, core], own.at[2]),
        pltpu.make_async_copy(moments.at[k], olds.at[local], own.at[3]),
    ]
    for copy in keep:
        copy.start()
    loop(1, 16, lambda j: state_copy(0, j, chip).start())
    loop(1, 16, lambda j: state_copy(1, j, chip).start())
    mine.wait()
    loop(1, 8, lambda j: dp_copy(j, (me + 8 - j) % 8).wait_recv())
    for slot in range(2):
        acc = parts[0, slot].astype(F32)
        for d in range(1, 8):
            acc = acc + parts[d, slot].astype(F32)
        total[slot] = acc.astype(BF)
    loop(1, 16, lambda j: grad_copy(j, chip).start())
    grad[chip, core] = total[k]
    loop(1, 4, lambda j: quad_copy(j, local).start())
    for copy in keep:
        copy.wait()
    for which, ref in enumerate((old_stat, basis)):
        loop(1, 16, lambda j: state_copy(which, j, (chip + 16 - j) % 16).wait_recv())
        share(ref, core, which).start()
    loop(1, 16, lambda j: grad_copy(j, (chip + 16 - j) % 16).wait_recv())
    share(grad, core, 2).start()
    for n, ref in ((2, grad), (0, old_stat), (1, basis)):
        share(ref, 1 - core, n).wait_recv()

    def tile(j):
        return pl.ds(pl.multiple_of(j * quarter, quarter), quarter)

    def row_tile(ref, j):
        return ref[pl.ds(j * 4, 4)].reshape(quarter, width)

    def column_tile(ref, j):
        return ref[:, :, :, tile(j)].reshape(width, quarter)

    def whole(ref):
        return ref[...].reshape(width, width)

    @pl.when(side == 0)
    def _():
        def body(j):
            a[tile(j), :] = dot(row_tile(grad, j), whole(grad), 1, 1)

        loop(0, 4, body)

    @pl.when(side != 0)
    def _():
        def body(j):
            a[tile(j), :] = dot(column_tile(grad, j), whole(grad), 0, 0)

        loop(0, 4, body)

    def owned_rows(n):
        return pl.ds(pl.multiple_of((2 * member(n) + core) * rows, rows), rows)

    def row_copy(which, j, source):
        number = (local + j) % 4
        src, out = ((term_rows, terms_out), (q_rows, bases_out))[which]
        return remote(
            src.at[number], out.at[source], row_send.at[which, number],
            row_recv.at[which, source], chip_coords(member(number)),
        )

    for n in range(4):
        term_rows[n] = a[owned_rows(n), :]
    loop(1, 4, lambda j: row_copy(0, j, local).start())
    kept_terms = pltpu.make_async_copy(term_rows.at[local], terms_out.at[local], own.at[4])
    kept_terms.start()

    def mix(j):
        stat[tile(j), :] = (
            BETA_STATS * row_tile(old_stat, j).astype(F32) + (1.0 - BETA_STATS) * a[tile(j), :]
        ).astype(BF)

    loop(0, 4, mix)

    def power(j):
        q[tile(j), :] = dot(column_tile(basis, j), stat[...], 0, 0).astype(BF).astype(F32)

    loop(0, 4, power)

    def keep_power(j):
        stat[tile(j), :] = q[tile(j), :].astype(BF)

    loop(0, 4, keep_power)

    def gram(j):
        a[tile(j), :] = dot(stat[tile(j), :], stat[...], 1, 1)

    loop(0, 4, gram)

    mul[...] = jnp.zeros_like(mul)
    cat[...] = jnp.zeros_like(cat)
    d_ref[...] = a[0:T, 0:T]
    lane = lax.broadcasted_iota(jnp.int32, (T, width), 1)

    def trail(g):
        if g % 2 == 0:
            return
        start = g // 2 * T
        there = slice(start, start + T)
        m = mul[:, there]
        a[there, start:width] -= dot(m, cat[:, start:width], 0, 0)
        q[there, :] -= dot(m, cat[:, width : 2 * width], 0, 0)

    def panel(i):
        here = pl.ds(pl.multiple_of(i * T, T), T)
        high, low = split(base_factor(d_ref[...], trail))
        inverse = jnp.concatenate([high, low, high], axis=1)
        for ref, start in ((a, 0), (q, width)):
            high, low = split(ref[here, :])
            u = dot(inverse, jnp.concatenate([high, high, low], axis=0), 1, 0)
            high, low = split(u)
            part = slice(start, start + width)
            cat[0:T, part], cat[T : 2 * T, part], cat[2 * T : 3 * T, part] = high, high, low
            if start == 0:
                high, low = split(jnp.where(lane >= (i + 1) * T, u, 0.0))
                mul[0:T, :], mul[T : 2 * T, :], mul[2 * T : 3 * T, :] = high, low, high
            else:
                q[here, :] = u
        following = pl.ds(pl.multiple_of(jnp.minimum(i + 1, width // T - 1) * T, T), T)
        d_ref[...] = a[following, following] - dot(mul[:, following], cat[:, following], 0, 0)

    loop(0, width // T, panel)

    def payload(which):
        return half if which else q_part

    def box_copy(which, number, source):
        return remote(
            payload(which).at[number], box.at[which, source], box_send.at[which, number],
            box_recv.at[which, source], chip_coords(member(number)),
        )

    def piece_copy(which, j, source):
        there = (me + j) % 8
        return remote(
            pieces.at[which, there], arrived.at[which, source], piece_send.at[which, there],
            piece_recv.at[which, source], {"dp": there},
        )

    def home_copy(which, j, source):
        there = (chip + j) % 16
        return remote(
            home_rows.at[which], home.at[which, source, core], home_send.at[which, there],
            home_recv.at[which, source], chip_coords(there),
        )

    left_copy = remote(q_part, left, left_sem.at[0], left_sem.at[1], {"s": 1 - side})

    def send_box(which):
        @pl.when(side == which)
        def _():
            loop(1, 4, lambda j: box_copy(which, (local + j) % 4, local).start())
            box[which, local] = payload(which)[local]

    def receive_box(which):
        for source in (which, which + 2):
            @pl.when(local != source)
            def _():
                box_copy(which, local, source).wait_recv()

        def piece(b):
            return (
                box[which, which].astype(F32) * owned[2 * b]
                + box[which, which + 2].astype(F32) * owned[2 * b + 1]
            ).astype(BF)

        def send_piece(j):
            there = (me + j) % 8
            pieces[which, there] = piece(there)
            piece_copy(which, j, me).start()

        loop(1, 8, send_piece)
        arrived[which, me] = piece(me)

    def gather_home(which):
        loop(1, 8, lambda j: piece_copy(which, j, (me + 8 - j) % 8).wait_recv())
        acc = arrived[which, 0].astype(F32)
        for d in range(1, 8):
            acc = acc + arrived[which, d].astype(F32)
        home_rows[which] = acc.astype(BF)
        loop(1, 16, lambda j: home_copy(which, j, chip).start())
        home[which, chip, core] = home_rows[which]

    for n in range(4):
        q_part[n] = q[owned_rows(n), :].astype(BF)

    @pl.when(side == 0)
    def _():
        left_copy.start()

    send_box(0)

    @pl.when(side == 1)
    def _():
        def cast(j):
            q_t[tile(j), :] = q[tile(j), :].astype(BF)

        def move(j):
            stat[tile(j), :] = dot(row_tile(grad, j), q_t[...], 1, 1).astype(BF)

        loop(0, 4, cast)
        loop(0, 4, move)

    receive_box(0)

    @pl.when(side == 1)
    def _():
        left_copy.wait_recv()

    loop(1, 4, lambda j: quad_copy(j, (local + 4 - j) % 4).wait_recv())

    @pl.when(side == 1)
    def _():
        def normalize(n):
            rotated = dot(left[n], stat[...], 1, 0)
            first = BETA_FIRST * olds[n, 0].astype(F32) + (1.0 - BETA_FIRST) * rotated
            second = (
                BETA_SECOND * olds[n, 1].astype(F32) + (1.0 - BETA_SECOND) * rotated * rotated
            )
            left[n] = (first / (jnp.sqrt(second) + EPSILON)).astype(BF)

        loop(0, 4, normalize)
        normed = left[...].reshape(4 * rows, width)
        half[...] = dot(normed, q_t[...], 1, 0).astype(BF).reshape(4, rows, width)

    send_box(1)
    receive_box(1)
    for slot in range(2):
        columns = pl.ds(pl.multiple_of((corner + 4 * slot) // 2 * T, T), T)
        turned[...] = q[:, columns].T
        for side_to in range(2):
            these = pl.ds(pl.multiple_of((2 * side_to + core) * rows, rows), rows)
            q_rows[2 * slot + side_to] = turned[these, :].astype(BF)
    gather_home(0)
    loop(1, 4, lambda j: row_copy(1, j, local).start())
    kept_bases = pltpu.make_async_copy(q_rows.at[local], bases_out.at[local], own.at[5])
    kept_bases.start()
    gather_home(1)
    for which in range(2):
        loop(1, 16, lambda j: home_copy(which, j, (chip + 16 - j) % 16).wait_recv())
        share(home.at[which], core, 3 + which).start()
    for which in range(2):
        share(home.at[which], 1 - core, 3 + which).wait_recv()

    def multiply(j):
        update[tile(j), :] = dot(
            home[0, :, :, :, tile(j)].reshape(width, quarter), home[1].reshape(width, width), 0, 0
        ).astype(BF)

    loop(0, 4, multiply)

    kept_terms.wait()
    kept_bases.wait()
    for which in range(2):
        loop(1, 4, lambda j: row_copy(which, j, (local + 4 - j) % 4).wait_recv())
        loop(1, 4, lambda j: row_copy(which, j, local).wait_send())
        loop(1, 8, lambda j: piece_copy(which, j, me).wait_send())
        loop(1, 16, lambda j: home_copy(which, j, chip).wait_send())
        loop(1, 16, lambda j: state_copy(which, j, chip).wait_send())
        share(home.at[which], core, 3 + which).wait_send()

        @pl.when(side == which)
        def _():
            loop(1, 4, lambda j: box_copy(which, (local + j) % 4, local).wait_send())

    for n, ref in enumerate((old_stat, basis, grad)):
        share(ref, core, n).wait_send()
    loop(1, 8, lambda j: dp_copy(j, me).wait_send())
    loop(1, 16, lambda j: grad_copy(j, chip).wait_send())
    loop(1, 4, lambda j: quad_copy(j, local).wait_send())

    @pl.when(side == 0)
    def _():
        left_copy.wait_send()


def optimizer_step(owned, slot_grads, state, moments):
    rows, width = state.shape[-2:]
    dma = pltpu.SemaphoreType.DMA
    vmem = pltpu.VMEM
    full = vmem((16, 2, rows, width), BF)
    return pl.pallas_call(
        step_kernel,
        out_shape=(
            jax.ShapeDtypeStruct((width, width), BF),
            jax.ShapeDtypeStruct((4, rows, width), F32),
            jax.ShapeDtypeStruct((4, rows, width), BF),
        ),
        in_specs=[pl.BlockSpec(memory_space=pltpu.SMEM), ANY, ANY, ANY],
        out_specs=(pl.BlockSpec(memory_space=vmem), ANY, ANY),
        scratch_shapes=[
            vmem((8, 2, rows, width), BF),
            vmem((2, rows, width), BF),
            full, full, full,
            vmem((4, 2, rows, width), BF),
            vmem((width, width), F32), vmem((width, width), F32), vmem((width, width), BF),
            vmem((3 * T, width), BF), vmem((3 * T, 2 * width), BF),
            vmem((T, T), F32), vmem((T, width), F32),
            vmem((4, rows, width), BF), vmem((4, rows, width), BF), vmem((4, rows, width), F32),
            vmem((width, width), BF),
            vmem((4, rows, width), BF), vmem((4, rows, width), BF),
            vmem((2, 4, rows, width), BF),
            vmem((2, 8, rows, width), BF), vmem((2, 8, rows, width), BF),
            vmem((2, rows, width), BF), vmem((2, 16, 2, rows, width), BF),
            dma((8,)), dma((8,)), dma((2, 16)), dma((2, 16)), dma((4,)), dma((4,)), dma((16,)), dma((16,)),
            dma((2,)), dma((2, 4)), dma((2, 4)), dma((2, 4)), dma((2, 4)), dma((2, 8)), dma((2, 8)),
            dma((2, 16)), dma((2, 16)), dma((5,)), dma((5,)), dma((6,)),
        ],
        compiler_params=pltpu.CompilerParams(
            collective_id=0, has_side_effects=True, vmem_limit_bytes=56 * 2**20
        ),
    )(owned, slot_grads, state, moments)


def per_device(
    grads, block_slot, left_stats, right_stats, left_basis, right_basis, first_moment, second_moment
):
    capacity, rows, width = left_stats.shape
    group_size = lax.axis_size("dp")
    block_total = block_slot.shape[0]
    slot_total = capacity * group_size
    slot_ids = lax.axis_index("dp") * capacity + jnp.arange(capacity, dtype=jnp.int32)
    owns = block_slot[:, None] == slot_ids[None, :]
    held_mask = jnp.any(owns, axis=0)[:, None, None]

    placing = (
        block_slot[:, None] == lax.broadcasted_iota(jnp.int32, (block_total, slot_total), 1)
    ).astype(BF)
    slot_grads = jnp.einsum("bs,brc->src", placing, grads[0], preferred_element_type=F32).astype(BF)
    stats = jnp.stack([left_stats, right_stats], axis=1).astype(BF)
    bases = jnp.stack([left_basis, right_basis], axis=1)
    update, terms, new_bases = optimizer_step(
        owns.astype(F32).reshape(block_total * capacity),
        slot_grads.reshape(group_size, capacity, rows, width),
        jnp.stack([stats, bases], axis=2),
        jnp.stack([first_moment, second_moment], axis=1).astype(BF),
    )

    def merged(new, old):
        return jnp.where(held_mask, new, old)

    terms = terms.reshape(2, 2, rows, width)
    new_bases = new_bases.reshape(2, 2, rows, width)
    return (
        update[None],
        merged(BETA_STATS * left_stats + (1.0 - BETA_STATS) * terms[:, 0], left_stats),
        merged(BETA_STATS * right_stats + (1.0 - BETA_STATS) * terms[:, 1], right_stats),
        merged(new_bases[:, 0], left_basis),
        merged(new_bases[:, 1], right_basis),
    )


def solution(mesh):
    groups = mesh.shape["dp"]
    fine = Mesh(mesh.devices.reshape(groups, 2, 2, 2, 2, 2), ("dp",) + MP)
    rows = P("dp", MP, None)
    return jax.shard_map(
        per_device,
        mesh=fine,
        in_specs=(P("dp", None, MP, None), P()) + (rows,) * 6,
        out_specs=(P("dp", None, None),) + (rows,) * 4,
        check_vma=False,
    )
```

time: 201 us -> 190 us (0.945)
  Pallas kernels: 184 us -> 176 us
  local copies, waits for them, and re-layouts: 11.1 us -> 3.51 us
  other arithmetic: 4.16 us -> 7.76 us
    unnamed x33 -> x19, local copies, waits for them, and re-layouts: 10.4 us -> 1.37 us
    pallas_call x3 -> x1, Pallas kernels: 184 us -> 176 us  [optimizer_step(): pl.pallas_call(step_kernel, out_shape=(jax.ShapeDtypeStruct((width, width...]
    select_n x2, other arithmetic: 1.76 us -> 3.91 us  [merged(): return jnp.where(held_mask, new, old)]
where the time goes in v4:
time: 190 us; the launch traced here: 189 us
  Pallas kernels  176 us (93%)
  other arithmetic  7.76 us (4%)
  local copies, waits for them, and re-layouts  3.51 us (2%)
    pallas_call x1, Pallas kernels, optimizer_step(): pl.pallas_call(step_kernel, out_shape=(jax.ShapeDtypeStruct((width, width...  176 us
    select_n x2, other arithmetic, merged(): return jnp.where(held_mask, new, old)  3.91 us

profile of v4, /device:TPU:1, one launch (start us, length us, event | category | flops | bytes accessed | tf_op | source)
XLA Modules:
  0.0 188.6 jit_solution(2408990253405135117)
XLA Ops:
  0.6 0.0 copy-start
  0.6 0.0 copy-start.7
  0.7 0.0 copy-start.6
  0.7 0.0 copy-start.8
  0.7 1.1 convert_bitcast_fusion.2
  1.8 1.0 maximum_bitcast_fusion
  2.8 0.9 pad_maximum_fusion.state
  3.7 0.0 copy-done.7
  3.7 0.0 copy-done.6
  3.7 0.7 pad_maximum_fusion.1.moments
  4.5 0.0 copy-done.8
  4.5 0.1 compare_reduce_fusion
  4.6 0.6 reshape.71.owned
  5.1 0.0 copy-done
  5.2 0.6 convolution_convert_fusion
  5.7 0.0 copy-start.2
  5.7 0.0 copy-start.3
  5.8 1.5 copy.20
  7.3 0.0 copy-start.4
  7.3 0.0 copy-start.5
  7.3 176.0 %shard_map.119 = (bf16[1024,1024]{1,0:T(8,128)(2,1)}, f32[4,32,1024]{2,1,0:T(8,128)}, bf16[4,32,1024]{2,1,0:T(8,128)(2,1)}) custom-call(f32[16]{0:T(128)} %reshape.71.owned, bf16[8,2,32,1024]{3,2,1,0:T(8,128)(2,1)} %bitcast.65, bf16[2,2,2,32,1024]{4,3,2,1,0:T(8,128)(2,1)} %pad_maximum_fusion.state, bf16[2,2,32,1024]{3,2,1,0:T(8,128)(2,1)} %pad_maximum_fusion.1.moments), custom_call_target="tpu_custom_call" | custom-call | tf_op jit(solution)/shard_map/pallas_call | solution.py:490
  183.3 0.0 copy-start.1
  183.3 0.0 copy-done.2
  183.3 0.0 copy-done.3
  183.3 2.1 %fusion.4 = (f32[2,32,1024]{2,1,0:T(8,128)}, f32[2,32,1024]{2,1,0:T(8,128)}) fusion(f32[2,32,1024]{2,1,0:T(8,128)S(1)} %copy-done.2, f32[2,2,32,1024]{3,2,1,0:T(8,128)} %bitcast.67, pred[2]{0:T(512)(128)(4,1)S(1)} %get-tuple-element.15, f32[2,32,1024]{2,1,0:T(8,128)S(1)} %copy-done.3), kind=kLoop, calls=%fused_computation.7 | loop fusion | flops 524288 | bytes 1572866 | tf_op jit(solution)/shard_map/jit(_where)/select_n | solution.py:548
  185.5 0.0 copy-done.4
  185.5 0.0 copy-done.5
  185.5 1.8 fusion.9
  187.2 0.0 copy-done.1
  187.2 1.3 copy.32
  (2 shorter events, 0.0 us)
Async XLA Ops:
  0.6 4.5 %copy-start = (bf16[1,8,32,1024]{3,2,1,0:T(8,128)(2,1)S(1)}, bf16[1,8,32,1024]{3,2,1,0:T(8,128)(2,1)}, u32[]{:S(2)}) copy-start(bf16[1,8,32,1024]{3,2,1,0:T(8,128)(2,1)} %param.8) | copy-start | bytes 1572868
  0.6 3.0 %copy-start.7 = (f32[2,32,1024]{2,1,0:T(8,128)S(1)}, f32[2,32,1024]{2,1,0:T(8,128)}, u32[]{:S(2)}) copy-start(f32[2,32,1024]{2,1,0:T(8,128)} %param.14) | copy-start | bytes 786436
  0.7 3.0 %copy-start.6 = (f32[2,32,1024]{2,1,0:T(8,128)S(1)}, f32[2,32,1024]{2,1,0:T(8,128)}, u32[]{:S(2)}) copy-start(f32[2,32,1024]{2,1,0:T(8,128)} %param.15) | copy-start | bytes 786436
  0.7 3.8 %copy-start.8 = (s32[8]{0:T(128)S(1)}, s32[8]{0:T(128)}, u32[]{:S(2)}) copy-start(s32[8]{0:T(128)} %param.9) | copy-start | bytes 100
  5.7 177.6 %copy-start.2 = (f32[2,32,1024]{2,1,0:T(8,128)S(1)}, f32[2,32,1024]{2,1,0:T(8,128)}, u32[]{:S(2)}) copy-start(f32[2,32,1024]{2,1,0:T(8,128)} %param.11) | copy-start | bytes 786436
  5.7 177.6 %copy-start.3 = (f32[2,32,1024]{2,1,0:T(8,128)S(1)}, f32[2,32,1024]{2,1,0:T(8,128)}, u32[]{:S(2)}) copy-start(f32[2,32,1024]{2,1,0:T(8,128)} %param.10) | copy-start | bytes 786436
  7.3 178.2 %copy-start.4 = (bf16[2,32,1024]{2,1,0:T(8,128)(2,1)S(1)}, bf16[2,32,1024]{2,1,0:T(8,128)(2,1)}, u32[]{:S(2)}) copy-start(bf16[2,32,1024]{2,1,0:T(8,128)(2,1)} %param.13) | copy-start | bytes 393220
  7.3 178.2 %copy-start.5 = (bf16[2,32,1024]{2,1,0:T(8,128)(2,1)S(1)}, bf16[2,32,1024]{2,1,0:T(8,128)(2,1)}, u32[]{:S(2)}) copy-start(bf16[2,32,1024]{2,1,0:T(8,128)(2,1)} %param.12) | copy-start | bytes 393220
  183.3 3.9 %copy-start.1 = (bf16[1024,1024]{1,0:T(8,128)(2,1)S(1)}, bf16[1024,1024]{1,0:T(8,128)(2,1)}, u32[]{:S(2)}) copy-start(bf16[1024,1024]{1,0:T(8,128)(2,1)} %get-tuple-element.8) | copy-start | bytes 6291460

commit v5 on v4

--- a/solution.py
+++ b/solution.py
@@ -90,14 +90,27 @@
                 r = r - (m0 * spread(r, q) + m1 * spread(r, q + 1))
                 e = e - (m0 * spread(e, q) + m1 * spread(e, q + 1))
         out.append((f - coef * pltpu.roll(f, 1, 0)) * scale * across)
-        hook(g)
         if g < groups - 1:
             rr = [spread(r, q) for q in range(8)]
             ee = [spread(e, q) for q in range(8)]
-            for h in range(g + 1, groups):
-                m = [column(rows[h], 8 * g + q) for q in range(8)]
-                rows[h] = rows[h] - tree([m[q] * rr[q] for q in range(8)])
-                inv[h] = inv[h] - tree([m[q] * ee[q] for q in range(8)])
+            m = [column(rows[g + 1], 8 * g + q) for q in range(8)]
+            if g < groups - 2:
+                x = jnp.concatenate(rows[g + 2 :], axis=0)
+                xh, xl = split(x)
+                both = jnp.concatenate([r, e], axis=1)
+                rh = both.astype(BF).astype(F32)
+                above = [jnp.zeros((8 * g, 2 * T), F32)] * (g > 0)
+                under = [jnp.zeros((T - 8 * g - 8, 2 * T), F32)]
+                yh = jnp.concatenate(above + [rh] + under, axis=0).astype(BF)
+                yl = jnp.concatenate(above + [both - rh] + under, axis=0).astype(BF)
+                z = dot(xh, yh, 1, 0) + (dot(xl, yh, 1, 0) + dot(xh, yl, 1, 0))
+                for h in range(g + 2, groups):
+                    at = 8 * (h - g - 2)
+                    rows[h] = rows[h] - z[at : at + 8, :T]
+                    inv[h] = inv[h] - z[at : at + 8, T:]
+            rows[g + 1] = rows[g + 1] - tree([m[q] * rr[q] for q in range(8)])
+            inv[g + 1] = inv[g + 1] - tree([m[q] * ee[q] for q in range(8)])
+        hook(g)
     return jnp.concatenate(out, axis=0)
 
 
@@ -140,11 +153,12 @@
     lax.fori_loop(1, 8, to_dp, 0)
     lax.fori_loop(1, 16, to_chip, 0)
     pl.semaphore_signal(barrier, inc=1, device_id={"c": 1 - core}, device_id_type=MESH)
-    pl.semaphore_wait(barrier, 7 + 15 + 1)
+    return lambda: pl.semaphore_wait(barrier, 7 + 15 + 1)
 
 
 def step_kernel(
-    owned, slot_grads, state, moments, update, terms_out, bases_out,
+    named, owned, grads, left_stats, right_stats, first, second, left_basis, right_basis,
+    update, terms_out, bases_out, slot_grads, stats, moments,
     parts, total, grad, old_stat, basis, olds, a, q, stat, mul, cat, d_ref, turned,
     q_part, q_rows, term_rows, q_t, left, half, box, pieces, arrived, home_rows, home,
     dp_send, dp_recv, state_send, state_recv, quad_send, quad_recv, grad_send, grad_recv,
@@ -158,7 +172,22 @@
     local = 2 * k + side
     rows, width = q_part.shape[1:]
     quarter = width // 4
-    greet(me, chip, core)
+    slot_total = 16
+    all_here = greet(me, chip, core)
+    for slot in range(2):
+        stats[slot, 0] = left_stats[slot].astype(BF)
+        stats[slot, 1] = right_stats[slot].astype(BF)
+        moments[slot, 0] = first[slot].astype(BF)
+        moments[slot, 1] = second[slot].astype(BF)
+
+    def place_grads(d):
+        for slot in range(2):
+            present = named[slot_total + 2 * d + slot].astype(F32)
+            rows_of = grads[named[2 * d + slot]].astype(F32)
+            slot_grads[d, slot] = (rows_of * present).astype(BF)
+
+    loop(0, 8, place_grads)
+    all_here()
 
     def member(number):
         return corner + 4 * (number // 2) + number % 2
@@ -172,13 +201,23 @@
     def state_copy(which, j, source):
         there = (chip + j) % 16
         return remote(
-            state.at[(there // 4) % 2, there % 2, which],
+            stats.at[(there // 4) % 2, there % 2],
             (old_stat, basis)[which].at[source, core],
             state_send.at[which, there],
             state_recv.at[which, source],
             chip_coords(there),
         )
 
+    def basis_copy(to_side, j):
+        there = 2 * ((chip // 2 + j) % 8) + to_side
+        return remote(
+            (left_basis, right_basis)[to_side].at[(there // 4) % 2],
+            basis.at[chip, core],
+            state_send.at[1, there],
+            state_recv.at[1, chip],
+            chip_coords(there),
+        )
+
     def quad_copy(j, source):
         number = (local + j) % 4
         return remote(
@@ -199,18 +238,17 @@
         )
 
     loop(1, 8, lambda j: dp_copy(j, me).start())
-    mine = pltpu.make_async_copy(slot_grads.at[me], parts.at[me], own.at[0])
-    mine.start()
-    keep = [
-        pltpu.make_async_copy(state.at[k, side, 0], old_stat.at[chip, core], own.at[1]),
-        pltpu.make_async_copy(state.at[k, side, 1], basis.at[chip, core], own.at[2]),
-        pltpu.make_async_copy(moments.at[k], olds.at[local], own.at[3]),
-    ]
-    for copy in keep:
-        copy.start()
+    parts[me] = slot_grads[me]
     loop(1, 16, lambda j: state_copy(0, j, chip).start())
-    loop(1, 16, lambda j: state_copy(1, j, chip).start())
-    mine.wait()
+    for to_side, ref in enumerate((left_basis, right_basis)):
+        loop(jnp.where(side == to_side, 1, 0), 8, lambda j: basis_copy(to_side, j).start())
+
+        @pl.when(side == to_side)
+        def _():
+            pltpu.make_async_copy(ref.at[k], basis.at[chip, core], own.at[2]).start()
+
+    old_stat[chip, core] = stats[k, side]
+    olds[local] = moments[k]
     loop(1, 8, lambda j: dp_copy(j, (me + 8 - j) % 8).wait_recv())
     for slot in range(2):
         acc = parts[0, slot].astype(F32)
@@ -220,8 +258,7 @@
     loop(1, 16, lambda j: grad_copy(j, chip).start())
     grad[chip, core] = total[k]
     loop(1, 4, lambda j: quad_copy(j, local).start())
-    for copy in keep:
-        copy.wait()
+    pltpu.make_async_copy(left_basis.at[k], basis.at[chip, core], own.at[2]).wait()
     for which, ref in enumerate((old_stat, basis)):
         loop(1, 16, lambda j: state_copy(which, j, (chip + 16 - j) % 16).wait_recv())
         share(ref, core, which).start()
@@ -482,8 +519,8 @@
         left_copy.wait_send()
 
 
-def optimizer_step(owned, slot_grads, state, moments):
-    rows, width = state.shape[-2:]
+def optimizer_step(named, owned, grads, left_stats, right_stats, first, second, left_basis, right_basis):
+    rows, width = grads.shape[-2:]
     dma = pltpu.SemaphoreType.DMA
     vmem = pltpu.VMEM
     full = vmem((16, 2, rows, width), BF)
@@ -494,9 +531,11 @@
             jax.ShapeDtypeStruct((4, rows, width), F32),
             jax.ShapeDtypeStruct((4, rows, width), BF),
         ),
-        in_specs=[pl.BlockSpec(memory_space=pltpu.SMEM), ANY, ANY, ANY],
+        in_specs=[pl.BlockSpec(memory_space=pltpu.SMEM)] * 2 + [pl.BlockSpec(memory_space=vmem)] * 5 + [ANY] * 2,
         out_specs=(pl.BlockSpec(memory_space=vmem), ANY, ANY),
         scratch_shapes=[
+            vmem((8, 2, rows, width), BF),
+            vmem((2, 2, rows, width), BF), vmem((2, 2, rows, width), BF),
             vmem((8, 2, rows, width), BF),
             vmem((2, rows, width), BF),
             full, full, full,
@@ -517,31 +556,34 @@
         compiler_params=pltpu.CompilerParams(
             collective_id=0, has_side_effects=True, vmem_limit_bytes=56 * 2**20
         ),
-    )(owned, slot_grads, state, moments)
+    )(named, owned, grads, left_stats, right_stats, first, second, left_basis, right_basis)
 
 
 def per_device(
     grads, block_slot, left_stats, right_stats, left_basis, right_basis, first_moment, second_moment
 ):
     capacity, rows, width = left_stats.shape
-    group_size = lax.axis_size("dp")
     block_total = block_slot.shape[0]
-    slot_total = capacity * group_size
+    slot_total = capacity * lax.axis_size("dp")
     slot_ids = lax.axis_index("dp") * capacity + jnp.arange(capacity, dtype=jnp.int32)
     owns = block_slot[:, None] == slot_ids[None, :]
     held_mask = jnp.any(owns, axis=0)[:, None, None]
 
-    placing = (
-        block_slot[:, None] == lax.broadcasted_iota(jnp.int32, (block_total, slot_total), 1)
-    ).astype(BF)
-    slot_grads = jnp.einsum("bs,brc->src", placing, grads[0], preferred_element_type=F32).astype(BF)
-    stats = jnp.stack([left_stats, right_stats], axis=1).astype(BF)
-    bases = jnp.stack([left_basis, right_basis], axis=1)
+    naming = block_slot[None, :] == jnp.arange(slot_total, dtype=jnp.int32)[:, None]
+    numbers = jnp.arange(block_total, dtype=jnp.int32)[None, :]
+    named = jnp.concatenate(
+        [jnp.sum(jnp.where(naming, numbers, 0), axis=1), jnp.any(naming, axis=1).astype(jnp.int32)]
+    )
     update, terms, new_bases = optimizer_step(
+        named,
         owns.astype(F32).reshape(block_total * capacity),
-        slot_grads.reshape(group_size, capacity, rows, width),
-        jnp.stack([stats, bases], axis=2),
-        jnp.stack([first_moment, second_moment], axis=1).astype(BF),
+        grads[0],
+        left_stats,
+        right_stats,
+        first_moment,
+        second_moment,
+        left_basis,
+        right_basis,
     )
 
     def merged(new, old):

time: 190 us -> 172 us (0.905)
  Pallas kernels: 176 us -> 161 us
    pallas_call x1, Pallas kernels: 176 us -> 161 us  [optimizer_step(): pl.pallas_call(step_kernel, out_shape=(jax.ShapeDtypeStruct((width, width...]
    another operation x5 -> x0, other arithmetic: 3.76 us -> none  [the longest x2 1.86 us: per_device(): jnp.stack([stats, bases], axis=2)]
where the time goes in v5:
time: 172 us; the launch traced here: 171 us
  Pallas kernels  161 us (94%)
  other arithmetic  6.94 us (4%)
  local copies, waits for them, and re-layouts  1.93 us (1%)
    pallas_call x1, Pallas kernels, optimizer_step(): pl.pallas_call(step_kernel, out_shape=(jax.ShapeDtypeStruct((width, width...  161 us
    select_n x2, other arithmetic, merged(): return jnp.where(held_mask, new, old)  4.07 us

profile of v5, /device:TPU:1, one launch (start us, length us, event | category | flops | bytes accessed | tf_op | source)
XLA Modules:
  0.0 170.7 jit_solution(16932764117685830554)
XLA Ops:
  0.6 0.0 copy-start.1
  0.6 0.0 copy-start.2
  0.7 0.8 compare_reduce_fusion
  1.5 0.6 reshape.35.owned
  2.1 0.7 fusion.10
  2.8 0.7 select_reduce_fusion
  3.5 0.6 pad_add_fusion.named
  4.1 161.2 %shard_map.119 = (bf16[1024,1024]{1,0:T(8,128)(2,1)}, f32[4,32,1024]{2,1,0:T(8,128)}, bf16[4,32,1024]{2,1,0:T(8,128)(2,1)}) custom-call(s32[32]{0:T(128)} %pad_add_fusion.named, f32[16]{0:T(128)} %reshape.35.owned, bf16[8,32,1024]{2,1,0:T(8,128)(2,1)} %bitcast.49, f32[2,32,1024]{2,1,0:T(8,128)} %left_stats.1, f32[2,32,1024]{2,1,0:T(8,128)} %right_stats.1, ...), custom_call_target="tpu_custom_call" | custom-call | tf_op jit(solution)/shard_map/pallas_call | solution.py:527
  165.3 0.0 copy-start
  165.3 2.3 %fusion.3 = (f32[2,32,1024]{2,1,0:T(8,128)}, f32[2,32,1024]{2,1,0:T(8,128)}) fusion(f32[2,32,1024]{2,1,0:T(8,128)} %right_stats.1, f32[2,2,32,1024]{3,2,1,0:T(8,128)} %bitcast.50, pred[2]{0:T(512)(128)(4,1)S(1)} %get-tuple-element.15, f32[2,32,1024]{2,1,0:T(8,128)} %left_stats.1), kind=kLoop, calls=%fused_computation.4 | loop fusion | flops 524288 | bytes 1572866 | tf_op jit(solution)/shard_map/jit(_where)/select_n | solution.py:590
  167.6 0.0 copy-done.1
  167.6 0.0 copy-done.2
  167.6 1.8 %fusion.8 = (bf16[2,32,1024]{2,1,0:T(8,128)(2,1)}, bf16[2,32,1024]{2,1,0:T(8,128)(2,1)}) fusion(bf16[2,32,1024]{2,1,0:T(8,128)(2,1)S(1)} %copy-done.2, bf16[2,2,32,1024]{3,2,1,0:T(8,128)(2,1)} %bitcast.51, pred[2]{0:T(512)(128)(4,1)S(1)} %get-tuple-element.15, bf16[2,32,1024]{2,1,0:T(8,128)(2,1)S(1)} %copy-done.1), kind=kLoop, calls=%fused_computation.11 | loop fusion | flops 131072 | bytes 786434 | tf_op jit(solution)/shard_map/jit(_where)/select_n | solution.py:590
  169.4 0.0 copy-done
  169.4 1.3 copy.30
  (2 shorter events, 0.0 us)
Async XLA Ops:
  0.6 167.0 %copy-start.1 = (bf16[2,32,1024]{2,1,0:T(8,128)(2,1)S(1)}, bf16[2,32,1024]{2,1,0:T(8,128)(2,1)}, u32[]{:S(2)}) copy-start(bf16[2,32,1024]{2,1,0:T(8,128)(2,1)} %left_basis.1) | copy-start | bytes 393220
  0.6 167.0 %copy-start.2 = (bf16[2,32,1024]{2,1,0:T(8,128)(2,1)S(1)}, bf16[2,32,1024]{2,1,0:T(8,128)(2,1)}, u32[]{:S(2)}) copy-start(bf16[2,32,1024]{2,1,0:T(8,128)(2,1)} %right_basis.1) | copy-start | bytes 393220
  165.3 4.1 %copy-start = (bf16[1024,1024]{1,0:T(8,128)(2,1)S(1)}, bf16[1024,1024]{1,0:T(8,128)(2,1)}, u32[]{:S(2)}) copy-start(bf16[1024,1024]{1,0:T(8,128)(2,1)} %get-tuple-element.8) | copy-start | bytes 6291460

commit v6 on v5

--- a/solution.py
+++ b/solution.py
@@ -157,7 +157,7 @@
 
 
 def step_kernel(
-    named, owned, grads, left_stats, right_stats, first, second, left_basis, right_basis,
+    block_slot, grads, left_stats, right_stats, first, second, left_basis, right_basis,
     update, terms_out, bases_out, slot_grads, stats, moments,
     parts, total, grad, old_stat, basis, olds, a, q, stat, mul, cat, d_ref, turned,
     q_part, q_rows, term_rows, q_t, left, half, box, pieces, arrived, home_rows, home,
@@ -172,7 +172,6 @@
     local = 2 * k + side
     rows, width = q_part.shape[1:]
     quarter = width // 4
-    slot_total = 16
     all_here = greet(me, chip, core)
     for slot in range(2):
         stats[slot, 0] = left_stats[slot].astype(BF)
@@ -182,8 +181,12 @@
 
     def place_grads(d):
         for slot in range(2):
-            present = named[slot_total + 2 * d + slot].astype(F32)
-            rows_of = grads[named[2 * d + slot]].astype(F32)
+            present, block = jnp.float32(0.0), jnp.int32(0)
+            for b in range(grads.shape[0]):
+                hit = block_slot[b] == 2 * d + slot
+                present = jnp.where(hit, jnp.float32(1.0), present)
+                block = jnp.where(hit, jnp.int32(b), block)
+            rows_of = grads[block].astype(F32)
             slot_grads[d, slot] = (rows_of * present).astype(BF)
 
     loop(0, 8, place_grads)
@@ -236,6 +239,10 @@
         return remote(
             ref.at[:, part], ref.at[:, part], pair_send.at[n], pair_recv.at[n], {"c": 1 - core}
         )
+
+    def share_rows(ref, source, n):
+        rows_of = ref.at[source, core]
+        return remote(rows_of, rows_of, pair_send.at[n], pair_recv.at[n], {"c": 1 - core})
 
     loop(1, 8, lambda j: dp_copy(j, me).start())
     parts[me] = slot_grads[me]
@@ -262,8 +269,14 @@
     for which, ref in enumerate((old_stat, basis)):
         loop(1, 16, lambda j: state_copy(which, j, (chip + 16 - j) % 16).wait_recv())
         share(ref, core, which).start()
-    loop(1, 16, lambda j: grad_copy(j, (chip + 16 - j) % 16).wait_recv())
-    share(grad, core, 2).start()
+    share_rows(grad, chip, 2).start()
+
+    def take_grad(j):
+        source = (chip + 16 - j) % 16
+        grad_copy(j, source).wait_recv()
+        share_rows(grad, source, 2).start()
+
+    loop(1, 16, take_grad)
     for n, ref in ((2, grad), (0, old_stat), (1, basis)):
         share(ref, 1 - core, n).wait_recv()
 
@@ -404,9 +417,12 @@
                 box_copy(which, local, source).wait_recv()
 
         def piece(b):
+            one, none = jnp.float32(1.0), jnp.float32(0.0)
+            first_owned = jnp.where(block_slot[b] == 2 * me, one, none)
+            second_owned = jnp.where(block_slot[b] == 2 * me + 1, one, none)
             return (
-                box[which, which].astype(F32) * owned[2 * b]
-                + box[which, which + 2].astype(F32) * owned[2 * b + 1]
+                box[which, which].astype(F32) * first_owned
+                + box[which, which + 2].astype(F32) * second_owned
             ).astype(BF)
 
         def send_piece(j):
@@ -429,11 +445,11 @@
     for n in range(4):
         q_part[n] = q[owned_rows(n), :].astype(BF)
 
+    send_box(0)
+
     @pl.when(side == 0)
     def _():
         left_copy.start()
-
-    send_box(0)
 
     @pl.when(side == 1)
     def _():
@@ -482,8 +498,14 @@
     kept_bases.start()
     gather_home(1)
     for which in range(2):
-        loop(1, 16, lambda j: home_copy(which, j, (chip + 16 - j) % 16).wait_recv())
-        share(home.at[which], core, 3 + which).start()
+        share_rows(home.at[which], chip, 3 + which).start()
+
+        def take_home(j):
+            source = (chip + 16 - j) % 16
+            home_copy(which, j, source).wait_recv()
+            share_rows(home.at[which], source, 3 + which).start()
+
+        loop(1, 16, take_home)
     for which in range(2):
         share(home.at[which], 1 - core, 3 + which).wait_recv()
 
@@ -519,7 +541,7 @@
         left_copy.wait_send()
 
 
-def optimizer_step(named, owned, grads, left_stats, right_stats, first, second, left_basis, right_basis):
+def optimizer_step(block_slot, grads, left_stats, right_stats, first, second, left_basis, right_basis):
     rows, width = grads.shape[-2:]
     dma = pltpu.SemaphoreType.DMA
     vmem = pltpu.VMEM
@@ -531,7 +553,7 @@
             jax.ShapeDtypeStruct((4, rows, width), F32),
             jax.ShapeDtypeStruct((4, rows, width), BF),
         ),
-        in_specs=[pl.BlockSpec(memory_space=pltpu.SMEM)] * 2 + [pl.BlockSpec(memory_space=vmem)] * 5 + [ANY] * 2,
+        in_specs=[pl.BlockSpec(memory_space=pltpu.SMEM)] + [pl.BlockSpec(memory_space=vmem)] * 5 + [ANY] * 2,
         out_specs=(pl.BlockSpec(memory_space=vmem), ANY, ANY),
         scratch_shapes=[
             vmem((8, 2, rows, width), BF),
@@ -556,27 +578,19 @@
         compiler_params=pltpu.CompilerParams(
             collective_id=0, has_side_effects=True, vmem_limit_bytes=56 * 2**20
         ),
-    )(named, owned, grads, left_stats, right_stats, first, second, left_basis, right_basis)
+    )(block_slot, grads, left_stats, right_stats, first, second, left_basis, right_basis)
 
 
 def per_device(
     grads, block_slot, left_stats, right_stats, left_basis, right_basis, first_moment, second_moment
 ):
     capacity, rows, width = left_stats.shape
-    block_total = block_slot.shape[0]
-    slot_total = capacity * lax.axis_size("dp")
     slot_ids = lax.axis_index("dp") * capacity + jnp.arange(capacity, dtype=jnp.int32)
     owns = block_slot[:, None] == slot_ids[None, :]
     held_mask = jnp.any(owns, axis=0)[:, None, None]
 
-    naming = block_slot[None, :] == jnp.arange(slot_total, dtype=jnp.int32)[:, None]
-    numbers = jnp.arange(block_total, dtype=jnp.int32)[None, :]
-    named = jnp.concatenate(
-        [jnp.sum(jnp.where(naming, numbers, 0), axis=1), jnp.any(naming, axis=1).astype(jnp.int32)]
-    )
     update, terms, new_bases = optimizer_step(
-        named,
-        owns.astype(F32).reshape(block_total * capacity),
+        block_slot,
         grads[0],
         left_stats,
         right_stats,

time: 172 us -> 164 us (0.953)
  Pallas kernels: 161 us -> 157 us
  other arithmetic: 6.94 us -> 4.91 us
    pallas_call x1, Pallas kernels: 161 us -> 157 us  [optimizer_step(): pl.pallas_call(step_kernel, out_shape=(jax.ShapeDtypeStruct((width, width...]
where the time goes in v6:
time: 164 us
  Pallas kernels  157 us (96%)
  other arithmetic  4.91 us (3%)
    pallas_call x1, Pallas kernels, optimizer_step(): pl.pallas_call(step_kernel, out_shape=(jax.ShapeDtypeStruct((width, width...  157 us
    select_n x2, other arithmetic, merged(): return jnp.where(held_mask, new, old)  3.92 us

profile of v6, /device:TPU:1, one launch (start us, length us, event | category | flops | bytes accessed | tf_op | source)
XLA Modules:
  0.0 164.3 jit_solution(6374919657477646968)
XLA Ops:
  0.6 0.0 copy-start.1
  0.6 0.0 copy-start.2
  0.7 157.4 %shard_map.119 = (bf16[1024,1024]{1,0:T(8,128)(2,1)}, f32[4,32,1024]{2,1,0:T(8,128)}, bf16[4,32,1024]{2,1,0:T(8,128)(2,1)}) custom-call(s32[8]{0:T(128)} %block_slot.1, bf16[8,32,1024]{2,1,0:T(8,128)(2,1)} %bitcast.50, f32[2,32,1024]{2,1,0:T(8,128)} %left_stats.1, f32[2,32,1024]{2,1,0:T(8,128)} %right_stats.1, f32[2,32,1024]{2,1,0:T(8,128)} %first.1, ...), custom_call_target="tpu_custom_call" | custom-call | tf_op jit(solution)/shard_map/pallas_call | solution.py:549
  158.0 0.0 copy-start
  158.0 1.0 compare_reduce_fusion
  159.0 2.2 %fusion.3 = (f32[2,32,1024]{2,1,0:T(8,128)}, f32[2,32,1024]{2,1,0:T(8,128)}) fusion(f32[2,32,1024]{2,1,0:T(8,128)} %right_stats.1, f32[2,2,32,1024]{3,2,1,0:T(8,128)} %bitcast.49, pred[2]{0:T(512)(128)(4,1)S(1)} %compare_reduce_fusion, f32[2,32,1024]{2,1,0:T(8,128)} %left_stats.1), kind=kLoop, calls=%fused_computation.4 | loop fusion | flops 524288 | bytes 1572866 | tf_op jit(solution)/shard_map/jit(_where)/select_n | solution.py:604
  161.2 0.0 copy-done.1
  161.2 0.0 copy-done.2
  161.2 1.8 %fusion.8 = (bf16[2,32,1024]{2,1,0:T(8,128)(2,1)}, bf16[2,32,1024]{2,1,0:T(8,128)(2,1)}) fusion(bf16[2,32,1024]{2,1,0:T(8,128)(2,1)S(1)} %copy-done.2, bf16[2,2,32,1024]{3,2,1,0:T(8,128)(2,1)} %bitcast.51, pred[2]{0:T(512)(128)(4,1)S(1)} %compare_reduce_fusion, bf16[2,32,1024]{2,1,0:T(8,128)(2,1)S(1)} %copy-done.1), kind=kLoop, calls=%fused_computation.11 | loop fusion | flops 131072 | bytes 786434 | tf_op jit(solution)/shard_map/jit(_where)/select_n | solution.py:604
  163.0 0.0 copy-done
  163.0 1.3 copy.26
  (1 shorter events, 0.0 us)
Async XLA Ops:
  0.6 160.6 %copy-start.1 = (bf16[2,32,1024]{2,1,0:T(8,128)(2,1)S(1)}, bf16[2,32,1024]{2,1,0:T(8,128)(2,1)}, u32[]{:S(2)}) copy-start(bf16[2,32,1024]{2,1,0:T(8,128)(2,1)} %left_basis.1) | copy-start | bytes 393220
  0.6 160.6 %copy-start.2 = (bf16[2,32,1024]{2,1,0:T(8,128)(2,1)S(1)}, bf16[2,32,1024]{2,1,0:T(8,128)(2,1)}, u32[]{:S(2)}) copy-start(bf16[2,32,1024]{2,1,0:T(8,128)(2,1)} %right_basis.1) | copy-start | bytes 393220
  158.0 4.9 %copy-start = (bf16[1024,1024]{1,0:T(8,128)(2,1)S(1)}, bf16[1024,1024]{1,0:T(8,128)(2,1)}, u32[]{:S(2)}) copy-start(bf16[1024,1024]{1,0:T(8,128)(2,1)} %get-tuple-element.8) | copy-start | bytes 6291460

commit v7 on v6

--- a/solution.py
+++ b/solution.py
@@ -388,18 +388,29 @@
             box_recv.at[which, source], chip_coords(member(number)),
         )
 
-    def piece_copy(which, j, source):
+    ways = ((0, 0, rows), (1, 0, rows // 2), (1, rows // 2, rows))
+
+    def piece_copy(way, j, source):
         there = (me + j) % 8
-        return remote(
-            pieces.at[which, there], arrived.at[which, source], piece_send.at[which, there],
-            piece_recv.at[which, source], {"dp": there},
-        )
-
-    def home_copy(which, j, source):
+        which, low, high = ways[way]
+        return remote(
+            pieces.at[which, there, low:high], arrived.at[which, source, low:high],
+            piece_send.at[way, there], piece_recv.at[way, source], {"dp": there},
+        )
+
+    def home_copy(way, j, source):
         there = (chip + j) % 16
-        return remote(
-            home_rows.at[which], home.at[which, source, core], home_send.at[which, there],
-            home_recv.at[which, source], chip_coords(there),
+        which, low, high = ways[way]
+        return remote(
+            home_rows.at[which, low:high], home.at[which, source, core, low:high],
+            home_send.at[way, there], home_recv.at[way, source], chip_coords(there),
+        )
+
+    def pair_copy(way, source, part):
+        which, low, high = ways[way]
+        rows_of = home.at[which, source, part, low:high]
+        return remote(
+            rows_of, rows_of, pair_send.at[3 + way], pair_recv.at[3 + way], {"c": 1 - core}
         )
 
     left_copy = remote(q_part, left, left_sem.at[0], left_sem.at[1], {"s": 1 - side})
@@ -431,16 +442,20 @@
             piece_copy(which, j, me).start()
 
         loop(1, 8, send_piece)
+        if which == 1:
+            loop(1, 8, lambda j: piece_copy(2, j, me).start())
         arrived[which, me] = piece(me)
 
-    def gather_home(which):
-        loop(1, 8, lambda j: piece_copy(which, j, (me + 8 - j) % 8).wait_recv())
-        acc = arrived[which, 0].astype(F32)
+    def gather_home(way):
+        which, low, high = ways[way]
+        loop(1, 8, lambda j: piece_copy(way, j, (me + 8 - j) % 8).wait_recv())
+        acc = arrived[which, 0, low:high].astype(F32)
         for d in range(1, 8):
-            acc = acc + arrived[which, d].astype(F32)
-        home_rows[which] = acc.astype(BF)
-        loop(1, 16, lambda j: home_copy(which, j, chip).start())
-        home[which, chip, core] = home_rows[which]
+            acc = acc + arrived[which, d, low:high].astype(F32)
+        home_rows[which, low:high] = acc.astype(BF)
+        loop(1, 16, lambda j: home_copy(way, j, chip).start())
+        home[which, chip, core, low:high] = acc.astype(BF)
+        pair_copy(way, chip, core).start()
 
     for n in range(4):
         q_part[n] = q[owned_rows(n), :].astype(BF)
@@ -497,39 +512,56 @@
     kept_bases = pltpu.make_async_copy(q_rows.at[local], bases_out.at[local], own.at[5])
     kept_bases.start()
     gather_home(1)
-    for which in range(2):
-        share_rows(home.at[which], chip, 3 + which).start()
-
-        def take_home(j):
+    gather_home(2)
+
+    def take_home(way):
+        def take(j):
             source = (chip + 16 - j) % 16
-            home_copy(which, j, source).wait_recv()
-            share_rows(home.at[which], source, 3 + which).start()
-
-        loop(1, 16, take_home)
-    for which in range(2):
-        share(home.at[which], 1 - core, 3 + which).wait_recv()
-
-    def multiply(j):
-        update[tile(j), :] = dot(
-            home[0, :, :, :, tile(j)].reshape(width, quarter), home[1].reshape(width, width), 0, 0
-        ).astype(BF)
-
-    loop(0, 4, multiply)
+            home_copy(way, j, source).wait_recv()
+            pair_copy(way, source, core).start()
+
+        loop(1, 16, take)
+
+    everywhere = slice(None)
+    middle = rows // 2
+    take_home(0)
+    take_home(1)
+    for way in range(2):
+        pair_copy(way, everywhere, 1 - core).wait_recv()
+
+    def product(j, low, high):
+        deep = width * (high - low) // rows
+        return dot(
+            home[0, :, :, low:high, tile(j)].reshape(deep, quarter),
+            home[1, :, :, low:high].reshape(deep, width), 0, 0,
+        )
+
+    def multiply_first(j):
+        a[tile(j), :] = product(j, 0, middle)
+
+    def multiply_second(j):
+        update[tile(j), :] = (a[tile(j), :] + product(j, middle, rows)).astype(BF)
+
+    loop(0, 4, multiply_first)
+    take_home(2)
+    pair_copy(2, everywhere, 1 - core).wait_recv()
+    loop(0, 4, multiply_second)
 
     kept_terms.wait()
     kept_bases.wait()
     for which in range(2):
         loop(1, 4, lambda j: row_copy(which, j, (local + 4 - j) % 4).wait_recv())
         loop(1, 4, lambda j: row_copy(which, j, local).wait_send())
-        loop(1, 8, lambda j: piece_copy(which, j, me).wait_send())
-        loop(1, 16, lambda j: home_copy(which, j, chip).wait_send())
         loop(1, 16, lambda j: state_copy(which, j, chip).wait_send())
-        share(home.at[which], core, 3 + which).wait_send()
 
         @pl.when(side == which)
         def _():
             loop(1, 4, lambda j: box_copy(which, (local + j) % 4, local).wait_send())
 
+    for way in range(3):
+        loop(1, 8, lambda j: piece_copy(way, j, me).wait_send())
+        loop(1, 16, lambda j: home_copy(way, j, chip).wait_send())
+        pair_copy(way, everywhere, core).wait_send()
     for n, ref in enumerate((old_stat, basis, grad)):
         share(ref, core, n).wait_send()
     loop(1, 8, lambda j: dp_copy(j, me).wait_send())
@@ -572,8 +604,8 @@
             vmem((2, 8, rows, width), BF), vmem((2, 8, rows, width), BF),
             vmem((2, rows, width), BF), vmem((2, 16, 2, rows, width), BF),
             dma((8,)), dma((8,)), dma((2, 16)), dma((2, 16)), dma((4,)), dma((4,)), dma((16,)), dma((16,)),
-            dma((2,)), dma((2, 4)), dma((2, 4)), dma((2, 4)), dma((2, 4)), dma((2, 8)), dma((2, 8)),
-            dma((2, 16)), dma((2, 16)), dma((5,)), dma((5,)), dma((6,)),
+            dma((2,)), dma((2, 4)), dma((2, 4)), dma((2, 4)), dma((2, 4)), dma((3, 8)), dma((3, 8)),
+            dma((3, 16)), dma((3, 16)), dma((6,)), dma((6,)), dma((6,)),
         ],
         compiler_params=pltpu.CompilerParams(
             collective_id=0, has_side_effects=True, vmem_limit_bytes=56 * 2**20

time: 164 us -> 164 us (level)
  no operation moved by 1% of the time
where the time goes in v7:
time: 164 us; the launch traced here: 163 us
  Pallas kernels  156 us (95%)
  other arithmetic  4.91 us (3%)
    pallas_call x1, Pallas kernels, optimizer_step(): pl.pallas_call(step_kernel, out_shape=(jax.ShapeDtypeStruct((width, width...  156 us
    select_n x2, other arithmetic, merged(): return jnp.where(held_mask, new, old)  3.92 us

profile of v7, /device:TPU:1, one launch (start us, length us, event | category | flops | bytes accessed | tf_op | source)
XLA Modules:
  0.0 163.2 jit_solution(9517641112508044867)
XLA Ops:
  0.6 0.0 copy-start.1
  0.6 0.0 copy-start.2
  0.7 156.2 %shard_map.119 = (bf16[1024,1024]{1,0:T(8,128)(2,1)}, f32[4,32,1024]{2,1,0:T(8,128)}, bf16[4,32,1024]{2,1,0:T(8,128)(2,1)}) custom-call(s32[8]{0:T(128)} %block_slot.1, bf16[8,32,1024]{2,1,0:T(8,128)(2,1)} %bitcast.50, f32[2,32,1024]{2,1,0:T(8,128)} %left_stats.1, f32[2,32,1024]{2,1,0:T(8,128)} %right_stats.1, f32[2,32,1024]{2,1,0:T(8,128)} %first.1, ...), custom_call_target="tpu_custom_call" | custom-call | tf_op jit(solution)/shard_map/pallas_call | solution.py:581
  156.9 0.0 copy-start
  156.9 1.0 compare_reduce_fusion
  157.9 2.2 %fusion.3 = (f32[2,32,1024]{2,1,0:T(8,128)}, f32[2,32,1024]{2,1,0:T(8,128)}) fusion(f32[2,32,1024]{2,1,0:T(8,128)} %right_stats.1, f32[2,2,32,1024]{3,2,1,0:T(8,128)} %bitcast.49, pred[2]{0:T(512)(128)(4,1)S(1)} %compare_reduce_fusion, f32[2,32,1024]{2,1,0:T(8,128)} %left_stats.1), kind=kLoop, calls=%fused_computation.4 | loop fusion | flops 524288 | bytes 1572866 | tf_op jit(solution)/shard_map/jit(_where)/select_n | solution.py:636
  160.1 0.0 copy-done.1
  160.1 0.0 copy-done.2
  160.1 1.8 %fusion.8 = (bf16[2,32,1024]{2,1,0:T(8,128)(2,1)}, bf16[2,32,1024]{2,1,0:T(8,128)(2,1)}) fusion(bf16[2,32,1024]{2,1,0:T(8,128)(2,1)S(1)} %copy-done.2, bf16[2,2,32,1024]{3,2,1,0:T(8,128)(2,1)} %bitcast.51, pred[2]{0:T(512)(128)(4,1)S(1)} %compare_reduce_fusion, bf16[2,32,1024]{2,1,0:T(8,128)(2,1)S(1)} %copy-done.1), kind=kLoop, calls=%fused_computation.11 | loop fusion | flops 131072 | bytes 786434 | tf_op jit(solution)/shard_map/jit(_where)/select_n | solution.py:636
  161.8 0.0 copy-done
  161.8 1.3 copy.26
  (1 shorter events, 0.0 us)
Async XLA Ops:
  0.6 159.4 %copy-start.1 = (bf16[2,32,1024]{2,1,0:T(8,128)(2,1)S(1)}, bf16[2,32,1024]{2,1,0:T(8,128)(2,1)}, u32[]{:S(2)}) copy-start(bf16[2,32,1024]{2,1,0:T(8,128)(2,1)} %left_basis.1) | copy-start | bytes 393220
  0.6 159.4 %copy-start.2 = (bf16[2,32,1024]{2,1,0:T(8,128)(2,1)S(1)}, bf16[2,32,1024]{2,1,0:T(8,128)(2,1)}, u32[]{:S(2)}) copy-start(bf16[2,32,1024]{2,1,0:T(8,128)(2,1)} %right_basis.1) | copy-start | bytes 393220
  156.9 4.9 %copy-start = (bf16[1024,1024]{1,0:T(8,128)(2,1)S(1)}, bf16[1024,1024]{1,0:T(8,128)(2,1)}, u32[]{:S(2)}) copy-start(bf16[1024,1024]{1,0:T(8,128)(2,1)} %get-tuple-element.8) | copy-start | bytes 6291460

commit v8 on v7

--- a/solution.py
+++ b/solution.py
@@ -190,6 +190,8 @@
             slot_grads[d, slot] = (rows_of * present).astype(BF)
 
     loop(0, 8, place_grads)
+    mul[...] = jnp.zeros_like(mul)
+    cat[...] = jnp.zeros_like(cat)
     all_here()
 
     def member(number):
@@ -345,8 +347,6 @@
 
     loop(0, 4, gram)
 
-    mul[...] = jnp.zeros_like(mul)
-    cat[...] = jnp.zeros_like(cat)
     d_ref[...] = a[0:T, 0:T]
     lane = lax.broadcasted_iota(jnp.int32, (T, width), 1)
 
@@ -501,13 +501,13 @@
 
     send_box(1)
     receive_box(1)
+    gather_home(0)
     for slot in range(2):
         columns = pl.ds(pl.multiple_of((corner + 4 * slot) // 2 * T, T), T)
         turned[...] = q[:, columns].T
         for side_to in range(2):
             these = pl.ds(pl.multiple_of((2 * side_to + core) * rows, rows), rows)
             q_rows[2 * slot + side_to] = turned[these, :].astype(BF)
-    gather_home(0)
     loop(1, 4, lambda j: row_copy(1, j, local).start())
     kept_bases = pltpu.make_async_copy(q_rows.at[local], bases_out.at[local], own.at[5])
     kept_bases.start()

time: 164 us -> 164 us (level)
  no operation moved by 1% of the time
where the time goes in v8:
time: 164 us; the launch traced here: 162 us
  Pallas kernels  155 us (95%)
  other arithmetic  4.91 us (3%)
    pallas_call x1, Pallas kernels, optimizer_step(): pl.pallas_call(step_kernel, out_shape=(jax.ShapeDtypeStruct((width, width...  155 us
    select_n x2, other arithmetic, merged(): return jnp.where(held_mask, new, old)  3.92 us

profile of v8, /device:TPU:1, one launch (start us, length us, event | category | flops | bytes accessed | tf_op | source)
XLA Modules:
  0.0 162.4 jit_solution(15265533800247443654)
XLA Ops:
  0.6 0.0 copy-start.1
  0.6 0.0 copy-start.2
  0.7 155.5 %shard_map.119 = (bf16[1024,1024]{1,0:T(8,128)(2,1)}, f32[4,32,1024]{2,1,0:T(8,128)}, bf16[4,32,1024]{2,1,0:T(8,128)(2,1)}) custom-call(s32[8]{0:T(128)} %block_slot.1, bf16[8,32,1024]{2,1,0:T(8,128)(2,1)} %bitcast.50, f32[2,32,1024]{2,1,0:T(8,128)} %left_stats.1, f32[2,32,1024]{2,1,0:T(8,128)} %right_stats.1, f32[2,32,1024]{2,1,0:T(8,128)} %first.1, ...), custom_call_target="tpu_custom_call" | custom-call | tf_op jit(solution)/shard_map/pallas_call | solution.py:581
  156.2 0.0 copy-start
  156.2 1.0 compare_reduce_fusion
  157.2 2.2 %fusion.3 = (f32[2,32,1024]{2,1,0:T(8,128)}, f32[2,32,1024]{2,1,0:T(8,128)}) fusion(f32[2,32,1024]{2,1,0:T(8,128)} %right_stats.1, f32[2,2,32,1024]{3,2,1,0:T(8,128)} %bitcast.49, pred[2]{0:T(512)(128)(4,1)S(1)} %compare_reduce_fusion, f32[2,32,1024]{2,1,0:T(8,128)} %left_stats.1), kind=kLoop, calls=%fused_computation.4 | loop fusion | flops 524288 | bytes 1572866 | tf_op jit(solution)/shard_map/jit(_where)/select_n | solution.py:636
  159.3 0.0 copy-done.1
  159.3 0.0 copy-done.2
  159.3 1.8 %fusion.8 = (bf16[2,32,1024]{2,1,0:T(8,128)(2,1)}, bf16[2,32,1024]{2,1,0:T(8,128)(2,1)}) fusion(bf16[2,32,1024]{2,1,0:T(8,128)(2,1)S(1)} %copy-done.2, bf16[2,2,32,1024]{3,2,1,0:T(8,128)(2,1)} %bitcast.51, pred[2]{0:T(512)(128)(4,1)S(1)} %compare_reduce_fusion, bf16[2,32,1024]{2,1,0:T(8,128)(2,1)S(1)} %copy-done.1), kind=kLoop, calls=%fused_computation.11 | loop fusion | flops 131072 | bytes 786434 | tf_op jit(solution)/shard_map/jit(_where)/select_n | solution.py:636
  161.1 0.0 copy-done
  161.1 1.3 copy.26
  (1 shorter events, 0.0 us)
Async XLA Ops:
  0.6 158.7 %copy-start.1 = (bf16[2,32,1024]{2,1,0:T(8,128)(2,1)S(1)}, bf16[2,32,1024]{2,1,0:T(8,128)(2,1)}, u32[]{:S(2)}) copy-start(bf16[2,32,1024]{2,1,0:T(8,128)(2,1)} %left_basis.1) | copy-start | bytes 393220
  0.6 158.7 %copy-start.2 = (bf16[2,32,1024]{2,1,0:T(8,128)(2,1)S(1)}, bf16[2,32,1024]{2,1,0:T(8,128)(2,1)}, u32[]{:S(2)}) copy-start(bf16[2,32,1024]{2,1,0:T(8,128)(2,1)} %right_basis.1) | copy-start | bytes 393220
  156.2 4.9 %copy-start = (bf16[1024,1024]{1,0:T(8,128)(2,1)S(1)}, bf16[1024,1024]{1,0:T(8,128)(2,1)}, u32[]{:S(2)}) copy-start(bf16[1024,1024]{1,0:T(8,128)(2,1)} %get-tuple-element.8) | copy-start | bytes 6291460

commit v9 on v8

--- a/solution.py
+++ b/solution.py
@@ -266,7 +266,6 @@
         total[slot] = acc.astype(BF)
     loop(1, 16, lambda j: grad_copy(j, chip).start())
     grad[chip, core] = total[k]
-    loop(1, 4, lambda j: quad_copy(j, local).start())
     pltpu.make_async_copy(left_basis.at[k], basis.at[chip, core], own.at[2]).wait()
     for which, ref in enumerate((old_stat, basis)):
         loop(1, 16, lambda j: state_copy(which, j, (chip + 16 - j) % 16).wait_recv())
@@ -322,6 +321,7 @@
     for n in range(4):
         term_rows[n] = a[owned_rows(n), :]
     loop(1, 4, lambda j: row_copy(0, j, local).start())
+    loop(1, 4, lambda j: quad_copy(j, local).start())
     kept_terms = pltpu.make_async_copy(term_rows.at[local], terms_out.at[local], own.at[4])
     kept_terms.start()
 

time: 164 us -> 162 us (0.988)
    pallas_call x1, Pallas kernels: 155 us -> 154 us  [optimizer_step(): pl.pallas_call(step_kernel, out_shape=(jax.ShapeDtypeStruct((width, width...]
where the time goes in v9:
time: 162 us; the launch traced here: 161 us
  Pallas kernels  154 us (95%)
  other arithmetic  4.91 us (3%)
    pallas_call x1, Pallas kernels, optimizer_step(): pl.pallas_call(step_kernel, out_shape=(jax.ShapeDtypeStruct((width, width...  154 us
    select_n x2, other arithmetic, merged(): return jnp.where(held_mask, new, old)  3.92 us

profile of v9, /device:TPU:1, one launch (start us, length us, event | category | flops | bytes accessed | tf_op | source)
XLA Modules:
  0.0 160.5 jit_solution(9449595382753059004)
XLA Ops:
  0.6 0.0 copy-start.1
  0.6 0.0 copy-start.2
  0.7 153.6 %shard_map.119 = (bf16[1024,1024]{1,0:T(8,128)(2,1)}, f32[4,32,1024]{2,1,0:T(8,128)}, bf16[4,32,1024]{2,1,0:T(8,128)(2,1)}) custom-call(s32[8]{0:T(128)} %block_slot.1, bf16[8,32,1024]{2,1,0:T(8,128)(2,1)} %bitcast.50, f32[2,32,1024]{2,1,0:T(8,128)} %left_stats.1, f32[2,32,1024]{2,1,0:T(8,128)} %right_stats.1, f32[2,32,1024]{2,1,0:T(8,128)} %first.1, ...), custom_call_target="tpu_custom_call" | custom-call | tf_op jit(solution)/shard_map/pallas_call | solution.py:581
  154.3 0.0 copy-start
  154.3 1.0 compare_reduce_fusion
  155.3 2.2 %fusion.3 = (f32[2,32,1024]{2,1,0:T(8,128)}, f32[2,32,1024]{2,1,0:T(8,128)}) fusion(f32[2,32,1024]{2,1,0:T(8,128)} %right_stats.1, f32[2,2,32,1024]{3,2,1,0:T(8,128)} %bitcast.49, pred[2]{0:T(512)(128)(4,1)S(1)} %compare_reduce_fusion, f32[2,32,1024]{2,1,0:T(8,128)} %left_stats.1), kind=kLoop, calls=%fused_computation.4 | loop fusion | flops 524288 | bytes 1572866 | tf_op jit(solution)/shard_map/jit(_where)/select_n | solution.py:636
  157.5 0.0 copy-done.1
  157.5 0.0 copy-done.2
  157.5 1.8 %fusion.8 = (bf16[2,32,1024]{2,1,0:T(8,128)(2,1)}, bf16[2,32,1024]{2,1,0:T(8,128)(2,1)}) fusion(bf16[2,32,1024]{2,1,0:T(8,128)(2,1)S(1)} %copy-done.2, bf16[2,2,32,1024]{3,2,1,0:T(8,128)(2,1)} %bitcast.51, pred[2]{0:T(512)(128)(4,1)S(1)} %compare_reduce_fusion, bf16[2,32,1024]{2,1,0:T(8,128)(2,1)S(1)} %copy-done.1), kind=kLoop, calls=%fused_computation.11 | loop fusion | flops 131072 | bytes 786434 | tf_op jit(solution)/shard_map/jit(_where)/select_n | solution.py:636
  159.2 0.0 copy-done
  159.2 1.3 copy.26
  (1 shorter events, 0.0 us)
Async XLA Ops:
  0.6 156.8 %copy-start.1 = (bf16[2,32,1024]{2,1,0:T(8,128)(2,1)S(1)}, bf16[2,32,1024]{2,1,0:T(8,128)(2,1)}, u32[]{:S(2)}) copy-start(bf16[2,32,1024]{2,1,0:T(8,128)(2,1)} %left_basis.1) | copy-start | bytes 393220
  0.6 156.8 %copy-start.2 = (bf16[2,32,1024]{2,1,0:T(8,128)(2,1)S(1)}, bf16[2,32,1024]{2,1,0:T(8,128)(2,1)}, u32[]{:S(2)}) copy-start(bf16[2,32,1024]{2,1,0:T(8,128)(2,1)} %right_basis.1) | copy-start | bytes 393220
  154.3 4.9 %copy-start = (bf16[1024,1024]{1,0:T(8,128)(2,1)S(1)}, bf16[1024,1024]{1,0:T(8,128)(2,1)}, u32[]{:S(2)}) copy-start(bf16[1024,1024]{1,0:T(8,128)(2,1)} %get-tuple-element.8) | copy-start | bytes 6291460
